TPU v7x, 32 devices: a whole 2x2x4 slice. The times are simulated.
32 devices in a mesh: items: 8 (over z, y), rep: 4 (over x, core).
Axes of the slice: x: 2, y: 2, z: 4, core: 2. Of those that a mesh axis runs over, the one named last changes fastest.
Arguments:
- embeds: bfloat16 [8192, 256], P(('items', 'rep')), may hold values from -6 to 6
- assign: int32 [8192], P(('items', 'rep')), may hold values from 0 to 4095, as said below
- list_slot: int32 [4096], replicated, may hold values from 0 to 4095, as said below
- old_centroids: bfloat16 [4096, 256], P('items'), may hold values from -6 to 6
Outputs:
- new_centroids: bfloat16 [4096, 256], P('items')
- codes: bfloat16 [8, 4, 1024, 256], P('items', 'rep')
- row_scales: float32 [8, 4, 1024], P('items', 'rep')
Inputs may be any that keep to these rules, and one draw needn't show every extreme that they name: `assign`: on one device at most 128 items go to lists of one owner, and some owner receives exactly 128 items from every device. `list_slot`: A permutation of the lists.
All inputs are finite; a program needn't handle non-finite values. Where the computation divides by a largest or mean magnitude, that divisor is 1e-20 or more.
Results may differ from a plain program's by a relative error of at most 0.0041.
Values may be sent and summed in bfloat16 or wider, within the bound.
No kernel may reach another device: no remote copies, remote signals or barrier semaphores. Data moves between devices by JAX's collectives and lax.ppermute only.
A program may use at most 64 MiB of HBM per device.

v0:
```python
import jax
import jax.numpy as jnp
from jax import lax
from jax.sharding import PartitionSpec as P


def per_device(embeds, assign, list_slot, old_centroids):
    peers = lax.axis_size("items")
    list_dev = old_centroids.shape[0]
    width = embeds.shape[1]
    item_dev = embeds.shape[0]
    capacity = 4 * item_dev // peers
    slot = list_slot[assign]
    owner = slot // list_dev
    local = slot % list_dev
    member = (owner[:, None] == jnp.arange(peers, dtype=jnp.int32)[None, :]).astype(jnp.int32)
    rank = jnp.sum(member * (jnp.cumsum(member, axis=0) - 1), axis=1)
    target = owner * capacity + rank
    outgoing = jnp.zeros((peers * capacity, width), jnp.bfloat16).at[target].set(embeds)
    labels = jnp.full((peers * capacity,), -1, jnp.int32).at[target].set(local)
    arrived, arrived_ids = (
        lax.all_to_all(
            outgoing.reshape(peers, capacity, width),
            "items",
            split_axis=0,
            concat_axis=0,
            tiled=True,
        ),
        lax.all_to_all(
            labels.reshape(peers, capacity), "items", split_axis=0, concat_axis=0, tiled=True
        ),
    )
    arrived = arrived.reshape(peers * capacity, width)
    arrived_ids = arrived_ids.reshape(peers * capacity)
    member_t = (jnp.arange(list_dev, dtype=jnp.int32)[:, None] == arrived_ids[None, :]).astype(
        jnp.bfloat16
    )
    partial_sums = jnp.dot(member_t, arrived, preferred_element_type=jnp.float32)
    partial_counts = jnp.sum(member_t, axis=1, dtype=jnp.float32)
    total_sums, total_counts = lax.psum((partial_sums, partial_counts), "rep")
    fresh = (
        (total_sums + old_centroids.astype(jnp.float32)) / (total_counts + 1.0)[:, None]
    ).astype(jnp.bfloat16)
    lookup = lax.dot_general(
        member_t, fresh, (((0,), (0,)), ((), ())), preferred_element_type=jnp.float32
    )
    residual = arrived.astype(jnp.float32) - lookup
    amax = jnp.max(jnp.abs(residual), axis=1)
    codes = (residual * (127.0 / (amax + 1e-06))[:, None]).astype(jnp.bfloat16)
    row_scales = amax / 127.0
    return (
        fresh,
        codes.reshape(1, 1, peers * capacity, width),
        row_scales.reshape(1, 1, peers * capacity),
    )


def solution(mesh):
    in_specs = (P(("items", "rep"), None), P(("items", "rep")), P(), P("items", None))
    out_specs = (P("items", None), P("items", "rep", None, None), P("items", "rep", None))
    return jax.shard_map(
        per_device, mesh=mesh, in_specs=in_specs, out_specs=out_specs, check_vma=False
    )
```

profile of v0, /device:TPU:0, one launch (start us, length us, event | category | flops | bytes accessed | tf_op | source)
XLA Modules:
  0.0 86.1 jit_solution(4378615672808141915)
XLA Ops:
  7.2 0.0 copy-start
  7.2 0.7 compare_select_fusion.1
  7.9 0.0 copy-done
  7.9 1.7 %gather_fusion = s32[256]{0:T(256)S(1)} fusion(s32[4096]{0:T(1024)S(1)} %copy-done, s32[1024]{0:T(1024)S(1)} %pad_clamp_fusion), kind=kCustom, calls=%fused_computation | custom fusion | bytes 3072 | tf_op jit(solution)/shard_map/gather | solution.py:13
  9.7 0.6 reduce-window.6
  10.2 0.2 slice_reduce_fusion
  10.5 0.1 fusion.11
  10.6 2.0 %scatter_custom_fusion = s32[1024]{0:T(1024)} fusion(s32[256]{0:T(256)S(1)} %bitcast.43, s32[256]{0:T(256)S(1)} %get-tuple-element.17, s32[]{:T(128)} %constant.41.clone.1), kind=kCustom, calls=%fused_computation.34 | custom fusion | bytes 4100 | tf_op jit(solution)/shard_map/scatter | solution.py:20
  12.6 7.3 %all-to-all-start = ((s32[8,1,128]{2,1,0:T(1,128)}), s32[8,1,128]{2,1,0:T(1,128)S(1)}, u32[]{:S(2)}, u32[]{:S(2)}) async-start(s32[8,1,128]{2,1,0:T(1,128)} %bitcast.6), calls=%async_computation | async-start | bytes 8192 | tf_op jit(solution)/shard_map/all_to_all | solution.py:29
  19.9 0.0 all-reduce.2.cloned.1.call-start
  19.9 2.0 %scatter_custom_fusion.1 = bf16[1024,256]{1,0:T(8,128)(2,1)S(1)} fusion(s32[256]{0:T(256)S(1)} %bitcast.44, bf16[256,256]{1,0:T(8,128)(2,1)} %param.4, bf16[]{:T(256)} %constant.50.clone.1), kind=kCustom, calls=%fused_computation.17 | custom fusion | bytes 524800 | tf_op jit(solution)/shard_map/scatter | solution.py:19
  21.9 0.3 copy.13
  22.2 4.0 %all-to-all-done = s32[8,1,128]{2,1,0:T(1,128)S(1)} async-done(((s32[8,1,128]{2,1,0:T(1,128)}), s32[8,1,128]{2,1,0:T(1,128)S(1)}, u32[]{:S(2)}, u32[]{:S(2)}) %all-to-all-start) | async-done | bytes 4128 | tf_op jit(solution)/shard_map/all_to_all | solution.py:29
  26.3 15.7 %all_to_all.14 = bf16[8,128,256]{1,2,0:T(8,128)(2,1)S(1)} all-to-all(bf16[8,128,256]{1,2,0:T(8,128)(2,1)S(1)} %copy.13), channel_id=1, replica_groups=mesh['items'=8,'rep'=4] {'items'}, dimensions={0} | all-to-all | bytes 1048576 | tf_op jit(solution)/shard_map/all_to_all | solution.py:22
  42.0 0.0 copy-start.1
  42.0 1.3 %fusion.2 = f32[512,256]{1,0:T(8,128)} fusion(s32[1024]{0:T(1024)S(1)} %bitcast.39, bf16[8,128,256]{1,2,0:T(8,128)(2,1)S(1)} %all_to_all.14), kind=kOutput, calls=%fused_computation.7 | convolution fusion | flops 268959744 | bytes 1052672 | tf_op jit(solution)/shard_map/dot_general | solution.py:38
  43.3 0.0 all-reduce.2.cloned.1.call-update
  43.3 0.3 convert_reduce_fusion
  43.6 5.7 %psum.15 = f32[512]{0:T(512)S(1)} all-reduce(f32[512]{0:T(512)S(1)} %convert_reduce_fusion), channel_id=1, replica_groups=mesh['items'=8,'rep'=4] {'rep'}, use_global_device_ids=true, to_apply=%region_7.8 | all-reduce | flops 512 | bytes 4096 | tf_op jit(solution)/shard_map/psum | solution.py:40
  49.3 26.4 %all-reduce.2.cloned.1.call-done = f32[512,256]{1,0:T(8,128)} async-done(((f32[512,256]{1,0:T(8,128)}), f32[512,256]{1,0:T(8,128)}) %all-reduce.2.cloned.1.call-update) | async-done | bytes 524304 | tf_op jit(solution)/shard_map/psum | solution.py:40
  75.7 0.0 copy-done.1
  75.7 1.2 %divide_convert_fusion = bf16[512,256]{1,0:T(8,128)(2,1)S(1)} fusion(f32[512,256]{1,0:T(8,128)} %all-reduce.2.cloned.1.call-done, bf16[512,256]{1,0:T(8,128)(2,1)S(1)} %copy-done.1, f32[512]{0:T(512)S(1)} %broadcast_add_fusion), kind=kLoop, calls=%fused_computation.15 | loop fusion | flops 524288 | bytes 1050624 | tf_op jit(solution)/shard_map/convert_element_type | solution.py:43
  76.9 0.0 copy-start.2
  76.9 0.6 abs_reduce_fusion
  77.5 0.1 copy-done.2
  77.6 0.6 broadcast_multiply_fusion
  78.2 0.1 fusion.6
  78.3 1.0 %copy.15 = bf16[1,1,1024,256]{3,2,1,0:T(8,128)(2,1)} copy(bf16[1,1,1024,256]{2,3,1,0:T(8,128)(2,1)S(1)} %fusion.6) | data formatting | bytes 1048576
  (8 shorter events, 0.1 us)
Async XLA Ops:
  7.2 0.7 copy-start
  12.6 13.7 %all-to-all-start = ((s32[8,1,128]{2,1,0:T(1,128)}), s32[8,1,128]{2,1,0:T(1,128)S(1)}, u32[]{:S(2)}, u32[]{:S(2)}) async-start(s32[8,1,128]{2,1,0:T(1,128)} %bitcast.6), calls=%async_computation | async-start | bytes 8192 | tf_op jit(solution)/shard_map/all_to_all | solution.py:29
  19.9 55.8 %all-reduce.2.cloned.1.call-start = ((), (), s32[]{:S(2)}) async-start(), calls=%async_computation.2 | async-start | bytes 1048576 | tf_op jit(solution)/shard_map/psum | solution.py:40
  42.0 33.7 %copy-start.1 = (bf16[512,256]{1,0:T(8,128)(2,1)S(1)}, bf16[512,256]{1,0:T(8,128)(2,1)}, u32[]{:S(2)}) copy-start(bf16[512,256]{1,0:T(8,128)(2,1)} %param.7) | copy-start | bytes 786436
  76.9 0.7 copy-start.2
Sparse Core Ops, SparseCore 0:
  43.4 32.2 all-reduce.1
where the time goes:
time: 86.5 us; the launch traced here: 86.1 us
  waiting for transfers between devices  30.5 us (35%)
  blocking collectives  21.4 us (25%)
  between operations  14.1 us (16%)
  starting transfers between devices  7.32 us (8%)
  local copies, waits for them, and re-layouts  7.31 us (8%)
  other arithmetic  3.61 us (4%)
  matrix products  1.88 us (2%)
    psum x1, waiting for transfers between devices, per_device(): total_sums, total_counts = lax.psum((partial_sums, partial_counts), 'rep')  26.4 us
    all_to_all x1, blocking collectives, per_device(): lax.all_to_all(outgoing.reshape(peers, capacity, width), 'items', split_a...  15.7 us
    all_to_all x1, starting transfers between devices, per_device(): lax.all_to_all(labels.reshape(peers, capacity), 'items', split_axis=0, co...  7.28 us
    psum x1, blocking collectives, per_device(): total_sums, total_counts = lax.psum((partial_sums, partial_counts), 'rep')  5.66 us
    all_to_all x1, waiting for transfers between devices, per_device(): lax.all_to_all(labels.reshape(peers, capacity), 'items', split_axis=0, co...  4.05 us
    scatter x1, local copies, waits for them, and re-layouts, per_device(): jnp.zeros((peers * capacity, width), jnp.bfloat16).at[target].set(embeds)  2.01 us
    scatter x1, local copies, waits for them, and re-layouts, per_device(): labels = jnp.full((peers * capacity,), -1, jnp.int32).at[target].set(local)  1.97 us
  transfers between devices with their start and end apart: 2, of which 2 were waited for; matrix products, arithmetic and copies ran while one was open for 3% of the time, Pallas kernels for 0%

commit v1 on v0

--- a/solution.py
+++ b/solution.py
@@ -1,7 +1,219 @@
 import jax
 import jax.numpy as jnp
 from jax import lax
+from jax.experimental import pallas as pl
+from jax.experimental.pallas import tpu as pltpu
 from jax.sharding import PartitionSpec as P
+
+HEAD = 16
+VMEM = pl.BlockSpec(memory_space=pltpu.VMEM)
+SMEM = pl.BlockSpec(memory_space=pltpu.SMEM)
+
+
+def _log2(n):
+    return n.bit_length() - 1
+
+
+def _iota(shape, dim):
+    return lax.broadcasted_iota(jnp.int32, shape, dim)
+
+
+def _slots(table, assign):
+    t, n = table.shape[0], assign.shape[1]
+    hot = (_iota((t, n), 0) == (assign >> 7)).astype(jnp.float32).astype(jnp.bfloat16)
+    lane = _iota((128, n), 0) == (assign & 127)
+
+    def pick(part):
+        part = part.astype(jnp.float32).astype(jnp.bfloat16)
+        rows = lax.dot_general(
+            part, hot, (((0,), (0,)), ((), ())), preferred_element_type=jnp.float32
+        )
+        return jnp.sum(jnp.where(lane, rows, 0.0), axis=0, keepdims=True)
+
+    return (pick(table & 255) + 256.0 * pick(table >> 8)).astype(jnp.int32)
+
+
+def _route(sel, lo, hi, rows, outs):
+    n = rows.shape[0]
+    capacity = outs[0].shape[0] - HEAD
+    place = jnp.concatenate(
+        [(_iota((capacity, n), 0) == sel[k : k + 1, :]).astype(jnp.float32) for k in range(len(outs))],
+        axis=0,
+    ).astype(jnp.bfloat16)
+    moved = jnp.dot(place, rows, preferred_element_type=jnp.float32).astype(jnp.bfloat16)
+    first = _iota((HEAD, n), 0) == 0
+    values = jnp.where(first, lo, hi).astype(jnp.bfloat16)
+    labels = lax.dot_general(
+        values, place, (((1,), (1,)), ((), ())), preferred_element_type=jnp.float32
+    )
+    for k, out in enumerate(outs):
+        part = labels[:, k * capacity : (k + 1) * capacity]
+        head = jnp.concatenate([part[0:1, :], part[1:2, :]], axis=1)
+        out[0:capacity, :] = moved[k * capacity : (k + 1) * capacity, :]
+        out[capacity:, :] = jnp.broadcast_to(head, (HEAD, head.shape[1])).astype(jnp.bfloat16)
+
+
+def _route_own_kernel(list_dev, at, own_assign, far_assign, table, rows, o0, o1, o2, o3, far):
+    n = own_assign.shape[1]
+    me = at[0]
+    slot = _slots(table[...], jnp.concatenate([own_assign[...], far_assign[...]], axis=1))
+    relative = (slot >> _log2(list_dev)) ^ me
+    code = (slot & (list_dev - 1)) + 1
+    lo = (code & 255).astype(jnp.float32)
+    hi = (code >> 8).astype(jnp.float32)
+    member = (_iota((8, 2 * n), 0) == relative).astype(jnp.float32)
+    member = jnp.concatenate([member[:, :n], member[:, n:]], axis=0)
+    before = (_iota((n, n), 0) < _iota((n, n), 1)).astype(jnp.float32).astype(jnp.bfloat16)
+    count = jnp.dot(member.astype(jnp.bfloat16), before, preferred_element_type=jnp.float32)
+    sel = jnp.where(member > 0.0, count, -1.0).astype(jnp.int32)
+    _route(sel[0:8, :], lo[:, :n], hi[:, :n], rows[...], (o0, o1, o2, o3))
+    eight = _iota((8, n), 0)
+    far_sel = jnp.where(eight < 4, sel[8:16, :], 0)
+    far_sel = jnp.where(eight == 4, lo[:, n:].astype(jnp.int32), far_sel)
+    far[...] = jnp.where(eight == 5, hi[:, n:].astype(jnp.int32), far_sel)
+
+
+def _route_far_kernel(far, rows, o0, o1, o2, o3):
+    lo = far[4:5, :].astype(jnp.float32)
+    hi = far[5:6, :].astype(jnp.float32)
+    _route(far[...], lo, hi, rows[...], (o0, o1, o2, o3))
+
+
+def _labels(block):
+    capacity = block.shape[0] - HEAD
+    head = block[capacity:, :].astype(jnp.float32)[0:1, :]
+    return (head[:, :capacity] + 256.0 * head[:, capacity:]).astype(jnp.int32) - 1
+
+
+def _sums_kernel(at, *refs):
+    blocks, (send, keep) = refs[:8], refs[8:]
+    half = send.shape[0] - 8
+    capacity = blocks[0].shape[0] - HEAD
+    rows = jnp.concatenate([b[0:capacity, :] for b in blocks], axis=0)
+    labels = jnp.concatenate([_labels(b) for b in blocks], axis=1)
+    ones = jnp.ones((16, rows.shape[0]), jnp.bfloat16)
+    for out, side in ((send, 1 - at[1]), (keep, at[1])):
+        hot = (_iota((half, rows.shape[0]), 0) + side * half == labels).astype(jnp.float32)
+        hot = hot.astype(jnp.bfloat16)
+        out[0:half, :] = jnp.dot(hot, rows, preferred_element_type=jnp.float32)
+        out[half:, :] = lax.dot_general(
+            ones, hot, (((1,), (1,)), ((), ())), preferred_element_type=jnp.float32
+        )[0:8, :]
+
+
+def _fresh_kernel(at, part, got, old, out):
+    half = out.shape[0]
+    total = part[...] + got[...]
+    counts = jnp.sum(
+        jnp.where(_iota((half, half), 0) == _iota((half, half), 1), total[half : half + 1, :], 0.0),
+        axis=1,
+        keepdims=True,
+    )
+    mine = old[pl.ds(pl.multiple_of(at[1] * half, half), half), :].astype(jnp.float32)
+    out[...] = ((total[:half, :] + mine) / (counts + 1.0)).astype(jnp.bfloat16)
+
+
+def _codes_kernel(at, *refs):
+    blocks, (mine, other, fresh, codes, scales) = refs[:8], refs[8:]
+    half = mine.shape[0]
+    capacity = blocks[0].shape[0] - HEAD
+    me, side = at[0], at[1]
+    fresh[pl.ds(pl.multiple_of(side * half, half), half), :] = mine[...]
+    fresh[pl.ds(pl.multiple_of((1 - side) * half, half), half), :] = other[...]
+    table = fresh[...]
+    eye = _iota((capacity, capacity), 0) == _iota((capacity, capacity), 1)
+    for k, block in enumerate(blocks):
+        column = jnp.sum(
+            jnp.where(eye, _labels(block).astype(jnp.float32), 0.0), axis=1, keepdims=True
+        ).astype(jnp.int32)
+        hot = (_iota((capacity, 2 * half), 1) == column).astype(jnp.float32).astype(jnp.bfloat16)
+        lookup = jnp.dot(hot, table, preferred_element_type=jnp.float32)
+        residual = block[0:capacity, :].astype(jnp.float32) - lookup
+        amax = jnp.max(jnp.abs(residual), axis=1, keepdims=True)
+        source = me ^ k
+        codes[pl.ds(pl.multiple_of(source * capacity, capacity), capacity), :] = (
+            residual * (127.0 / (amax + 1e-06))
+        ).astype(jnp.bfloat16)
+        scales[pl.ds(source, 1), :] = jnp.sum(
+            jnp.where(eye, amax / 127.0, 0.0), axis=0, keepdims=True
+        )
+
+
+def _call(kernel, outs, args, flops=0):
+    moved = sum(a.size * a.dtype.itemsize for a in args) + sum(
+        o.size * o.dtype.itemsize for o in outs
+    )
+    return pl.pallas_call(
+        kernel,
+        out_shape=outs,
+        in_specs=[SMEM if a.ndim == 1 else VMEM for a in args],
+        out_specs=[VMEM] * len(outs),
+        compiler_params=pltpu.CompilerParams(vmem_limit_bytes=24 * 2**20),
+        cost_estimate=pl.CostEstimate(flops=flops, bytes_accessed=moved, transcendentals=0),
+    )(*args)
+
+
+def per_device_eight(embeds, assign, list_slot, old_centroids):
+    list_dev, width = old_centroids.shape
+    item_dev = embeds.shape[0]
+    peers = lax.axis_size("items")
+    capacity = 4 * item_dev // peers
+    half = list_dev // 2
+    hop = lambda a, axis, bit: lax.ppermute(
+        a, axis, [(i, i ^ bit) for i in range(lax.axis_size(axis))]
+    )
+    at = jnp.stack([lax.axis_index("items"), lax.axis_index("rep") & 1]).astype(jnp.int32)
+    far_rows = hop(embeds, "items", 4)
+    far_assign = hop(assign, "items", 4)
+    block = jax.ShapeDtypeStruct((capacity + HEAD, width), jnp.bfloat16)
+    *own, far = _call(
+        lambda *refs: _route_own_kernel(list_dev, *refs),
+        [block] * 4 + [jax.ShapeDtypeStruct((8, item_dev), jnp.int32)],
+        (
+            at,
+            assign.reshape(1, item_dev),
+            far_assign.reshape(1, item_dev),
+            list_slot.reshape(-1, 128),
+            embeds,
+        ),
+        flops=2 * 4 * capacity * item_dev * width,
+    )
+    own = [own[0]] + [hop(own[k], "items", k) for k in (1, 2, 3)]
+    away = _call(
+        _route_far_kernel, [block] * 4, (far, far_rows), flops=2 * 4 * capacity * item_dev * width
+    )
+    away = [away[0]] + [hop(away[k], "items", k) for k in (1, 2, 3)]
+    blocks = tuple(own) + tuple(away)
+    partial = jax.ShapeDtypeStruct((half + 8, width), jnp.float32)
+    send, keep = _call(
+        _sums_kernel,
+        [partial] * 2,
+        (at,) + blocks,
+        flops=2 * list_dev * peers * capacity * width,
+    )
+    part = keep + hop(send, "rep", 1)
+    got = hop(part, "rep", 2)
+    (mine,) = _call(
+        _fresh_kernel,
+        [jax.ShapeDtypeStruct((half, width), jnp.bfloat16)],
+        (at, part, got, old_centroids),
+    )
+    other = hop(mine, "rep", 1)
+    fresh, codes, scales = _call(
+        _codes_kernel,
+        [
+            jax.ShapeDtypeStruct((list_dev, width), jnp.bfloat16),
+            jax.ShapeDtypeStruct((peers * capacity, width), jnp.bfloat16),
+            jax.ShapeDtypeStruct((peers, capacity), jnp.float32),
+        ],
+        (at,) + blocks + (mine, other),
+        flops=2 * list_dev * peers * capacity * width,
+    )
+    return (
+        fresh,
+        codes.reshape(1, 1, peers * capacity, width),
+        scales.reshape(1, 1, peers * capacity),
+    )
 
 
 def per_device(embeds, assign, list_slot, old_centroids):
@@ -58,6 +270,11 @@
 def solution(mesh):
     in_specs = (P(("items", "rep"), None), P(("items", "rep")), P(), P("items", None))
     out_specs = (P("items", None), P("items", "rep", None, None), P("items", "rep", None))
+    small = mesh.shape["items"] == 8 and mesh.shape["rep"] == 4
     return jax.shard_map(
-        per_device, mesh=mesh, in_specs=in_specs, out_specs=out_specs, check_vma=False
-    )
+        per_device_eight if small else per_device,
+        mesh=mesh,
+        in_specs=in_specs,
+        out_specs=out_specs,
+        check_vma=False,
+    )

time: 86.5 us -> 38.2 us (0.44)
  the two profiles are of different devices: /device:TPU:0 before, /device:TPU:17 now
where the time goes in v1:
time: 38.2 us; the launch traced here: 38.1 us
  starting transfers between devices  16.5 us (43%)
  waiting for transfers between devices  13.8 us (36%)
  Pallas kernels  5.38 us (14%)
  local copies, waits for them, and re-layouts  1.59 us (4%)
  between operations  0.69 us (2%)
    ppermute x11, starting transfers between devices, per_device_eight(): lax.ppermute(a, axis, [(i, i ^ bit) for i in range(lax.axis_size(axis))])  16.5 us
    ppermute x11, waiting for transfers between devices, per_device_eight(): lax.ppermute(a, axis, [(i, i ^ bit) for i in range(lax.axis_size(axis))])  13.8 us
    pallas_call x5, Pallas kernels, _call(): pl.pallas_call(kernel, out_shape=outs, in_specs=[SMEM if a.ndim == 1 else...  5.38 us
    unnamed x8, local copies, waits for them, and re-layouts  1.59 us
  transfers between devices with their start and end apart: 11, of which 8 were waited for; matrix products, arithmetic and copies ran while one was open for 0% of the time, Pallas kernels for 4%

profile of v1, /device:TPU:17, one launch (start us, length us, event | category | flops | bytes accessed | tf_op | source)
XLA Modules:
  0.0 38.1 jit_solution(5701094756885535959)
XLA Ops:
  0.6 0.0 copy-start.2
  0.6 0.1 collective-permute-start
  0.7 2.3 %collective-permute-start.4 = (bf16[256,256]{1,0:T(8,128)(2,1)}, bf16[256,256]{1,0:T(8,128)(2,1)S(1)}, u32[]{:S(2)}, u32[]{:S(2)}) collective-permute-start(bf16[256,256]{1,0:T(8,128)(2,1)} %refs_4_.1), channel_id=1, source_target_pairs={{0,16},{4,20},{8,24},{12,28},{16,0},{20,4},{24,8},{28,12},{1,17},{... | collective-permute-start | bytes 393224 | tf_op jit(solution)/shard_map/ppermute | solution.py:162
  3.1 0.1 pad_add_fusion.refs_0_.at
  3.1 1.1 %collective-permute-done = s32[256]{0:T(256)S(1)} collective-permute-done((s32[256]{0:T(256)}, s32[256]{0:T(256)S(1)}, u32[]{:S(2)}, u32[]{:S(2)}) %collective-permute-start) | collective-permute-done | bytes 1056 | tf_op jit(solution)/shard_map/ppermute | solution.py:162
  4.2 0.0 copy-start.3
  4.2 0.0 copy-done.2
  4.2 0.7 %copy-done.3 = s32[256]{0:T(256)S(1)} copy-done((s32[256]{0:T(256)S(1)}, s32[256]{0:T(256)}, u32[]{:S(2)}) %copy-start.3) | copy-done | bytes 1048
  4.9 0.0 copy-start.1
  4.9 0.9 %copy-done.1 = bf16[256,256]{1,0:T(8,128)(2,1)S(1)} copy-done((bf16[256,256]{1,0:T(8,128)(2,1)S(1)}, bf16[256,256]{1,0:T(8,128)(2,1)}, u32[]{:S(2)}) %copy-start.1) | copy-done | bytes 131096
  5.8 1.2 %shard_map.67 = (bf16[144,256]{1,0:T(8,128)(2,1)S(1)}, bf16[144,256]{1,0:T(8,128)(2,1)S(1)}, bf16[144,256]{1,0:T(8,128)(2,1)S(1)}, bf16[144,256]{1,0:T(8,128)(2,1)S(1)}, s32[8,256]{1,0:T(8,128)S(1)}) custom-call(s32[2]{0:T(128)S(1)} %pad_add_fusion.refs_0_.at, s32[1,256]{1,0:T(1,128)S(1)} %bitcast.8, s32[1,256]{1,0:T(1,128)S(1)} %bitcast.9, ...), custom_call_target="tpu_custom_call" | custom-call | flops 67108864 | bytes 452616 | tf_op jit(solution)/shard_map/pallas_call | solution.py:146
  7.0 1.3 %collective-permute-start.1 = (bf16[144,256]{1,0:T(8,128)(2,1)S(1)}, bf16[144,256]{1,0:T(8,128)(2,1)S(1)}, u32[]{:S(2)}, u32[]{:S(2)}) collective-permute-start(bf16[144,256]{1,0:T(8,128)(2,1)S(1)} %get-tuple-element.18), channel_id=1, source_target_pairs={{0,4},{4,0},{8,12},{12,8},{16,20},{20,16},{24,28},{28,24},{1,5},{5... | collective-permute-start | bytes 221192 | tf_op jit(solution)/shard_map/ppermute | solution.py:162
  8.3 1.4 %collective-permute-start.2 = (bf16[144,256]{1,0:T(8,128)(2,1)S(1)}, bf16[144,256]{1,0:T(8,128)(2,1)S(1)}, u32[]{:S(2)}, u32[]{:S(2)}) collective-permute-start(bf16[144,256]{1,0:T(8,128)(2,1)S(1)} %get-tuple-element.19), channel_id=1, source_target_pairs={{0,8},{4,12},{8,0},{12,4},{16,24},{20,28},{24,16},{28,20},{1,9},{5... | collective-permute-start | bytes 221192 | tf_op jit(solution)/shard_map/ppermute | solution.py:162
  9.7 0.0 collective-permute-start.3
  9.7 0.0 collective-permute-done.4.rows
  9.7 0.3 shard_map.68
  10.0 1.3 %collective-permute-start.5 = (bf16[144,256]{1,0:T(8,128)(2,1)S(1)}, bf16[144,256]{1,0:T(8,128)(2,1)S(1)}, u32[]{:S(2)}, u32[]{:S(2)}) collective-permute-start(bf16[144,256]{1,0:T(8,128)(2,1)S(1)} %get-tuple-element.23), channel_id=1, source_target_pairs={{0,4},{4,0},{8,12},{12,8},{16,20},{20,16},{24,28},{28,24},{1,5},{5... | collective-permute-start | bytes 221192 | tf_op jit(solution)/shard_map/ppermute | solution.py:162
  11.3 1.6 %collective-permute-start.6 = (bf16[144,256]{1,0:T(8,128)(2,1)S(1)}, bf16[144,256]{1,0:T(8,128)(2,1)S(1)}, u32[]{:S(2)}, u32[]{:S(2)}) collective-permute-start(bf16[144,256]{1,0:T(8,128)(2,1)S(1)} %get-tuple-element.24), channel_id=1, source_target_pairs={{0,8},{4,12},{8,0},{12,4},{16,24},{20,28},{24,16},{28,20},{1,9},{5... | collective-permute-start | bytes 221192 | tf_op jit(solution)/shard_map/ppermute | solution.py:162
  12.9 0.0 collective-permute-done.1.refs_1_
  12.9 0.0 collective-permute-start.7
  12.9 0.0 collective-permute-done.2.refs_2_
  12.9 1.0 %collective-permute-done.3.refs_3_ = bf16[144,256]{1,0:T(8,128)(2,1)S(1)} collective-permute-done((bf16[144,256]{1,0:T(8,128)(2,1)S(1)}, bf16[144,256]{1,0:T(8,128)(2,1)S(1)}, u32[]{:S(2)}, u32[]{:S(2)}) %collective-permute-start.3) | collective-permute-done | bytes 73760 | tf_op jit(solution)/shard_map/ppermute | solution.py:162
  13.9 0.3 collective-permute-done.5.refs_5_
  14.3 0.8 %collective-permute-done.6.refs_6_ = bf16[144,256]{1,0:T(8,128)(2,1)S(1)} collective-permute-done((bf16[144,256]{1,0:T(8,128)(2,1)S(1)}, bf16[144,256]{1,0:T(8,128)(2,1)S(1)}, u32[]{:S(2)}, u32[]{:S(2)}) %collective-permute-start.6) | collective-permute-done | bytes 73760 | tf_op jit(solution)/shard_map/ppermute | solution.py:162
  15.1 2.0 %collective-permute-done.7.refs_7_ = bf16[144,256]{1,0:T(8,128)(2,1)S(1)} collective-permute-done((bf16[144,256]{1,0:T(8,128)(2,1)S(1)}, bf16[144,256]{1,0:T(8,128)(2,1)S(1)}, u32[]{:S(2)}, u32[]{:S(2)}) %collective-permute-start.7) | collective-permute-done | bytes 73760 | tf_op jit(solution)/shard_map/ppermute | solution.py:162
  17.0 1.2 %shard_map.69 = (f32[264,256]{1,0:T(8,128)S(1)}, f32[264,256]{1,0:T(8,128)S(1)}) custom-call(s32[2]{0:T(128)S(1)} %pad_add_fusion.refs_0_.at, bf16[144,256]{1,0:T(8,128)(2,1)S(1)} %get-tuple-element.17.refs_0_, bf16[144,256]{1,0:T(8,128)(2,1)S(1)} %collective-permute-done.1.refs_1_, bf16[144,256]{1,0:T(8,128)(2,1)S(1)} %collective-permute-done.2.refs_2_, ...), custom_call_target="tpu_custom_call" | custom-call | flops 268435456 | bytes 1130504 | tf_op jit(solution)/shard_map/pallas_call | solution.py:146
  18.3 5.9 %collective-permute-start.8 = (f32[264,256]{1,0:T(8,128)S(1)}, f32[264,256]{1,0:T(8,128)S(1)}, u32[]{:S(2)}, u32[]{:S(2)}) collective-permute-start(f32[264,256]{1,0:T(8,128)S(1)} %get-tuple-element.27), channel_id=1, source_target_pairs={{0,1},{1,0},{2,3},{3,2},{4,5},{5,4},{6,7},{7,6},{8,9},{9,8},{10,11... | collective-permute-start | bytes 811016 | tf_op jit(solution)/shard_map/ppermute | solution.py:162
  24.1 1.2 %collective-permute-done.8 = f32[264,256]{1,0:T(8,128)S(1)} collective-permute-done((f32[264,256]{1,0:T(8,128)S(1)}, f32[264,256]{1,0:T(8,128)S(1)}, u32[]{:S(2)}, u32[]{:S(2)}) %collective-permute-start.8) | collective-permute-done | bytes 270368 | tf_op jit(solution)/shard_map/ppermute | solution.py:162
  25.3 0.0 copy-start
  25.4 1.3 %collective-permute-start.9 = (f32[264,256]{1,0:T(8,128)S(1)}, f32[264,256]{1,0:T(8,128)S(1)}, u32[]{:S(2)}, u32[]{:S(2)}) collective-permute-start(f32[264,256]{1,0:T(8,128)S(1)} %add.3.part), channel_id=1, source_target_pairs={{0,2},{1,3},{2,0},{3,1},{4,6},{5,7},{6,4},{7,5},{8,10},{9,11},{10,... | collective-permute-start | bytes 811016 | tf_op jit(solution)/shard_map/ppermute | solution.py:162
  26.6 6.5 %collective-permute-done.9.got = f32[264,256]{1,0:T(8,128)S(1)} collective-permute-done((f32[264,256]{1,0:T(8,128)S(1)}, f32[264,256]{1,0:T(8,128)S(1)}, u32[]{:S(2)}, u32[]{:S(2)}) %collective-permute-start.9) | collective-permute-done | bytes 270368 | tf_op jit(solution)/shard_map/ppermute | solution.py:162
  33.1 0.0 copy-done
  33.1 0.7 %shard_map.70.refs_8_ = bf16[256,256]{1,0:T(8,128)(2,1)S(1)} custom-call(s32[2]{0:T(128)S(1)} %pad_add_fusion.refs_0_.at, f32[264,256]{1,0:T(8,128)S(1)} %add.3.part, f32[264,256]{1,0:T(8,128)S(1)} %collective-permute-done.9.got, bf16[512,256]{1,0:T(8,128)(2,1)S(1)} %copy-done), custom_call_target="tpu_custom_call" | custom-call | bytes 933896 | tf_op jit(solution)/shard_map/pallas_call | solution.py:146
  33.8 1.3 %collective-permute-start.10 = (bf16[256,256]{1,0:T(8,128)(2,1)S(1)}, bf16[256,256]{1,0:T(8,128)(2,1)S(1)}, u32[]{:S(2)}, u32[]{:S(2)}) collective-permute-start(bf16[256,256]{1,0:T(8,128)(2,1)S(1)} %shard_map.70.refs_8_), channel_id=1, source_target_pairs={{0,1},{1,0},{2,3},{3,2},{4,5},{5,4},{6,7},{7,6},{8,9},{9,8},{10,11... | collective-permute-start | bytes 393224 | tf_op jit(solution)/shard_map/ppermute | solution.py:162
  35.1 1.0 %collective-permute-done.10.refs_9_ = bf16[256,256]{1,0:T(8,128)(2,1)S(1)} collective-permute-done((bf16[256,256]{1,0:T(8,128)(2,1)S(1)}, bf16[256,256]{1,0:T(8,128)(2,1)S(1)}, u32[]{:S(2)}, u32[]{:S(2)}) %collective-permute-start.10) | collective-permute-done | bytes 131104 | tf_op jit(solution)/shard_map/ppermute | solution.py:162
  36.0 2.0 %shard_map.71 = (bf16[512,256]{1,0:T(8,128)(2,1)}, bf16[1024,256]{1,0:T(8,128)(2,1)}, f32[8,128]{1,0:T(8,128)}) custom-call(s32[2]{0:T(128)S(1)} %pad_add_fusion.refs_0_.at, bf16[144,256]{1,0:T(8,128)(2,1)S(1)} %get-tuple-element.17.refs_0_, bf16[144,256]{1,0:T(8,128)(2,1)S(1)} %collective-permute-done.1.refs_1_, ...), custom_call_target="tpu_custom_call" | custom-call | flops 268435456 | bytes 1642504 | tf_op jit(solution)/shard_map/pallas_call | solution.py:146
  (1 shorter events, 0.0 us)
Async XLA Ops:
  0.6 3.6 %copy-start.2 = (s32[4096]{0:T(1024)S(1)}, s32[4096]{0:T(1024)}, u32[]{:S(2)}) copy-start(s32[4096]{0:T(1024)} %param.6) | copy-start | bytes 49156
  0.6 3.6 %collective-permute-start = (s32[256]{0:T(256)}, s32[256]{0:T(256)S(1)}, u32[]{:S(2)}, u32[]{:S(2)}) collective-permute-start(s32[256]{0:T(256)} %param.5), channel_id=1, source_target_pairs={{0,16},{4,20},{8,24},{12,28},{16,0},{20,4},{24,8},{28,12},{1,17},{... | collective-permute-start | bytes 3080 | tf_op jit(solution)/shard_map/ppermute | solution.py:162
  0.7 9.0 %collective-permute-start.4 = (bf16[256,256]{1,0:T(8,128)(2,1)}, bf16[256,256]{1,0:T(8,128)(2,1)S(1)}, u32[]{:S(2)}, u32[]{:S(2)}) collective-permute-start(bf16[256,256]{1,0:T(8,128)(2,1)} %refs_4_.1), channel_id=1, source_target_pairs={{0,16},{4,20},{8,24},{12,28},{16,0},{20,4},{24,8},{28,12},{1,17},{... | collective-permute-start | bytes 393224 | tf_op jit(solution)/shard_map/ppermute | solution.py:162
  4.2 0.7 %copy-start.3 = (s32[256]{0:T(256)S(1)}, s32[256]{0:T(256)}, u32[]{:S(2)}) copy-start(s32[256]{0:T(256)} %param.5) | copy-start | bytes 3076
  4.9 0.9 %copy-start.1 = (bf16[256,256]{1,0:T(8,128)(2,1)S(1)}, bf16[256,256]{1,0:T(8,128)(2,1)}, u32[]{:S(2)}) copy-start(bf16[256,256]{1,0:T(8,128)(2,1)} %refs_4_.1) | copy-start | bytes 393220
  7.0 5.9 %collective-permute-start.1 = (bf16[144,256]{1,0:T(8,128)(2,1)S(1)}, bf16[144,256]{1,0:T(8,128)(2,1)S(1)}, u32[]{:S(2)}, u32[]{:S(2)}) collective-permute-start(bf16[144,256]{1,0:T(8,128)(2,1)S(1)} %get-tuple-element.18), channel_id=1, source_target_pairs={{0,4},{4,0},{8,12},{12,8},{16,20},{20,16},{24,28},{28,24},{1,5},{5... | collective-permute-start | bytes 221192 | tf_op jit(solution)/shard_map/ppermute | solution.py:162
  8.3 4.6 %collective-permute-start.2 = (bf16[144,256]{1,0:T(8,128)(2,1)S(1)}, bf16[144,256]{1,0:T(8,128)(2,1)S(1)}, u32[]{:S(2)}, u32[]{:S(2)}) collective-permute-start(bf16[144,256]{1,0:T(8,128)(2,1)S(1)} %get-tuple-element.19), channel_id=1, source_target_pairs={{0,8},{4,12},{8,0},{12,4},{16,24},{20,28},{24,16},{28,20},{1,9},{5... | collective-permute-start | bytes 221192 | tf_op jit(solution)/shard_map/ppermute | solution.py:162
  9.7 4.2 %collective-permute-start.3 = (bf16[144,256]{1,0:T(8,128)(2,1)S(1)}, bf16[144,256]{1,0:T(8,128)(2,1)S(1)}, u32[]{:S(2)}, u32[]{:S(2)}) collective-permute-start(bf16[144,256]{1,0:T(8,128)(2,1)S(1)} %get-tuple-element.20), channel_id=1, source_target_pairs={{0,12},{4,8},{8,4},{12,0},{16,28},{20,24},{24,20},{28,16},{1,13},{... | collective-permute-start | bytes 221192 | tf_op jit(solution)/shard_map/ppermute | solution.py:162
  10.0 4.2 %collective-permute-start.5 = (bf16[144,256]{1,0:T(8,128)(2,1)S(1)}, bf16[144,256]{1,0:T(8,128)(2,1)S(1)}, u32[]{:S(2)}, u32[]{:S(2)}) collective-permute-start(bf16[144,256]{1,0:T(8,128)(2,1)S(1)} %get-tuple-element.23), channel_id=1, source_target_pairs={{0,4},{4,0},{8,12},{12,8},{16,20},{20,16},{24,28},{28,24},{1,5},{5... | collective-permute-start | bytes 221192 | tf_op jit(solution)/shard_map/ppermute | solution.py:162
  11.3 3.8 %collective-permute-start.6 = (bf16[144,256]{1,0:T(8,128)(2,1)S(1)}, bf16[144,256]{1,0:T(8,128)(2,1)S(1)}, u32[]{:S(2)}, u32[]{:S(2)}) collective-permute-start(bf16[144,256]{1,0:T(8,128)(2,1)S(1)} %get-tuple-element.24), channel_id=1, source_target_pairs={{0,8},{4,12},{8,0},{12,4},{16,24},{20,28},{24,16},{28,20},{1,9},{5... | collective-permute-start | bytes 221192 | tf_op jit(solution)/shard_map/ppermute | solution.py:162
  12.9 4.1 %collective-permute-start.7 = (bf16[144,256]{1,0:T(8,128)(2,1)S(1)}, bf16[144,256]{1,0:T(8,128)(2,1)S(1)}, u32[]{:S(2)}, u32[]{:S(2)}) collective-permute-start(bf16[144,256]{1,0:T(8,128)(2,1)S(1)} %get-tuple-element.25), channel_id=1, source_target_pairs={{0,12},{4,8},{8,4},{12,0},{16,28},{20,24},{24,20},{28,16},{1,13},{... | collective-permute-start | bytes 221192 | tf_op jit(solution)/shard_map/ppermute | solution.py:162
  18.3 7.1 %collective-permute-start.8 = (f32[264,256]{1,0:T(8,128)S(1)}, f32[264,256]{1,0:T(8,128)S(1)}, u32[]{:S(2)}, u32[]{:S(2)}) collective-permute-start(f32[264,256]{1,0:T(8,128)S(1)} %get-tuple-element.27), channel_id=1, source_target_pairs={{0,1},{1,0},{2,3},{3,2},{4,5},{5,4},{6,7},{7,6},{8,9},{9,8},{10,11... | collective-permute-start | bytes 811016 | tf_op jit(solution)/shard_map/ppermute | solution.py:162
  25.3 7.8 %copy-start = (bf16[512,256]{1,0:T(8,128)(2,1)S(1)}, bf16[512,256]{1,0:T(8,128)(2,1)}, u32[]{:S(2)}) copy-start(bf16[512,256]{1,0:T(8,128)(2,1)} %old.1) | copy-start | bytes 786436
  25.4 7.8 %collective-permute-start.9 = (f32[264,256]{1,0:T(8,128)S(1)}, f32[264,256]{1,0:T(8,128)S(1)}, u32[]{:S(2)}, u32[]{:S(2)}) collective-permute-start(f32[264,256]{1,0:T(8,128)S(1)} %add.3.part), channel_id=1, source_target_pairs={{0,2},{1,3},{2,0},{3,1},{4,6},{5,7},{6,4},{7,5},{8,10},{9,11},{10,... | collective-permute-start | bytes 811016 | tf_op jit(solution)/shard_map/ppermute | solution.py:162
  33.8 2.3 %collective-permute-start.10 = (bf16[256,256]{1,0:T(8,128)(2,1)S(1)}, bf16[256,256]{1,0:T(8,128)(2,1)S(1)}, u32[]{:S(2)}, u32[]{:S(2)}) collective-permute-start(bf16[256,256]{1,0:T(8,128)(2,1)S(1)} %shard_map.70.refs_8_), channel_id=1, source_target_pairs={{0,1},{1,0},{2,3},{3,2},{4,5},{5,4},{6,7},{7,6},{8,9},{9,8},{10,11... | collective-permute-start | bytes 393224 | tf_op jit(solution)/shard_map/ppermute | solution.py:162

commit v2 on v0

--- a/solution.py
+++ b/solution.py
@@ -1,7 +1,246 @@
 import jax
 import jax.numpy as jnp
 from jax import lax
+from jax.experimental import pallas as pl
+from jax.experimental.pallas import tpu as pltpu
 from jax.sharding import PartitionSpec as P
+
+HEAD = 16
+VMEM = pl.BlockSpec(memory_space=pltpu.VMEM)
+
+
+def _log2(n):
+    return n.bit_length() - 1
+
+
+def _iota(shape, dim):
+    return lax.broadcasted_iota(jnp.int32, shape, dim)
+
+
+def _bf16(a):
+    return a.astype(jnp.float32).astype(jnp.bfloat16)
+
+
+def _slots(table, assign):
+    t, n = table.shape[0], assign.shape[1]
+    hot = _bf16(_iota((t, n), 0) == (assign >> 7))
+    lane = _iota((128, n), 0) == (assign & 127)
+
+    def pick(part):
+        rows = lax.dot_general(
+            _bf16(part), hot, (((0,), (0,)), ((), ())), preferred_element_type=jnp.float32
+        )
+        return jnp.sum(jnp.where(lane, rows, 0.0), axis=0, keepdims=True)
+
+    return (pick(table & 255) + 256.0 * pick(table >> 8)).astype(jnp.int32)
+
+
+def _head(list_dev, base, table, assign):
+    n = assign.shape[1]
+    slot = _slots(table, assign)
+    relative = (slot >> _log2(list_dev)) ^ base
+    code = (slot & (list_dev - 1)) + 1
+    member = (_iota((16, n), 0) == relative).astype(jnp.float32)
+    before = _bf16(_iota((n, n), 0) < _iota((n, n), 1))
+    count = jnp.dot(member.astype(jnp.bfloat16), before, preferred_element_type=jnp.float32)
+    head = jnp.where(member > 0.0, count, -1.0).astype(jnp.int32)[0:8, :]
+    row = _iota((8, n), 0)
+    head = jnp.where(row == 4, code & 255, head)
+    return jnp.where(row == 5, code >> 8, head)
+
+
+def _route(head, rows, outs, half):
+    n = rows.shape[0]
+    capacity = rows.shape[1] // 2
+    base = half * (capacity + HEAD)
+    hot = jnp.concatenate(
+        [(_iota((capacity, n), 0) == head[k : k + 1, :]).astype(jnp.float32) for k in range(len(outs))],
+        axis=0,
+    ).astype(jnp.bfloat16)
+    moved = jnp.dot(hot, rows, preferred_element_type=jnp.float32).astype(jnp.bfloat16)
+    lo, hi = head[4:5, :].astype(jnp.float32), head[5:6, :].astype(jnp.float32)
+    values = jnp.where(_iota((HEAD, n), 0) == 0, lo, hi).astype(jnp.bfloat16)
+    labels = lax.dot_general(
+        values, hot, (((1,), (1,)), ((), ())), preferred_element_type=jnp.float32
+    )
+    for i, out in enumerate(outs):
+        part = labels[:, i * capacity : (i + 1) * capacity]
+        line = jnp.concatenate([part[0:1, :], part[1:2, :]], axis=1)
+        out[base : base + capacity, :] = moved[i * capacity : (i + 1) * capacity, :]
+        out[base + capacity : base + capacity + HEAD, :] = jnp.broadcast_to(
+            line, (HEAD, line.shape[1])
+        ).astype(jnp.bfloat16)
+
+
+def _payload_head(list_dev, base, table, payload):
+    n = payload.shape[0] - HEAD
+    low = payload[n:, :].astype(jnp.float32)
+    assign = (low[0:1, :] + 256.0 * low[1:2, :]).astype(jnp.int32)
+    return _head(list_dev, base, table[...], assign)
+
+
+def _pair_kernel(list_dev, mine, side, table, o0, o1, o2, o3):
+    n = mine.shape[0] - HEAD
+    for half, payload in enumerate((mine, side)):
+        head = _payload_head(list_dev, lax.axis_index("items"), table, payload)
+        _route(head, payload[0:n, :], (o0, o1, o2, o3), half)
+
+
+def _labels(head):
+    head = head.astype(jnp.float32)[0:1, :]
+    capacity = head.shape[1] // 2
+    return (head[:, :capacity] + 256.0 * head[:, capacity:]).astype(jnp.int32) - 1
+
+
+def _parts(block):
+    capacity = block.shape[1] // 2
+    size = capacity + HEAD
+    return [
+        (block[i : i + capacity, :], _labels(block[i + capacity : i + size, :]))
+        for i in range(0, block.shape[0], size)
+    ]
+
+
+def _totals(blocks, lists):
+    rows = jnp.concatenate([r for r, _ in blocks], axis=0)
+    labels = jnp.concatenate([l for _, l in blocks], axis=1)
+    hot = (_iota((lists, rows.shape[0]), 0) == labels).astype(jnp.float32)
+    sums = jnp.dot(hot.astype(jnp.bfloat16), rows, preferred_element_type=jnp.float32)
+    return sums, jnp.sum(hot, axis=1, keepdims=True)
+
+
+def _both_planes(pairs, lists):
+    parts = [_parts(p) for p in pairs]
+    mine, mine_n = _totals([p[0] for p in parts], lists)
+    side, side_n = _totals([p[1] for p in parts], lists)
+    width = mine.shape[1]
+    eye = _iota((width, width), 0) == _iota((width, width), 1)
+    count = mine_n + side_n
+    lines = [
+        jnp.sum(jnp.where(eye, count[i : i + width, :], 0.0), axis=0, keepdims=True)
+        for i in range(0, lists, width)
+    ]
+    row = _iota((8, width), 0)
+    count = jnp.zeros((8, width), jnp.float32)
+    for i, line in enumerate(lines):
+        count = jnp.where(row == i, line, count)
+    return mine + side, count
+
+
+def _early_kernel(p0, p1, p2, p3, q0, out):
+    lists = out.shape[0] - 8
+    out[0:lists, :], out[lists:, :] = _both_planes((p0, p1, p2, p3, q0), lists)
+
+
+def _late_kernel(early, q1, q2, q3, out):
+    lists = out.shape[0] - 8
+    sums, count = _both_planes((q1, q2, q3), lists)
+    out[0:lists, :] = early[0:lists, :] + sums
+    out[lists:, :] = early[lists:, :] + count
+
+
+def _codes_kernel(mine, other, old, *refs):
+    (*blocks, fresh, codes, scales) = refs
+    lists, width = fresh.shape
+    capacity = width // 2
+    me = lax.axis_index("items")
+    wide = _iota((width, width), 0) == _iota((width, width), 1)
+    for i in range(lists // width):
+        row = mine[lists + i : lists + i + 1, :] + other[lists + i : lists + i + 1, :]
+        counts = jnp.sum(jnp.where(wide, row, 0.0), axis=1, keepdims=True)
+        at_i = slice(i * width, (i + 1) * width)
+        total = mine[at_i, :] + other[at_i, :] + old[at_i, :].astype(jnp.float32)
+        fresh[at_i, :] = (total / (counts + 1.0)).astype(jnp.bfloat16)
+    table = fresh[...]
+    eye = _iota((capacity, capacity), 0) == _iota((capacity, capacity), 1)
+    for k, (rows, labels) in enumerate(_parts(b)[0] for b in blocks):
+        column = jnp.sum(
+            jnp.where(eye, labels.astype(jnp.float32), 0.0), axis=1, keepdims=True
+        ).astype(jnp.int32)
+        hot = _bf16(_iota((capacity, lists), 1) == column)
+        lookup = jnp.dot(hot, table, preferred_element_type=jnp.float32)
+        residual = rows.astype(jnp.float32) - lookup
+        amax = jnp.max(jnp.abs(residual), axis=1, keepdims=True)
+        source = me ^ k
+        codes[pl.ds(pl.multiple_of(source * capacity, capacity), capacity), :] = (
+            residual * (127.0 / (amax + 1e-06))
+        ).astype(jnp.bfloat16)
+        scales[pl.ds(source, 1), :] = jnp.sum(
+            jnp.where(eye, amax / 127.0, 0.0), axis=0, keepdims=True
+        )
+
+
+def _call(kernel, outs, args, flops=0, **options):
+    moved = sum(a.size * a.dtype.itemsize for a in args) + sum(
+        o.size * o.dtype.itemsize for o in outs
+    )
+    limit = options.pop("limit", 24 * 2**20)
+    return pl.pallas_call(
+        kernel,
+        out_shape=outs,
+        in_specs=[VMEM] * len(args),
+        out_specs=[VMEM] * len(outs),
+        compiler_params=pltpu.CompilerParams(vmem_limit_bytes=limit),
+        cost_estimate=pl.CostEstimate(flops=flops, bytes_accessed=moved, transcendentals=0),
+        **options,
+    )(*args)
+
+
+def per_device_eight(embeds, assign, list_slot, old_centroids):
+    list_dev, width = old_centroids.shape
+    item_dev = embeds.shape[0]
+    peers, reps = lax.axis_size("items"), lax.axis_size("rep")
+    capacity = 4 * item_dev // peers
+
+    def hop(a, items, rep=0):
+        swap = items * reps + rep
+        return lax.ppermute(a, ("items", "rep"), [(i, i ^ swap) for i in range(peers * reps)])
+
+    table = list_slot.reshape(-1, 128)
+    pair = jax.ShapeDtypeStruct((2 * (capacity + HEAD), width), jnp.bfloat16)
+    flops = 2 * 8 * capacity * item_dev * width
+    row = lax.broadcasted_iota(jnp.int32, (item_dev + HEAD, width), 0)
+    ids = jnp.where(row == item_dev, assign & 255, assign >> 8).astype(jnp.bfloat16)
+    payload = jnp.where(row < item_dev, jnp.pad(embeds, ((0, HEAD), (0, 0))), ids)
+    far = hop(payload, 4)
+    side = hop(payload, 0, 2)
+
+    def routed(mine, side):
+        return _call(
+            lambda *refs: _pair_kernel(list_dev, *refs),
+            [pair] * 4,
+            (mine, side, table),
+            flops=flops,
+        )
+
+    def to_owners(pairs):
+        return [pairs[0]] + [hop(pairs[k], k) for k in (3, 2, 1)][::-1]
+
+    near = routed(payload, side)
+    far, *near = lax.optimization_barrier((far, *near))
+    far_side = hop(far, 0, 2)
+    near = to_owners(near)
+    away = to_owners(routed(far, far_side))
+    total = jax.ShapeDtypeStruct((list_dev + 8, width), jnp.float32)
+    flops = 2 * list_dev * capacity * width
+    (early,) = _call(_early_kernel, [total], (*near, away[0]), flops=10 * flops)
+    (mine,) = _call(_late_kernel, [total], (early, *away[1:]), flops=6 * flops)
+    other = hop(mine, 0, 1)
+    fresh, codes, scales = _call(
+        _codes_kernel,
+        [
+            jax.ShapeDtypeStruct((list_dev, width), jnp.bfloat16),
+            jax.ShapeDtypeStruct((peers * capacity, width), jnp.bfloat16),
+            jax.ShapeDtypeStruct((peers, capacity), jnp.float32),
+        ],
+        (mine, other, old_centroids, *near, *away),
+        flops=8 * flops,
+    )
+    return (
+        fresh,
+        codes.reshape(1, 1, peers * capacity, width),
+        scales.reshape(1, 1, peers * capacity),
+    )
 
 
 def per_device(embeds, assign, list_slot, old_centroids):
@@ -58,6 +297,11 @@
 def solution(mesh):
     in_specs = (P(("items", "rep"), None), P(("items", "rep")), P(), P("items", None))
     out_specs = (P("items", None), P("items", "rep", None, None), P("items", "rep", None))
+    small = mesh.shape["items"] == 8 and mesh.shape["rep"] == 4
     return jax.shard_map(
-        per_device, mesh=mesh, in_specs=in_specs, out_specs=out_specs, check_vma=False
-    )
+        per_device_eight if small else per_device,
+        mesh=mesh,
+        in_specs=in_specs,
+        out_specs=out_specs,
+        check_vma=False,
+    )

time: 86.5 us -> 35.2 us (0.41)
  blocking collectives: 21.4 us -> 0 us
  waiting for transfers between devices: 30.5 us -> 14.4 us
  between operations: 14.1 us -> 0.71 us
  local copies, waits for them, and re-layouts: 7.31 us -> 0.67 us
  starting transfers between devices: 7.32 us -> 13.2 us
  Pallas kernels: 0 us -> 5 us
  other arithmetic: 3.61 us -> 1.06 us
  matrix products: 1.88 us -> 0 us
    psum x1 -> x0, waiting for transfers between devices: 26.4 us -> none  [per_device(): total_sums, total_counts = lax.psum((partial_sums, partial_counts), 'rep')]
    all_to_all x1 -> x0, blocking collectives: 15.7 us -> none  [per_device(): lax.all_to_all(outgoing.reshape(peers, capacity, width), 'items', split_a...]
    ppermute x0 -> x10, waiting for transfers between devices: none -> 14.4 us  [hop(): lax.ppermute(a, ('items', 'rep'), [(i, i ^ swap) for i in range(peers * r...]
    ppermute x0 -> x10, starting transfers between devices: none -> 13.2 us  [hop(): lax.ppermute(a, ('items', 'rep'), [(i, i ^ swap) for i in range(peers * r...]
    all_to_all x1 -> x0, starting transfers between devices: 7.28 us -> none  [per_device(): lax.all_to_all(labels.reshape(peers, capacity), 'items', split_axis=0, co...]
    psum x1 -> x0, blocking collectives: 5.66 us -> none  [per_device(): total_sums, total_counts = lax.psum((partial_sums, partial_counts), 'rep')]
    pallas_call x0 -> x5, Pallas kernels: none -> 5 us  [_call(): pl.pallas_call(kernel, out_shape=outs, in_specs=[VMEM] * len(args), out_s...]
    all_to_all x1 -> x0, waiting for transfers between devices: 4.05 us -> none  [per_device(): lax.all_to_all(labels.reshape(peers, capacity), 'items', split_axis=0, co...]
  transfers between devices with their start and end apart: 2 -> 10, of which waited for: 2 -> 8; matrix products, arithmetic and copies ran while one was open for 3% -> 0% of each run, Pallas kernels for 0% -> 8%
where the time goes in v2:
time: 35.2 us; the launch traced here: 35 us
  waiting for transfers between devices  14.4 us (41%)
  starting transfers between devices  13.2 us (38%)
  Pallas kernels  5 us (14%)
  other arithmetic  1.06 us (3%)
  between operations  0.71 us (2%)
  local copies, waits for them, and re-layouts  0.67 us (2%)
    ppermute x10, waiting for transfers between devices, hop(): lax.ppermute(a, ('items', 'rep'), [(i, i ^ swap) for i in range(peers * r...  14.4 us
    ppermute x10, starting transfers between devices, hop(): lax.ppermute(a, ('items', 'rep'), [(i, i ^ swap) for i in range(peers * r...  13.2 us
    pallas_call x5, Pallas kernels, _call(): pl.pallas_call(kernel, out_shape=outs, in_specs=[VMEM] * len(args), out_s...  5 us
    select_n x1, other arithmetic, per_device_eight(): jnp.where(row < item_dev, jnp.pad(embeds, ((0, HEAD), (0, 0))), ids)  1.05 us
  transfers between devices with their start and end apart: 10, of which 8 were waited for; matrix products, arithmetic and copies ran while one was open for 0% of the time, Pallas kernels for 8%

profile of v2, /device:TPU:0, one launch (start us, length us, event | category | flops | bytes accessed | tf_op | source)
XLA Modules:
  0.0 35.0 jit_solution(12306180068095176033)
XLA Ops:
  0.6 0.0 copy-start.2
  0.7 0.7 %copy-done.2 = s32[256]{0:T(256)S(1)} copy-done((s32[256]{0:T(256)S(1)}, s32[256]{0:T(256)}, u32[]{:S(2)}) %copy-start.2) | copy-done | bytes 1048
  1.3 0.0 copy-start.1
  1.3 1.1 %fusion.refs_0_ = bf16[272,256]{1,0:T(8,128)(2,1)S(1)} fusion(s32[256]{0:T(256)S(1)} %get-tuple-element.36, s32[256]{0:T(256)S(1)} %get-tuple-element.35, bf16[256,256]{1,0:T(8,128)(2,1)} %param.4, pred[272]{0:T(512)(128)(4,1)S(1)} %get-tuple-element.37, pred[272]{0:T(512)(128)(4,1)S(1)} %get-tuple-element.38), kind=kLoop, calls=%fused_computation.1 | loop fusion | flops 208896 | bytes 272928 | tf_op jit(solution)/shard_map/jit(_where)/select_n | solution.py:204
  2.4 3.0 %collective-permute-start.1 = (bf16[272,256]{1,0:T(8,128)(2,1)S(1)}, bf16[272,256]{1,0:T(8,128)(2,1)S(1)}, u32[]{:S(2)}, u32[]{:S(2)}) collective-permute-start(bf16[272,256]{1,0:T(8,128)(2,1)S(1)} %fusion.refs_0_), channel_id=1, source_target_pairs={{0,2},{1,3},{2,0},{3,1},{4,6},{5,7},{6,4},{7,5},{8,10},{9,11},{10,... | collective-permute-start | bytes 417800 | tf_op jit(solution)/shard_map/ppermute | solution.py:197
  5.4 2.6 %collective-permute-start = (bf16[272,256]{1,0:T(8,128)(2,1)S(1)}, bf16[272,256]{1,0:T(8,128)(2,1)S(1)}, u32[]{:S(2)}, u32[]{:S(2)}) collective-permute-start(bf16[272,256]{1,0:T(8,128)(2,1)S(1)} %fusion.refs_0_), channel_id=1, source_target_pairs={{0,16},{1,17},{2,18},{3,19},{4,20},{5,21},{6,22},{7,23},{8,24},{9,... | collective-permute-start | bytes 417800 | tf_op jit(solution)/shard_map/ppermute | solution.py:197
  8.0 1.1 %collective-permute-done.1.refs_1_ = bf16[272,256]{1,0:T(8,128)(2,1)S(1)} collective-permute-done((bf16[272,256]{1,0:T(8,128)(2,1)S(1)}, bf16[272,256]{1,0:T(8,128)(2,1)S(1)}, u32[]{:S(2)}, u32[]{:S(2)}) %collective-permute-start.1) | collective-permute-done | bytes 139296 | tf_op jit(solution)/shard_map/ppermute | solution.py:197
  9.1 0.0 copy-done.1
  9.1 1.0 %shard_map.67 = (bf16[288,256]{1,0:T(8,128)(2,1)S(1)}, bf16[288,256]{1,0:T(8,128)(2,1)S(1)}, bf16[288,256]{1,0:T(8,128)(2,1)S(1)}, bf16[288,256]{1,0:T(8,128)(2,1)S(1)}) custom-call(bf16[272,256]{1,0:T(8,128)(2,1)S(1)} %fusion.refs_0_, bf16[272,256]{1,0:T(8,128)(2,1)S(1)} %collective-permute-done.1.refs_1_, s32[32,128]{1,0:T(8,128)S(1)} %bitcast.3), custom_call_target="tpu_custom_call" | custom-call | flops 134217728 | bytes 884736 | tf_op jit(solution)/shard_map/pallas_call | solution.py:178
  10.1 4.3 %collective-permute-done.refs_0_ = bf16[272,256]{1,0:T(8,128)(2,1)S(1)} collective-permute-done((bf16[272,256]{1,0:T(8,128)(2,1)S(1)}, bf16[272,256]{1,0:T(8,128)(2,1)S(1)}, u32[]{:S(2)}, u32[]{:S(2)}) %collective-permute-start) | collective-permute-done | bytes 139296 | tf_op jit(solution)/shard_map/ppermute | solution.py:197
  14.4 0.5 %collective-permute-start.5 = (bf16[272,256]{1,0:T(8,128)(2,1)S(1)}, bf16[272,256]{1,0:T(8,128)(2,1)S(1)}, u32[]{:S(2)}, u32[]{:S(2)}) collective-permute-start(bf16[272,256]{1,0:T(8,128)(2,1)S(1)} %collective-permute-done.refs_0_), channel_id=1, source_target_pairs={{0,2},{1,3},{2,0},{3,1},{4,6},{5,7},{6,4},{7,5},{8,10},{9,11},{10,... | collective-permute-start | bytes 417800 | tf_op jit(solution)/shard_map/ppermute | solution.py:197
  14.9 1.6 %collective-permute-start.2 = (bf16[288,256]{1,0:T(8,128)(2,1)S(1)}, bf16[288,256]{1,0:T(8,128)(2,1)S(1)}, u32[]{:S(2)}, u32[]{:S(2)}) collective-permute-start(bf16[288,256]{1,0:T(8,128)(2,1)S(1)} %get-tuple-element.24), channel_id=1, source_target_pairs={{0,4},{1,5},{2,6},{3,7},{4,0},{5,1},{6,2},{7,3},{8,12},{9,13},{10,... | collective-permute-start | bytes 442376 | tf_op jit(solution)/shard_map/ppermute | solution.py:197
  16.5 0.7 %collective-permute-start.3 = (bf16[288,256]{1,0:T(8,128)(2,1)S(1)}, bf16[288,256]{1,0:T(8,128)(2,1)S(1)}, u32[]{:S(2)}, u32[]{:S(2)}) collective-permute-start(bf16[288,256]{1,0:T(8,128)(2,1)S(1)} %get-tuple-element.25), channel_id=1, source_target_pairs={{0,8},{1,9},{2,10},{3,11},{4,12},{5,13},{6,14},{7,15},{8,0},{9,1},... | collective-permute-start | bytes 442376 | tf_op jit(solution)/shard_map/ppermute | solution.py:197
  17.1 1.2 %collective-permute-start.4 = (bf16[288,256]{1,0:T(8,128)(2,1)S(1)}, bf16[288,256]{1,0:T(8,128)(2,1)S(1)}, u32[]{:S(2)}, u32[]{:S(2)}) collective-permute-start(bf16[288,256]{1,0:T(8,128)(2,1)S(1)} %get-tuple-element.26), channel_id=1, source_target_pairs={{0,12},{1,13},{2,14},{3,15},{4,8},{5,9},{6,10},{7,11},{8,4},{9,5},... | collective-permute-start | bytes 442376 | tf_op jit(solution)/shard_map/ppermute | solution.py:197
  18.4 1.1 %collective-permute-done.5.refs_1_ = bf16[272,256]{1,0:T(8,128)(2,1)S(1)} collective-permute-done((bf16[272,256]{1,0:T(8,128)(2,1)S(1)}, bf16[272,256]{1,0:T(8,128)(2,1)S(1)}, u32[]{:S(2)}, u32[]{:S(2)}) %collective-permute-start.5) | collective-permute-done | bytes 139296 | tf_op jit(solution)/shard_map/ppermute | solution.py:197
  19.5 1.0 %shard_map.68 = (bf16[288,256]{1,0:T(8,128)(2,1)S(1)}, bf16[288,256]{1,0:T(8,128)(2,1)S(1)}, bf16[288,256]{1,0:T(8,128)(2,1)S(1)}, bf16[288,256]{1,0:T(8,128)(2,1)S(1)}) custom-call(bf16[272,256]{1,0:T(8,128)(2,1)S(1)} %collective-permute-done.refs_0_, bf16[272,256]{1,0:T(8,128)(2,1)S(1)} %collective-permute-done.5.refs_1_, s32[32,128]{1,0:T(8,128)S(1)} %bitcast.4), custom_call_target="tpu_custom_call" | custom-call | flops 134217728 | bytes 884736 | tf_op jit(solution)/shard_map/pallas_call | solution.py:178
  20.5 1.6 %collective-permute-start.6 = (bf16[288,256]{1,0:T(8,128)(2,1)S(1)}, bf16[288,256]{1,0:T(8,128)(2,1)S(1)}, u32[]{:S(2)}, u32[]{:S(2)}) collective-permute-start(bf16[288,256]{1,0:T(8,128)(2,1)S(1)} %get-tuple-element.29), channel_id=1, source_target_pairs={{0,4},{1,5},{2,6},{3,7},{4,0},{5,1},{6,2},{7,3},{8,12},{9,13},{10,... | collective-permute-start | bytes 442376 | tf_op jit(solution)/shard_map/ppermute | solution.py:197
  22.1 1.2 %collective-permute-start.7 = (bf16[288,256]{1,0:T(8,128)(2,1)S(1)}, bf16[288,256]{1,0:T(8,128)(2,1)S(1)}, u32[]{:S(2)}, u32[]{:S(2)}) collective-permute-start(bf16[288,256]{1,0:T(8,128)(2,1)S(1)} %get-tuple-element.30), channel_id=1, source_target_pairs={{0,8},{1,9},{2,10},{3,11},{4,12},{5,13},{6,14},{7,15},{8,0},{9,1},... | collective-permute-start | bytes 442376 | tf_op jit(solution)/shard_map/ppermute | solution.py:197
  23.3 0.0 collective-permute-done.2.p1.refs_1_
  23.3 0.8 %collective-permute-start.8 = (bf16[288,256]{1,0:T(8,128)(2,1)S(1)}, bf16[288,256]{1,0:T(8,128)(2,1)S(1)}, u32[]{:S(2)}, u32[]{:S(2)}) collective-permute-start(bf16[288,256]{1,0:T(8,128)(2,1)S(1)} %get-tuple-element.31), channel_id=1, source_target_pairs={{0,12},{1,13},{2,14},{3,15},{4,8},{5,9},{6,10},{7,11},{8,4},{9,5},... | collective-permute-start | bytes 442376 | tf_op jit(solution)/shard_map/ppermute | solution.py:197
  24.0 0.0 collective-permute-done.3.p2.refs_2_
  24.0 2.0 %collective-permute-done.4.p3.refs_3_ = bf16[288,256]{1,0:T(8,128)(2,1)S(1)} collective-permute-done((bf16[288,256]{1,0:T(8,128)(2,1)S(1)}, bf16[288,256]{1,0:T(8,128)(2,1)S(1)}, u32[]{:S(2)}, u32[]{:S(2)}) %collective-permute-start.4) | collective-permute-done | bytes 147488 | tf_op jit(solution)/shard_map/ppermute | solution.py:197
  26.0 0.8 %shard_map.69.early = f32[520,256]{1,0:T(8,128)S(1)} custom-call(bf16[288,256]{1,0:T(8,128)(2,1)S(1)} %get-tuple-element.23.p0.refs_0_, bf16[288,256]{1,0:T(8,128)(2,1)S(1)} %collective-permute-done.2.p1.refs_1_, bf16[288,256]{1,0:T(8,128)(2,1)S(1)} %collective-permute-done.3.p2.refs_2_, bf16[288,256]{1,0:T(8,128)(2,1)S(1)} %collective-permute-done.4.p3.refs_3_, ...), custom_call_target="tpu_custom_call" | custom-call | flops 335544320 | bytes 1269760 | tf_op jit(solution)/shard_map/pallas_call | solution.py:178
  26.8 0.0 copy-start
  26.8 0.3 collective-permute-done.6.q1.refs_5_
  27.1 1.4 %collective-permute-done.7.q2.refs_6_ = bf16[288,256]{1,0:T(8,128)(2,1)S(1)} collective-permute-done((bf16[288,256]{1,0:T(8,128)(2,1)S(1)}, bf16[288,256]{1,0:T(8,128)(2,1)S(1)}, u32[]{:S(2)}, u32[]{:S(2)}) %collective-permute-start.7) | collective-permute-done | bytes 147488 | tf_op jit(solution)/shard_map/ppermute | solution.py:197
  28.5 2.3 %collective-permute-done.8.q3.refs_7_ = bf16[288,256]{1,0:T(8,128)(2,1)S(1)} collective-permute-done((bf16[288,256]{1,0:T(8,128)(2,1)S(1)}, bf16[288,256]{1,0:T(8,128)(2,1)S(1)}, u32[]{:S(2)}, u32[]{:S(2)}) %collective-permute-start.8) | collective-permute-done | bytes 147488 | tf_op jit(solution)/shard_map/ppermute | solution.py:197
  30.9 0.6 %shard_map.70.mine = f32[520,256]{1,0:T(8,128)S(1)} custom-call(f32[520,256]{1,0:T(8,128)S(1)} %shard_map.69.early, bf16[288,256]{1,0:T(8,128)(2,1)S(1)} %collective-permute-done.6.q1.refs_5_, bf16[288,256]{1,0:T(8,128)(2,1)S(1)} %collective-permute-done.7.q2.refs_6_, bf16[288,256]{1,0:T(8,128)(2,1)S(1)} %collective-permute-done.8.q3.refs_7_), custom_call_target="tpu_custom_call" | custom-call | flops 201326592 | bytes 1507328 | tf_op jit(solution)/shard_map/pallas_call | solution.py:178
  31.4 0.1 collective-permute-start.9
  31.5 1.9 %collective-permute-done.9.other = f32[520,256]{1,0:T(8,128)S(1)} collective-permute-done((f32[520,256]{1,0:T(8,128)S(1)}, f32[520,256]{1,0:T(8,128)S(1)}, u32[]{:S(2)}, u32[]{:S(2)}) %collective-permute-start.9) | collective-permute-done | bytes 532512 | tf_op jit(solution)/shard_map/ppermute | solution.py:197
  33.4 0.0 copy-done
  33.4 1.6 %shard_map.71 = (bf16[512,256]{1,0:T(8,128)(2,1)}, bf16[1024,256]{1,0:T(8,128)(2,1)}, f32[8,128]{1,0:T(8,128)}) custom-call(f32[520,256]{1,0:T(8,128)S(1)} %shard_map.70.mine, f32[520,256]{1,0:T(8,128)S(1)} %collective-permute-done.9.other, bf16[512,256]{1,0:T(8,128)(2,1)S(1)} %copy-done, bf16[288,256]{1,0:T(8,128)(2,1)S(1)} %get-tuple-element.23.p0.refs_0_, ...), custom_call_target="tpu_custom_call" | custom-call | flops 268435456 | bytes 3297280 | tf_op jit(solution)/shard_map/pallas_call | solution.py:178
  (2 shorter events, 0.0 us)
Async XLA Ops:
  0.6 0.7 %copy-start.2 = (s32[256]{0:T(256)S(1)}, s32[256]{0:T(256)}, u32[]{:S(2)}) copy-start(s32[256]{0:T(256)} %param.5) | copy-start | bytes 3076
  1.3 7.7 %copy-start.1 = (s32[4096]{0:T(1024)S(1)}, s32[4096]{0:T(1024)}, u32[]{:S(2)}) copy-start(s32[4096]{0:T(1024)} %param.6) | copy-start | bytes 49156
  2.4 6.7 %collective-permute-start.1 = (bf16[272,256]{1,0:T(8,128)(2,1)S(1)}, bf16[272,256]{1,0:T(8,128)(2,1)S(1)}, u32[]{:S(2)}, u32[]{:S(2)}) collective-permute-start(bf16[272,256]{1,0:T(8,128)(2,1)S(1)} %fusion.refs_0_), channel_id=1, source_target_pairs={{0,2},{1,3},{2,0},{3,1},{4,6},{5,7},{6,4},{7,5},{8,10},{9,11},{10,... | collective-permute-start | bytes 417800 | tf_op jit(solution)/shard_map/ppermute | solution.py:197
  5.4 9.0 %collective-permute-start = (bf16[272,256]{1,0:T(8,128)(2,1)S(1)}, bf16[272,256]{1,0:T(8,128)(2,1)S(1)}, u32[]{:S(2)}, u32[]{:S(2)}) collective-permute-start(bf16[272,256]{1,0:T(8,128)(2,1)S(1)} %fusion.refs_0_), channel_id=1, source_target_pairs={{0,16},{1,17},{2,18},{3,19},{4,20},{5,21},{6,22},{7,23},{8,24},{9,... | collective-permute-start | bytes 417800 | tf_op jit(solution)/shard_map/ppermute | solution.py:197
  14.4 5.1 %collective-permute-start.5 = (bf16[272,256]{1,0:T(8,128)(2,1)S(1)}, bf16[272,256]{1,0:T(8,128)(2,1)S(1)}, u32[]{:S(2)}, u32[]{:S(2)}) collective-permute-start(bf16[272,256]{1,0:T(8,128)(2,1)S(1)} %collective-permute-done.refs_0_), channel_id=1, source_target_pairs={{0,2},{1,3},{2,0},{3,1},{4,6},{5,7},{6,4},{7,5},{8,10},{9,11},{10,... | collective-permute-start | bytes 417800 | tf_op jit(solution)/shard_map/ppermute | solution.py:197
  14.9 8.4 %collective-permute-start.2 = (bf16[288,256]{1,0:T(8,128)(2,1)S(1)}, bf16[288,256]{1,0:T(8,128)(2,1)S(1)}, u32[]{:S(2)}, u32[]{:S(2)}) collective-permute-start(bf16[288,256]{1,0:T(8,128)(2,1)S(1)} %get-tuple-element.24), channel_id=1, source_target_pairs={{0,4},{1,5},{2,6},{3,7},{4,0},{5,1},{6,2},{7,3},{8,12},{9,13},{10,... | collective-permute-start | bytes 442376 | tf_op jit(solution)/shard_map/ppermute | solution.py:197
  16.5 7.6 %collective-permute-start.3 = (bf16[288,256]{1,0:T(8,128)(2,1)S(1)}, bf16[288,256]{1,0:T(8,128)(2,1)S(1)}, u32[]{:S(2)}, u32[]{:S(2)}) collective-permute-start(bf16[288,256]{1,0:T(8,128)(2,1)S(1)} %get-tuple-element.25), channel_id=1, source_target_pairs={{0,8},{1,9},{2,10},{3,11},{4,12},{5,13},{6,14},{7,15},{8,0},{9,1},... | collective-permute-start | bytes 442376 | tf_op jit(solution)/shard_map/ppermute | solution.py:197
  17.1 8.9 %collective-permute-start.4 = (bf16[288,256]{1,0:T(8,128)(2,1)S(1)}, bf16[288,256]{1,0:T(8,128)(2,1)S(1)}, u32[]{:S(2)}, u32[]{:S(2)}) collective-permute-start(bf16[288,256]{1,0:T(8,128)(2,1)S(1)} %get-tuple-element.26), channel_id=1, source_target_pairs={{0,12},{1,13},{2,14},{3,15},{4,8},{5,9},{6,10},{7,11},{8,4},{9,5},... | collective-permute-start | bytes 442376 | tf_op jit(solution)/shard_map/ppermute | solution.py:197
  20.5 6.6 %collective-permute-start.6 = (bf16[288,256]{1,0:T(8,128)(2,1)S(1)}, bf16[288,256]{1,0:T(8,128)(2,1)S(1)}, u32[]{:S(2)}, u32[]{:S(2)}) collective-permute-start(bf16[288,256]{1,0:T(8,128)(2,1)S(1)} %get-tuple-element.29), channel_id=1, source_target_pairs={{0,4},{1,5},{2,6},{3,7},{4,0},{5,1},{6,2},{7,3},{8,12},{9,13},{10,... | collective-permute-start | bytes 442376 | tf_op jit(solution)/shard_map/ppermute | solution.py:197
  22.1 6.5 %collective-permute-start.7 = (bf16[288,256]{1,0:T(8,128)(2,1)S(1)}, bf16[288,256]{1,0:T(8,128)(2,1)S(1)}, u32[]{:S(2)}, u32[]{:S(2)}) collective-permute-start(bf16[288,256]{1,0:T(8,128)(2,1)S(1)} %get-tuple-element.30), channel_id=1, source_target_pairs={{0,8},{1,9},{2,10},{3,11},{4,12},{5,13},{6,14},{7,15},{8,0},{9,1},... | collective-permute-start | bytes 442376 | tf_op jit(solution)/shard_map/ppermute | solution.py:197
  23.3 7.6 %collective-permute-start.8 = (bf16[288,256]{1,0:T(8,128)(2,1)S(1)}, bf16[288,256]{1,0:T(8,128)(2,1)S(1)}, u32[]{:S(2)}, u32[]{:S(2)}) collective-permute-start(bf16[288,256]{1,0:T(8,128)(2,1)S(1)} %get-tuple-element.31), channel_id=1, source_target_pairs={{0,12},{1,13},{2,14},{3,15},{4,8},{5,9},{6,10},{7,11},{8,4},{9,5},... | collective-permute-start | bytes 442376 | tf_op jit(solution)/shard_map/ppermute | solution.py:197
  26.8 6.6 %copy-start = (bf16[512,256]{1,0:T(8,128)(2,1)S(1)}, bf16[512,256]{1,0:T(8,128)(2,1)}, u32[]{:S(2)}) copy-start(bf16[512,256]{1,0:T(8,128)(2,1)} %old.1) | copy-start | bytes 786436
  31.4 2.0 %collective-permute-start.9 = (f32[520,256]{1,0:T(8,128)S(1)}, f32[520,256]{1,0:T(8,128)S(1)}, u32[]{:S(2)}, u32[]{:S(2)}) collective-permute-start(f32[520,256]{1,0:T(8,128)S(1)} %shard_map.70.mine), channel_id=1, source_target_pairs={{0,1},{1,0},{2,3},{3,2},{4,5},{5,4},{6,7},{7,6},{8,9},{9,8},{10,11... | collective-permute-start | bytes 1597448 | tf_op jit(solution)/shard_map/ppermute | solution.py:197

commit v3 on v2

--- a/solution.py
+++ b/solution.py
@@ -35,55 +35,58 @@
     return (pick(table & 255) + 256.0 * pick(table >> 8)).astype(jnp.int32)
 
 
-def _head(list_dev, base, table, assign):
-    n = assign.shape[1]
-    slot = _slots(table, assign)
-    relative = (slot >> _log2(list_dev)) ^ base
+def _core():
+    return lax.axis_index("rep") & 1
+
+
+def _head(list_dev, me, table, payload):
+    n = payload.shape[0] - HEAD
+    low = payload[n:, :].astype(jnp.float32)
+    slot = _slots(table, (low[0:1, :] + 256.0 * low[1:2, :]).astype(jnp.int32))
+    relative = (slot >> _log2(list_dev)) ^ me
     code = (slot & (list_dev - 1)) + 1
-    member = (_iota((16, n), 0) == relative).astype(jnp.float32)
+    member = (_iota((HEAD, n), 0) == relative).astype(jnp.float32)
     before = _bf16(_iota((n, n), 0) < _iota((n, n), 1))
     count = jnp.dot(member.astype(jnp.bfloat16), before, preferred_element_type=jnp.float32)
-    head = jnp.where(member > 0.0, count, -1.0).astype(jnp.int32)[0:8, :]
-    row = _iota((8, n), 0)
-    head = jnp.where(row == 4, code & 255, head)
-    return jnp.where(row == 5, code >> 8, head)
-
-
-def _route(head, rows, outs, half):
+    rank = jnp.sum(member * count, axis=0, keepdims=True).astype(jnp.int32)
+    return rank, relative, (code & 255).astype(jnp.float32), (code >> 8).astype(jnp.float32)
+
+
+def _route(head, rows, outs, base):
+    rank, relative, lo, hi = head
     n = rows.shape[0]
-    capacity = rows.shape[1] // 2
-    base = half * (capacity + HEAD)
+    capacity = n // 2
     hot = jnp.concatenate(
-        [(_iota((capacity, n), 0) == head[k : k + 1, :]).astype(jnp.float32) for k in range(len(outs))],
+        [
+            (_iota((capacity, n), 0) == jnp.where(relative == k, rank, -1)).astype(jnp.float32)
+            for k, _ in outs
+        ],
         axis=0,
     ).astype(jnp.bfloat16)
     moved = jnp.dot(hot, rows, preferred_element_type=jnp.float32).astype(jnp.bfloat16)
-    lo, hi = head[4:5, :].astype(jnp.float32), head[5:6, :].astype(jnp.float32)
     values = jnp.where(_iota((HEAD, n), 0) == 0, lo, hi).astype(jnp.bfloat16)
     labels = lax.dot_general(
         values, hot, (((1,), (1,)), ((), ())), preferred_element_type=jnp.float32
     )
-    for i, out in enumerate(outs):
-        part = labels[:, i * capacity : (i + 1) * capacity]
-        line = jnp.concatenate([part[0:1, :], part[1:2, :]], axis=1)
-        out[base : base + capacity, :] = moved[i * capacity : (i + 1) * capacity, :]
+    for i, (_, out) in enumerate(outs):
+        at = slice(i * capacity, (i + 1) * capacity)
+        line = jnp.concatenate([labels[0:1, at], labels[1:2, at]], axis=1)
+        out[base : base + capacity, :] = moved[at, :]
         out[base + capacity : base + capacity + HEAD, :] = jnp.broadcast_to(
             line, (HEAD, line.shape[1])
         ).astype(jnp.bfloat16)
 
 
-def _payload_head(list_dev, base, table, payload):
+def _split_kernel(list_dev, payload, twin, table, *refs):
+    a, b = refs[-2:]
+    core, me = _core(), lax.axis_index("items")
     n = payload.shape[0] - HEAD
-    low = payload[n:, :].astype(jnp.float32)
-    assign = (low[0:1, :] + 256.0 * low[1:2, :]).astype(jnp.int32)
-    return _head(list_dev, base, table[...], assign)
-
-
-def _pair_kernel(list_dev, mine, side, table, o0, o1, o2, o3):
-    n = mine.shape[0] - HEAD
-    for half, payload in enumerate((mine, side)):
-        head = _payload_head(list_dev, lax.axis_index("items"), table, payload)
-        _route(head, payload[0:n, :], (o0, o1, o2, o3), half)
+    size = n // 2 + HEAD
+    mine, other = payload[...], twin[...]
+    for i in range(2):
+        part = jnp.where(core == i, mine, other)
+        head = _head(list_dev, me, table[...], part)
+        _route(head, part[0:n, :], ((1 + 2 * core, a), (2 - 2 * core, b)), i * size)
 
 
 def _labels(head):
@@ -102,48 +105,44 @@
 
 
 def _totals(blocks, lists):
-    rows = jnp.concatenate([r for r, _ in blocks], axis=0)
-    labels = jnp.concatenate([l for _, l in blocks], axis=1)
+    parts = [p for b in blocks for p in _parts(b)]
+    rows = jnp.concatenate([r for r, _ in parts], axis=0)
+    labels = jnp.concatenate([l for _, l in parts], axis=1)
     hot = (_iota((lists, rows.shape[0]), 0) == labels).astype(jnp.float32)
     sums = jnp.dot(hot.astype(jnp.bfloat16), rows, preferred_element_type=jnp.float32)
     return sums, jnp.sum(hot, axis=1, keepdims=True)
 
 
-def _both_planes(pairs, lists):
-    parts = [_parts(p) for p in pairs]
-    mine, mine_n = _totals([p[0] for p in parts], lists)
-    side, side_n = _totals([p[1] for p in parts], lists)
-    width = mine.shape[1]
+def _sums_kernel(*refs):
+    *before, a, b, side_a, side_b, out, pack = refs
+    lists, width = out.shape[0] - 8, out.shape[1]
+    mine, mine_n = _totals((a, b), lists)
+    side, side_n = _totals((side_a, side_b), lists)
+    count = mine_n + side_n
     eye = _iota((width, width), 0) == _iota((width, width), 1)
-    count = mine_n + side_n
-    lines = [
-        jnp.sum(jnp.where(eye, count[i : i + width, :], 0.0), axis=0, keepdims=True)
-        for i in range(0, lists, width)
-    ]
     row = _iota((8, width), 0)
-    count = jnp.zeros((8, width), jnp.float32)
-    for i, line in enumerate(lines):
-        count = jnp.where(row == i, line, count)
-    return mine + side, count
-
-
-def _early_kernel(p0, p1, p2, p3, q0, out):
-    lists = out.shape[0] - 8
-    out[0:lists, :], out[lists:, :] = _both_planes((p0, p1, p2, p3, q0), lists)
-
-
-def _late_kernel(early, q1, q2, q3, out):
-    lists = out.shape[0] - 8
-    sums, count = _both_planes((q1, q2, q3), lists)
-    out[0:lists, :] = early[0:lists, :] + sums
-    out[lists:, :] = early[lists:, :] + count
+    lines = jnp.zeros((8, width), jnp.float32)
+    for i in range(lists // width):
+        line = jnp.where(eye, count[i * width : (i + 1) * width, :], 0.0)
+        lines = jnp.where(row == i, jnp.sum(line, axis=0, keepdims=True), lines)
+    if before:
+        out[0:lists, :] = before[0][0:lists, :] + (mine + side)
+        out[lists:, :] = before[0][lists:, :] + lines
+    else:
+        out[0:lists, :] = mine + side
+        out[lists:, :] = lines
+    size = a.shape[0] // 2
+    for i, block in enumerate((a, b)):
+        pack[i * size : (i + 1) * size, :] = jnp.where(
+            _core() == 0, block[size:, :], block[0:size, :]
+        )
 
 
 def _codes_kernel(mine, other, old, *refs):
     (*blocks, fresh, codes, scales) = refs
     lists, width = fresh.shape
     capacity = width // 2
-    me = lax.axis_index("items")
+    me, core = lax.axis_index("items"), _core()
     wide = _iota((width, width), 0) == _iota((width, width), 1)
     for i in range(lists // width):
         row = mine[lists + i : lists + i + 1, :] + other[lists + i : lists + i + 1, :]
@@ -153,7 +152,16 @@
         fresh[at_i, :] = (total / (counts + 1.0)).astype(jnp.bfloat16)
     table = fresh[...]
     eye = _iota((capacity, capacity), 0) == _iota((capacity, capacity), 1)
-    for k, (rows, labels) in enumerate(_parts(b)[0] for b in blocks):
+    size = capacity + HEAD
+    ordered = []
+    for i, (a, b, pack) in enumerate((blocks[0:3], blocks[3:6])):
+        base = me ^ (4 * i)
+        for block, k in ((a, 1 + 2 * core), (b, 2 - 2 * core)):
+            part = jnp.where(core == 0, block[0:size, :], block[size:, :])
+            ordered.append((base ^ k, _parts(part)[0]))
+        for part, k in zip(_parts(pack), (3 - 2 * core, 2 * core)):
+            ordered.append((base ^ k, part))
+    for source, (rows, labels) in ordered:
         column = jnp.sum(
             jnp.where(eye, labels.astype(jnp.float32), 0.0), axis=1, keepdims=True
         ).astype(jnp.int32)
@@ -161,7 +169,6 @@
         lookup = jnp.dot(hot, table, preferred_element_type=jnp.float32)
         residual = rows.astype(jnp.float32) - lookup
         amax = jnp.max(jnp.abs(residual), axis=1, keepdims=True)
-        source = me ^ k
         codes[pl.ds(pl.multiple_of(source * capacity, capacity), capacity), :] = (
             residual * (127.0 / (amax + 1e-06))
         ).astype(jnp.bfloat16)
@@ -198,33 +205,35 @@
 
     table = list_slot.reshape(-1, 128)
     pair = jax.ShapeDtypeStruct((2 * (capacity + HEAD), width), jnp.bfloat16)
-    flops = 2 * 8 * capacity * item_dev * width
+    total = jax.ShapeDtypeStruct((list_dev + 8, width), jnp.float32)
+    flops = 2 * 4 * capacity * item_dev * width
+
+    def spread(a, items, rep):
+        swap = [x * reps + rep for x in items]
+        return lax.ppermute(a, ("items", "rep"), [(i, i ^ swap[i & 1]) for i in range(peers * reps)])
+
+    def to_owners(payload, weight, *after):
+        a, b = _call(
+            lambda *refs: _split_kernel(list_dev, *refs),
+            [pair] * 2,
+            (payload, hop(payload, 0, 1), table, *after),
+            flops=weight * flops,
+        )
+        side_b, near_b = spread(b, (2, 0), 2), spread(b, (2, 0), 0)
+        side_a, near_a = spread(a, (1, 3), 2), spread(a, (1, 3), 0)
+        return near_a, near_b, side_a, side_b
+
     row = lax.broadcasted_iota(jnp.int32, (item_dev + HEAD, width), 0)
     ids = jnp.where(row == item_dev, assign & 255, assign >> 8).astype(jnp.bfloat16)
     payload = jnp.where(row < item_dev, jnp.pad(embeds, ((0, HEAD), (0, 0))), ids)
     far = hop(payload, 4)
-    side = hop(payload, 0, 2)
-
-    def routed(mine, side):
-        return _call(
-            lambda *refs: _pair_kernel(list_dev, *refs),
-            [pair] * 4,
-            (mine, side, table),
-            flops=flops,
-        )
-
-    def to_owners(pairs):
-        return [pairs[0]] + [hop(pairs[k], k) for k in (3, 2, 1)][::-1]
-
-    near = routed(payload, side)
-    far, *near = lax.optimization_barrier((far, *near))
-    far_side = hop(far, 0, 2)
-    near = to_owners(near)
-    away = to_owners(routed(far, far_side))
-    total = jax.ShapeDtypeStruct((list_dev + 8, width), jnp.float32)
+    near = to_owners(payload, 1000)
+    away = to_owners(far, 1, near[3])
     flops = 2 * list_dev * capacity * width
-    (early,) = _call(_early_kernel, [total], (*near, away[0]), flops=10 * flops)
-    (mine,) = _call(_late_kernel, [total], (early, *away[1:]), flops=6 * flops)
+    mine, near_pack = _call(_sums_kernel, [total, pair], near, flops=8 * flops)
+    near_pack = hop(near_pack, 0, 1)
+    mine, away_pack = _call(_sums_kernel, [total, pair], (mine, *away), flops=8 * flops)
+    away_pack = hop(away_pack, 0, 1)
     other = hop(mine, 0, 1)
     fresh, codes, scales = _call(
         _codes_kernel,
@@ -233,7 +242,7 @@
             jax.ShapeDtypeStruct((peers * capacity, width), jnp.bfloat16),
             jax.ShapeDtypeStruct((peers, capacity), jnp.float32),
         ],
-        (mine, other, old_centroids, *near, *away),
+        (mine, other, old_centroids, *near[0:2], near_pack, *away[0:2], away_pack),
         flops=8 * flops,
     )
     return (

time: 35.2 us -> 33.6 us (0.955)
  waiting for transfers between devices: 14.4 us -> 7.36 us
  starting transfers between devices: 13.2 us -> 19 us
  Pallas kernels: 5 us -> 4.62 us
    ppermute x0 -> x8, starting transfers between devices: none -> 14.1 us  [spread(): lax.ppermute(a, ('items', 'rep'), [(i, i ^ swap[i & 1]) for i in range(pe...]
    ppermute x10 -> x6, waiting for transfers between devices: 14.4 us -> 3.63 us  [hop(): lax.ppermute(a, ('items', 'rep'), [(i, i ^ swap) for i in range(peers * r...]
    ppermute x10 -> x6, starting transfers between devices: 13.2 us -> 4.83 us  [hop(): lax.ppermute(a, ('items', 'rep'), [(i, i ^ swap) for i in range(peers * r...]
    ppermute x0 -> x8, waiting for transfers between devices: none -> 3.73 us  [spread(): lax.ppermute(a, ('items', 'rep'), [(i, i ^ swap[i & 1]) for i in range(pe...]
    pallas_call x5, Pallas kernels: 5 us -> 4.62 us  [_call(): pl.pallas_call(kernel, out_shape=outs, in_specs=[VMEM] * len(args), out_s...]
  transfers between devices with their start and end apart: 10 -> 14, of which waited for: 8 -> 6; matrix products, arithmetic and copies ran while one was open for 0% -> 0% of each run, Pallas kernels for 8% -> 7%
where the time goes in v3:
time: 33.6 us; the launch traced here: 33.4 us
  starting transfers between devices  19 us (57%)
  waiting for transfers between devices  7.36 us (22%)
  Pallas kernels  4.62 us (14%)
  other arithmetic  1.06 us (3%)
  between operations  0.74 us (2%)
  local copies, waits for them, and re-layouts  0.67 us (2%)
    ppermute x8, starting transfers between devices, spread(): lax.ppermute(a, ('items', 'rep'), [(i, i ^ swap[i & 1]) for i in range(pe...  14.1 us
    ppermute x6, starting transfers between devices, hop(): lax.ppermute(a, ('items', 'rep'), [(i, i ^ swap) for i in range(peers * r...  4.83 us
    pallas_call x5, Pallas kernels, _call(): pl.pallas_call(kernel, out_shape=outs, in_specs=[VMEM] * len(args), out_s...  4.62 us
    ppermute x8, waiting for transfers between devices, spread(): lax.ppermute(a, ('items', 'rep'), [(i, i ^ swap[i & 1]) for i in range(pe...  3.73 us
    ppermute x6, waiting for transfers between devices, hop(): lax.ppermute(a, ('items', 'rep'), [(i, i ^ swap) for i in range(peers * r...  3.63 us
    select_n x1, other arithmetic, per_device_eight(): jnp.where(row < item_dev, jnp.pad(embeds, ((0, HEAD), (0, 0))), ids)  1.05 us
  transfers between devices with their start and end apart: 14, of which 6 were waited for; matrix products, arithmetic and copies ran while one was open for 0% of the time, Pallas kernels for 7%

profile of v3, /device:TPU:0, one launch (start us, length us, event | category | flops | bytes accessed | tf_op | source)
XLA Modules:
  0.0 33.4 jit_solution(12183308569791629399)
XLA Ops:
  0.6 0.0 copy-start.2
  0.7 0.7 %copy-done.2 = s32[256]{0:T(256)S(1)} copy-done((s32[256]{0:T(256)S(1)}, s32[256]{0:T(256)}, u32[]{:S(2)}) %copy-start.2) | copy-done | bytes 1048
  1.3 0.0 copy-start.1
  1.3 1.1 %fusion.refs_0_ = bf16[272,256]{1,0:T(8,128)(2,1)S(1)} fusion(s32[256]{0:T(256)S(1)} %get-tuple-element.26, s32[256]{0:T(256)S(1)} %get-tuple-element.25, bf16[256,256]{1,0:T(8,128)(2,1)} %param.4, pred[272]{0:T(512)(128)(4,1)S(1)} %get-tuple-element.27, pred[272]{0:T(512)(128)(4,1)S(1)} %get-tuple-element.28), kind=kLoop, calls=%fused_computation.1 | loop fusion | flops 208896 | bytes 272928 | tf_op jit(solution)/shard_map/jit(_where)/select_n | solution.py:228
  2.4 0.5 %collective-permute-start = (bf16[272,256]{1,0:T(8,128)(2,1)S(1)}, bf16[272,256]{1,0:T(8,128)(2,1)S(1)}, u32[]{:S(2)}, u32[]{:S(2)}) collective-permute-start(bf16[272,256]{1,0:T(8,128)(2,1)S(1)} %fusion.refs_0_), channel_id=1, source_target_pairs={{0,1},{1,0},{2,3},{3,2},{4,5},{5,4},{6,7},{7,6},{8,9},{9,8},{10,11... | collective-permute-start | bytes 417800 | tf_op jit(solution)/shard_map/ppermute | solution.py:204
  2.9 3.7 %collective-permute-start.5 = (bf16[272,256]{1,0:T(8,128)(2,1)S(1)}, bf16[272,256]{1,0:T(8,128)(2,1)S(1)}, u32[]{:S(2)}, u32[]{:S(2)}) collective-permute-start(bf16[272,256]{1,0:T(8,128)(2,1)S(1)} %fusion.refs_0_), channel_id=1, source_target_pairs={{0,16},{1,17},{2,18},{3,19},{4,20},{5,21},{6,22},{7,23},{8,24},{9,... | collective-permute-start | bytes 417800 | tf_op jit(solution)/shard_map/ppermute | solution.py:204
  6.6 0.0 collective-permute-done.refs_1_
  6.6 0.0 copy-done.1
  6.6 0.9 %shard_map.67 = (bf16[288,256]{1,0:T(8,128)(2,1)S(1)}, bf16[288,256]{1,0:T(8,128)(2,1)S(1)}) custom-call(bf16[272,256]{1,0:T(8,128)(2,1)S(1)} %fusion.refs_0_, bf16[272,256]{1,0:T(8,128)(2,1)S(1)} %collective-permute-done.refs_1_, s32[32,128]{1,0:T(8,128)S(1)} %bitcast.3), custom_call_target="tpu_custom_call" | custom-call | flops 67108864000 | bytes 589824 | tf_op jit(solution)/shard_map/pallas_call | solution.py:185
  7.5 2.6 %collective-permute-start.4 = (bf16[288,256]{1,0:T(8,128)(2,1)S(1)}, bf16[288,256]{1,0:T(8,128)(2,1)S(1)}, u32[]{:S(2)}, u32[]{:S(2)}) collective-permute-start(bf16[288,256]{1,0:T(8,128)(2,1)S(1)} %get-tuple-element.15), channel_id=1, source_target_pairs={{0,10},{1,3},{2,8},{3,1},{4,14},{5,7},{6,12},{7,5},{8,2},{9,11},{1... | collective-permute-start | bytes 442376 | tf_op jit(solution)/shard_map/ppermute | solution.py:213
  10.0 1.5 %collective-permute-start.3 = (bf16[288,256]{1,0:T(8,128)(2,1)S(1)}, bf16[288,256]{1,0:T(8,128)(2,1)S(1)}, u32[]{:S(2)}, u32[]{:S(2)}) collective-permute-start(bf16[288,256]{1,0:T(8,128)(2,1)S(1)} %get-tuple-element.14), channel_id=1, source_target_pairs={{0,6},{1,15},{2,4},{3,13},{4,2},{5,11},{6,0},{7,9},{8,14},{9,7},{1... | collective-permute-start | bytes 442376 | tf_op jit(solution)/shard_map/ppermute | solution.py:213
  11.5 0.5 %collective-permute-start.1 = (bf16[288,256]{1,0:T(8,128)(2,1)S(1)}, bf16[288,256]{1,0:T(8,128)(2,1)S(1)}, u32[]{:S(2)}, u32[]{:S(2)}) collective-permute-start(bf16[288,256]{1,0:T(8,128)(2,1)S(1)} %get-tuple-element.14), channel_id=1, source_target_pairs={{0,4},{1,13},{2,6},{3,15},{4,0},{5,9},{6,2},{7,11},{8,12},{9,5},{1... | collective-permute-start | bytes 442376 | tf_op jit(solution)/shard_map/ppermute | solution.py:213
  12.0 1.9 %collective-permute-done.5.refs_0_ = bf16[272,256]{1,0:T(8,128)(2,1)S(1)} collective-permute-done((bf16[272,256]{1,0:T(8,128)(2,1)S(1)}, bf16[272,256]{1,0:T(8,128)(2,1)S(1)}, u32[]{:S(2)}, u32[]{:S(2)}) %collective-permute-start.5) | collective-permute-done | bytes 139296 | tf_op jit(solution)/shard_map/ppermute | solution.py:204
  13.9 0.0 collective-permute-start.6
  13.9 2.6 %collective-permute-start.2 = (bf16[288,256]{1,0:T(8,128)(2,1)S(1)}, bf16[288,256]{1,0:T(8,128)(2,1)S(1)}, u32[]{:S(2)}, u32[]{:S(2)}) collective-permute-start(bf16[288,256]{1,0:T(8,128)(2,1)S(1)} %get-tuple-element.15), channel_id=1, source_target_pairs={{0,8},{1,1},{2,10},{3,3},{4,12},{5,5},{6,14},{7,7},{8,0},{9,9},{10... | collective-permute-start | bytes 442376 | tf_op jit(solution)/shard_map/ppermute | solution.py:213
  16.6 0.0 collective-permute-done.6.refs_1_
  16.6 0.0 collective-permute-done.4.refs_3_
  16.6 0.9 %shard_map.69 = (bf16[288,256]{1,0:T(8,128)(2,1)S(1)}, bf16[288,256]{1,0:T(8,128)(2,1)S(1)}) custom-call(bf16[272,256]{1,0:T(8,128)(2,1)S(1)} %collective-permute-done.5.refs_0_, bf16[272,256]{1,0:T(8,128)(2,1)S(1)} %collective-permute-done.6.refs_1_, s32[32,128]{1,0:T(8,128)S(1)} %bitcast.4, bf16[288,256]{1,0:T(8,128)(2,1)S(1)} %collective-permute-done.4.refs_3_), custom_call_target="tpu_custom_call" | custom-call | flops 67108864 | bytes 737280 | tf_op jit(solution)/shard_map/pallas_call | solution.py:185
  17.5 2.9 %collective-permute-start.9 = (bf16[288,256]{1,0:T(8,128)(2,1)S(1)}, bf16[288,256]{1,0:T(8,128)(2,1)S(1)}, u32[]{:S(2)}, u32[]{:S(2)}) collective-permute-start(bf16[288,256]{1,0:T(8,128)(2,1)S(1)} %get-tuple-element.17), channel_id=1, source_target_pairs={{0,6},{1,15},{2,4},{3,13},{4,2},{5,11},{6,0},{7,9},{8,14},{9,7},{1... | collective-permute-start | bytes 442376 | tf_op jit(solution)/shard_map/ppermute | solution.py:213
  20.4 0.5 %collective-permute-start.7 = (bf16[288,256]{1,0:T(8,128)(2,1)S(1)}, bf16[288,256]{1,0:T(8,128)(2,1)S(1)}, u32[]{:S(2)}, u32[]{:S(2)}) collective-permute-start(bf16[288,256]{1,0:T(8,128)(2,1)S(1)} %get-tuple-element.17), channel_id=1, source_target_pairs={{0,4},{1,13},{2,6},{3,15},{4,0},{5,9},{6,2},{7,11},{8,12},{9,5},{1... | collective-permute-start | bytes 442376 | tf_op jit(solution)/shard_map/ppermute | solution.py:213
  20.9 0.0 collective-permute-done.3.refs_2_
  20.9 0.8 %collective-permute-start.10 = (bf16[288,256]{1,0:T(8,128)(2,1)S(1)}, bf16[288,256]{1,0:T(8,128)(2,1)S(1)}, u32[]{:S(2)}, u32[]{:S(2)}) collective-permute-start(bf16[288,256]{1,0:T(8,128)(2,1)S(1)} %get-tuple-element.18), channel_id=1, source_target_pairs={{0,10},{1,3},{2,8},{3,1},{4,14},{5,7},{6,12},{7,5},{8,2},{9,11},{1... | collective-permute-start | bytes 442376 | tf_op jit(solution)/shard_map/ppermute | solution.py:213
  21.8 0.0 collective-permute-done.1.refs_0_
  21.8 2.7 %collective-permute-start.8 = (bf16[288,256]{1,0:T(8,128)(2,1)S(1)}, bf16[288,256]{1,0:T(8,128)(2,1)S(1)}, u32[]{:S(2)}, u32[]{:S(2)}) collective-permute-start(bf16[288,256]{1,0:T(8,128)(2,1)S(1)} %get-tuple-element.18), channel_id=1, source_target_pairs={{0,8},{1,1},{2,10},{3,3},{4,12},{5,5},{6,14},{7,7},{8,0},{9,9},{10... | collective-permute-start | bytes 442376 | tf_op jit(solution)/shard_map/ppermute | solution.py:213
  24.4 0.0 collective-permute-done.2.refs_1_
  24.5 0.6 %shard_map.68 = (f32[520,256]{1,0:T(8,128)S(1)}, bf16[288,256]{1,0:T(8,128)(2,1)S(1)}) custom-call(bf16[288,256]{1,0:T(8,128)(2,1)S(1)} %collective-permute-done.1.refs_0_, bf16[288,256]{1,0:T(8,128)(2,1)S(1)} %collective-permute-done.2.refs_1_, bf16[288,256]{1,0:T(8,128)(2,1)S(1)} %collective-permute-done.3.refs_2_, ...), custom_call_target="tpu_custom_call" | custom-call | flops 268435456 | bytes 1269760 | tf_op jit(solution)/shard_map/pallas_call | solution.py:185
  25.1 1.2 %collective-permute-done.9.refs_3_ = bf16[288,256]{1,0:T(8,128)(2,1)S(1)} collective-permute-done((bf16[288,256]{1,0:T(8,128)(2,1)S(1)}, bf16[288,256]{1,0:T(8,128)(2,1)S(1)}, u32[]{:S(2)}, u32[]{:S(2)}) %collective-permute-start.9) | collective-permute-done | bytes 147488 | tf_op jit(solution)/shard_map/ppermute | solution.py:213
  26.2 1.4 %collective-permute-done.7.refs_1_.refs_3_ = bf16[288,256]{1,0:T(8,128)(2,1)S(1)} collective-permute-done((bf16[288,256]{1,0:T(8,128)(2,1)S(1)}, bf16[288,256]{1,0:T(8,128)(2,1)S(1)}, u32[]{:S(2)}, u32[]{:S(2)}) %collective-permute-start.7) | collective-permute-done | bytes 147488 | tf_op jit(solution)/shard_map/ppermute | solution.py:213
  27.6 0.0 collective-permute-done.10.refs_4_
  27.6 1.2 %collective-permute-done.8.refs_2_.refs_4_ = bf16[288,256]{1,0:T(8,128)(2,1)S(1)} collective-permute-done((bf16[288,256]{1,0:T(8,128)(2,1)S(1)}, bf16[288,256]{1,0:T(8,128)(2,1)S(1)}, u32[]{:S(2)}, u32[]{:S(2)}) %collective-permute-start.8) | collective-permute-done | bytes 147488 | tf_op jit(solution)/shard_map/ppermute | solution.py:213
  28.8 0.0 copy-start
  28.8 0.6 %shard_map.70 = (f32[520,256]{1,0:T(8,128)S(1)}, bf16[288,256]{1,0:T(8,128)(2,1)S(1)}) custom-call(f32[520,256]{1,0:T(8,128)S(1)} %get-tuple-element.16.refs_0_, bf16[288,256]{1,0:T(8,128)(2,1)S(1)} %collective-permute-done.7.refs_1_.refs_3_, bf16[288,256]{1,0:T(8,128)(2,1)S(1)} %collective-permute-done.8.refs_2_.refs_4_, ...), custom_call_target="tpu_custom_call" | custom-call | flops 268435456 | bytes 1802240 | tf_op jit(solution)/shard_map/pallas_call | solution.py:185
  29.4 0.1 collective-permute-start.11
  29.5 0.5 %collective-permute-start.12 = (bf16[288,256]{1,0:T(8,128)(2,1)S(1)}, bf16[288,256]{1,0:T(8,128)(2,1)S(1)}, u32[]{:S(2)}, u32[]{:S(2)}) collective-permute-start(bf16[288,256]{1,0:T(8,128)(2,1)S(1)} %get-tuple-element.20), channel_id=1, source_target_pairs={{0,1},{1,0},{2,3},{3,2},{4,5},{5,4},{6,7},{7,6},{8,9},{9,8},{10,11... | collective-permute-start | bytes 442376 | tf_op jit(solution)/shard_map/ppermute | solution.py:204
  30.0 0.1 collective-permute-start.13
  30.1 1.5 %collective-permute-done.12.refs_2_ = bf16[288,256]{1,0:T(8,128)(2,1)S(1)} collective-permute-done((bf16[288,256]{1,0:T(8,128)(2,1)S(1)}, bf16[288,256]{1,0:T(8,128)(2,1)S(1)}, u32[]{:S(2)}, u32[]{:S(2)}) %collective-permute-start.12) | collective-permute-done | bytes 147488 | tf_op jit(solution)/shard_map/ppermute | solution.py:204
  31.6 0.2 collective-permute-done.13.refs_5_
  31.8 0.0 collective-permute-done.11.other
  31.8 0.0 copy-done
  31.8 1.6 %shard_map.71 = (bf16[512,256]{1,0:T(8,128)(2,1)}, bf16[1024,256]{1,0:T(8,128)(2,1)}, f32[8,128]{1,0:T(8,128)}) custom-call(f32[520,256]{1,0:T(8,128)S(1)} %get-tuple-element.19.mine, f32[520,256]{1,0:T(8,128)S(1)} %collective-permute-done.11.other, bf16[512,256]{1,0:T(8,128)(2,1)S(1)} %copy-done, bf16[288,256]{1,0:T(8,128)(2,1)S(1)} %collective-permute-done.1.refs_0_, ...), custom_call_target="tpu_custom_call" | custom-call | flops 268435456 | bytes 3002368 | tf_op jit(solution)/shard_map/pallas_call | solution.py:185
  (2 shorter events, 0.0 us)
Async XLA Ops:
  0.6 0.7 %copy-start.2 = (s32[256]{0:T(256)S(1)}, s32[256]{0:T(256)}, u32[]{:S(2)}) copy-start(s32[256]{0:T(256)} %param.5) | copy-start | bytes 3076
  1.3 5.3 %copy-start.1 = (s32[4096]{0:T(1024)S(1)}, s32[4096]{0:T(1024)}, u32[]{:S(2)}) copy-start(s32[4096]{0:T(1024)} %param.6) | copy-start | bytes 49156
  2.4 4.2 %collective-permute-start = (bf16[272,256]{1,0:T(8,128)(2,1)S(1)}, bf16[272,256]{1,0:T(8,128)(2,1)S(1)}, u32[]{:S(2)}, u32[]{:S(2)}) collective-permute-start(bf16[272,256]{1,0:T(8,128)(2,1)S(1)} %fusion.refs_0_), channel_id=1, source_target_pairs={{0,1},{1,0},{2,3},{3,2},{4,5},{5,4},{6,7},{7,6},{8,9},{9,8},{10,11... | collective-permute-start | bytes 417800 | tf_op jit(solution)/shard_map/ppermute | solution.py:204
  2.9 11.0 %collective-permute-start.5 = (bf16[272,256]{1,0:T(8,128)(2,1)S(1)}, bf16[272,256]{1,0:T(8,128)(2,1)S(1)}, u32[]{:S(2)}, u32[]{:S(2)}) collective-permute-start(bf16[272,256]{1,0:T(8,128)(2,1)S(1)} %fusion.refs_0_), channel_id=1, source_target_pairs={{0,16},{1,17},{2,18},{3,19},{4,20},{5,21},{6,22},{7,23},{8,24},{9,... | collective-permute-start | bytes 417800 | tf_op jit(solution)/shard_map/ppermute | solution.py:204
  7.5 9.1 %collective-permute-start.4 = (bf16[288,256]{1,0:T(8,128)(2,1)S(1)}, bf16[288,256]{1,0:T(8,128)(2,1)S(1)}, u32[]{:S(2)}, u32[]{:S(2)}) collective-permute-start(bf16[288,256]{1,0:T(8,128)(2,1)S(1)} %get-tuple-element.15), channel_id=1, source_target_pairs={{0,10},{1,3},{2,8},{3,1},{4,14},{5,7},{6,12},{7,5},{8,2},{9,11},{1... | collective-permute-start | bytes 442376 | tf_op jit(solution)/shard_map/ppermute | solution.py:213
  10.0 10.9 %collective-permute-start.3 = (bf16[288,256]{1,0:T(8,128)(2,1)S(1)}, bf16[288,256]{1,0:T(8,128)(2,1)S(1)}, u32[]{:S(2)}, u32[]{:S(2)}) collective-permute-start(bf16[288,256]{1,0:T(8,128)(2,1)S(1)} %get-tuple-element.14), channel_id=1, source_target_pairs={{0,6},{1,15},{2,4},{3,13},{4,2},{5,11},{6,0},{7,9},{8,14},{9,7},{1... | collective-permute-start | bytes 442376 | tf_op jit(solution)/shard_map/ppermute | solution.py:213
  11.5 10.2 %collective-permute-start.1 = (bf16[288,256]{1,0:T(8,128)(2,1)S(1)}, bf16[288,256]{1,0:T(8,128)(2,1)S(1)}, u32[]{:S(2)}, u32[]{:S(2)}) collective-permute-start(bf16[288,256]{1,0:T(8,128)(2,1)S(1)} %get-tuple-element.14), channel_id=1, source_target_pairs={{0,4},{1,13},{2,6},{3,15},{4,0},{5,9},{6,2},{7,11},{8,12},{9,5},{1... | collective-permute-start | bytes 442376 | tf_op jit(solution)/shard_map/ppermute | solution.py:213
  13.9 2.7 %collective-permute-start.6 = (bf16[272,256]{1,0:T(8,128)(2,1)S(1)}, bf16[272,256]{1,0:T(8,128)(2,1)S(1)}, u32[]{:S(2)}, u32[]{:S(2)}) collective-permute-start(bf16[272,256]{1,0:T(8,128)(2,1)S(1)} %collective-permute-done.5.refs_0_), channel_id=1, source_target_pairs={{0,1},{1,0},{2,3},{3,2},{4,5},{5,4},{6,7},{7,6},{8,9},{9,8},{10,11... | collective-permute-start | bytes 417800 | tf_op jit(solution)/shard_map/ppermute | solution.py:204
  13.9 10.5 %collective-permute-start.2 = (bf16[288,256]{1,0:T(8,128)(2,1)S(1)}, bf16[288,256]{1,0:T(8,128)(2,1)S(1)}, u32[]{:S(2)}, u32[]{:S(2)}) collective-permute-start(bf16[288,256]{1,0:T(8,128)(2,1)S(1)} %get-tuple-element.15), channel_id=1, source_target_pairs={{0,8},{1,1},{2,10},{3,3},{4,12},{5,5},{6,14},{7,7},{8,0},{9,9},{10... | collective-permute-start | bytes 442376 | tf_op jit(solution)/shard_map/ppermute | solution.py:213
  17.5 8.7 %collective-permute-start.9 = (bf16[288,256]{1,0:T(8,128)(2,1)S(1)}, bf16[288,256]{1,0:T(8,128)(2,1)S(1)}, u32[]{:S(2)}, u32[]{:S(2)}) collective-permute-start(bf16[288,256]{1,0:T(8,128)(2,1)S(1)} %get-tuple-element.17), channel_id=1, source_target_pairs={{0,6},{1,15},{2,4},{3,13},{4,2},{5,11},{6,0},{7,9},{8,14},{9,7},{1... | collective-permute-start | bytes 442376 | tf_op jit(solution)/shard_map/ppermute | solution.py:213
  20.4 7.2 %collective-permute-start.7 = (bf16[288,256]{1,0:T(8,128)(2,1)S(1)}, bf16[288,256]{1,0:T(8,128)(2,1)S(1)}, u32[]{:S(2)}, u32[]{:S(2)}) collective-permute-start(bf16[288,256]{1,0:T(8,128)(2,1)S(1)} %get-tuple-element.17), channel_id=1, source_target_pairs={{0,4},{1,13},{2,6},{3,15},{4,0},{5,9},{6,2},{7,11},{8,12},{9,5},{1... | collective-permute-start | bytes 442376 | tf_op jit(solution)/shard_map/ppermute | solution.py:213
  20.9 6.7 %collective-permute-start.10 = (bf16[288,256]{1,0:T(8,128)(2,1)S(1)}, bf16[288,256]{1,0:T(8,128)(2,1)S(1)}, u32[]{:S(2)}, u32[]{:S(2)}) collective-permute-start(bf16[288,256]{1,0:T(8,128)(2,1)S(1)} %get-tuple-element.18), channel_id=1, source_target_pairs={{0,10},{1,3},{2,8},{3,1},{4,14},{5,7},{6,12},{7,5},{8,2},{9,11},{1... | collective-permute-start | bytes 442376 | tf_op jit(solution)/shard_map/ppermute | solution.py:213
  21.8 7.0 %collective-permute-start.8 = (bf16[288,256]{1,0:T(8,128)(2,1)S(1)}, bf16[288,256]{1,0:T(8,128)(2,1)S(1)}, u32[]{:S(2)}, u32[]{:S(2)}) collective-permute-start(bf16[288,256]{1,0:T(8,128)(2,1)S(1)} %get-tuple-element.18), channel_id=1, source_target_pairs={{0,8},{1,1},{2,10},{3,3},{4,12},{5,5},{6,14},{7,7},{8,0},{9,9},{10... | collective-permute-start | bytes 442376 | tf_op jit(solution)/shard_map/ppermute | solution.py:213
  28.8 3.0 %copy-start = (bf16[512,256]{1,0:T(8,128)(2,1)S(1)}, bf16[512,256]{1,0:T(8,128)(2,1)}, u32[]{:S(2)}) copy-start(bf16[512,256]{1,0:T(8,128)(2,1)} %old.1) | copy-start | bytes 786436
  29.4 2.4 %collective-permute-start.11 = (f32[520,256]{1,0:T(8,128)S(1)}, f32[520,256]{1,0:T(8,128)S(1)}, u32[]{:S(2)}, u32[]{:S(2)}) collective-permute-start(f32[520,256]{1,0:T(8,128)S(1)} %get-tuple-element.19.mine), channel_id=1, source_target_pairs={{0,1},{1,0},{2,3},{3,2},{4,5},{5,4},{6,7},{7,6},{8,9},{9,8},{10,11... | collective-permute-start | bytes 1597448 | tf_op jit(solution)/shard_map/ppermute | solution.py:204
  29.5 2.1 %collective-permute-start.12 = (bf16[288,256]{1,0:T(8,128)(2,1)S(1)}, bf16[288,256]{1,0:T(8,128)(2,1)S(1)}, u32[]{:S(2)}, u32[]{:S(2)}) collective-permute-start(bf16[288,256]{1,0:T(8,128)(2,1)S(1)} %get-tuple-element.20), channel_id=1, source_target_pairs={{0,1},{1,0},{2,3},{3,2},{4,5},{5,4},{6,7},{7,6},{8,9},{9,8},{10,11... | collective-permute-start | bytes 442376 | tf_op jit(solution)/shard_map/ppermute | solution.py:204
  30.0 1.8 %collective-permute-start.13 = (bf16[288,256]{1,0:T(8,128)(2,1)S(1)}, bf16[288,256]{1,0:T(8,128)(2,1)S(1)}, u32[]{:S(2)}, u32[]{:S(2)}) collective-permute-start(bf16[288,256]{1,0:T(8,128)(2,1)S(1)} %get-tuple-element.21), channel_id=1, source_target_pairs={{0,1},{1,0},{2,3},{3,2},{4,5},{5,4},{6,7},{7,6},{8,9},{9,8},{10,11... | collective-permute-start | bytes 442376 | tf_op jit(solution)/shard_map/ppermute | solution.py:204

commit v4 on v3

--- a/solution.py
+++ b/solution.py
@@ -39,27 +39,36 @@
     return lax.axis_index("rep") & 1
 
 
-def _head(list_dev, me, table, payload):
-    n = payload.shape[0] - HEAD
-    low = payload[n:, :].astype(jnp.float32)
+def _heads(list_dev, me, table, payloads):
+    n = payloads[0].shape[0] - HEAD
+    low = jnp.concatenate([p[n:, :].astype(jnp.float32) for p in payloads], axis=1)
     slot = _slots(table, (low[0:1, :] + 256.0 * low[1:2, :]).astype(jnp.int32))
     relative = (slot >> _log2(list_dev)) ^ me
     code = (slot & (list_dev - 1)) + 1
-    member = (_iota((HEAD, n), 0) == relative).astype(jnp.float32)
+    lo, hi = (code & 255).astype(jnp.float32), (code >> 8).astype(jnp.float32)
+    member = (_iota((HEAD, low.shape[1]), 0) == relative).astype(jnp.float32)
+    at = [slice(i * n, (i + 1) * n) for i in range(len(payloads))]
     before = _bf16(_iota((n, n), 0) < _iota((n, n), 1))
-    count = jnp.dot(member.astype(jnp.bfloat16), before, preferred_element_type=jnp.float32)
-    rank = jnp.sum(member * count, axis=0, keepdims=True).astype(jnp.int32)
-    return rank, relative, (code & 255).astype(jnp.float32), (code >> 8).astype(jnp.float32)
-
-
-def _route(head, rows, outs, base):
+    count = jnp.dot(
+        jnp.concatenate([member[:, i] for i in at], axis=0).astype(jnp.bfloat16),
+        before,
+        preferred_element_type=jnp.float32,
+    )
+    out = []
+    for j, i in enumerate(at):
+        rank = jnp.sum(member[:, i] * count[j * HEAD : (j + 1) * HEAD, :], axis=0, keepdims=True)
+        out.append((rank.astype(jnp.int32), relative[:, i], lo[:, i], hi[:, i]))
+    return out
+
+
+def _route(head, rows, ks):
     rank, relative, lo, hi = head
     n = rows.shape[0]
     capacity = n // 2
     hot = jnp.concatenate(
         [
             (_iota((capacity, n), 0) == jnp.where(relative == k, rank, -1)).astype(jnp.float32)
-            for k, _ in outs
+            for k in ks
         ],
         axis=0,
     ).astype(jnp.bfloat16)
@@ -68,39 +77,43 @@
     labels = lax.dot_general(
         values, hot, (((1,), (1,)), ((), ())), preferred_element_type=jnp.float32
     )
-    for i, (_, out) in enumerate(outs):
-        at = slice(i * capacity, (i + 1) * capacity)
-        line = jnp.concatenate([labels[0:1, at], labels[1:2, at]], axis=1)
-        out[base : base + capacity, :] = moved[at, :]
-        out[base + capacity : base + capacity + HEAD, :] = jnp.broadcast_to(
-            line, (HEAD, line.shape[1])
+    at = [slice(i * capacity, (i + 1) * capacity) for i in range(len(ks))]
+    return [
+        (moved[i, :], jnp.concatenate([labels[0:1, i], labels[1:2, i]], axis=1)) for i in at
+    ]
+
+
+def _owners():
+    return 1 - _core(), 2 + _core()
+
+
+def _split_kernel(list_dev, payload, twin, table, *refs):
+    mine, other = payload[...], twin[...]
+    both = jnp.where(_core() == 0, mine, other), jnp.where(_core() == 0, other, mine)
+    n = mine.shape[0] - HEAD
+    heads = _heads(list_dev, lax.axis_index("items"), table[...], both)
+    first, second = (_route(h, p[0:n, :], _owners()) for h, p in zip(heads, both))
+    for out, (rows0, line0), (rows1, line1) in zip(refs[-2:], first, second):
+        capacity = rows0.shape[0]
+        out[0:capacity, :] = rows0
+        out[capacity : 2 * capacity, :] = rows1
+        out[2 * capacity : 2 * capacity + HEAD, :] = jnp.where(
+            _iota((HEAD, line0.shape[1]), 0) == 0, line0, line1
         ).astype(jnp.bfloat16)
 
 
-def _split_kernel(list_dev, payload, twin, table, *refs):
-    a, b = refs[-2:]
-    core, me = _core(), lax.axis_index("items")
-    n = payload.shape[0] - HEAD
-    size = n // 2 + HEAD
-    mine, other = payload[...], twin[...]
-    for i in range(2):
-        part = jnp.where(core == i, mine, other)
-        head = _head(list_dev, me, table[...], part)
-        _route(head, part[0:n, :], ((1 + 2 * core, a), (2 - 2 * core, b)), i * size)
-
-
-def _labels(head):
-    head = head.astype(jnp.float32)[0:1, :]
-    capacity = head.shape[1] // 2
-    return (head[:, :capacity] + 256.0 * head[:, capacity:]).astype(jnp.int32) - 1
+def _labels(line):
+    line = line.astype(jnp.float32)
+    capacity = line.shape[1] // 2
+    return (line[:, :capacity] + 256.0 * line[:, capacity:]).astype(jnp.int32) - 1
 
 
 def _parts(block):
     capacity = block.shape[1] // 2
-    size = capacity + HEAD
+    head = block[2 * capacity :, :].astype(jnp.float32)
     return [
-        (block[i : i + capacity, :], _labels(block[i + capacity : i + size, :]))
-        for i in range(0, block.shape[0], size)
+        (block[i * capacity : (i + 1) * capacity, :], _labels(head[i : i + 1, :]))
+        for i in range(2)
     ]
 
 
@@ -131,11 +144,16 @@
     else:
         out[0:lists, :] = mine + side
         out[lists:, :] = lines
-    size = a.shape[0] // 2
+    capacity = width // 2
+    lines = []
     for i, block in enumerate((a, b)):
-        pack[i * size : (i + 1) * size, :] = jnp.where(
-            _core() == 0, block[size:, :], block[0:size, :]
-        )
+        rows = jnp.where(_core() == 0, block[capacity : 2 * capacity, :], block[0:capacity, :])
+        pack[i * capacity : (i + 1) * capacity, :] = rows
+        head = block[2 * capacity :, :].astype(jnp.float32)
+        lines.append(jnp.where(_core() == 0, head[1:2, :], head[0:1, :]))
+    pack[2 * capacity :, :] = jnp.where(
+        _iota((HEAD, width), 0) == 0, lines[0], lines[1]
+    ).astype(jnp.bfloat16)
 
 
 def _codes_kernel(mine, other, old, *refs):
@@ -152,14 +170,14 @@
         fresh[at_i, :] = (total / (counts + 1.0)).astype(jnp.bfloat16)
     table = fresh[...]
     eye = _iota((capacity, capacity), 0) == _iota((capacity, capacity), 1)
-    size = capacity + HEAD
     ordered = []
     for i, (a, b, pack) in enumerate((blocks[0:3], blocks[3:6])):
         base = me ^ (4 * i)
-        for block, k in ((a, 1 + 2 * core), (b, 2 - 2 * core)):
-            part = jnp.where(core == 0, block[0:size, :], block[size:, :])
-            ordered.append((base ^ k, _parts(part)[0]))
-        for part, k in zip(_parts(pack), (3 - 2 * core, 2 * core)):
+        for block, k in zip((a, b), _owners()):
+            (rows0, labels0), (rows1, labels1) = _parts(block)
+            part = jnp.where(core == 0, rows0, rows1), jnp.where(core == 0, labels0, labels1)
+            ordered.append((base ^ k, part))
+        for part, k in zip(_parts(pack), (core, 3 - core)):
             ordered.append((base ^ k, part))
     for source, (rows, labels) in ordered:
         column = jnp.sum(
@@ -204,7 +222,7 @@
         return lax.ppermute(a, ("items", "rep"), [(i, i ^ swap) for i in range(peers * reps)])
 
     table = list_slot.reshape(-1, 128)
-    pair = jax.ShapeDtypeStruct((2 * (capacity + HEAD), width), jnp.bfloat16)
+    pair = jax.ShapeDtypeStruct((2 * capacity + HEAD, width), jnp.bfloat16)
     total = jax.ShapeDtypeStruct((list_dev + 8, width), jnp.float32)
     flops = 2 * 4 * capacity * item_dev * width
 
@@ -212,23 +230,24 @@
         swap = [x * reps + rep for x in items]
         return lax.ppermute(a, ("items", "rep"), [(i, i ^ swap[i & 1]) for i in range(peers * reps)])
 
-    def to_owners(payload, weight, *after):
+    def to_owners(payload, weight, extra, *after):
+        wide = jax.ShapeDtypeStruct((pair.shape[0] + extra, width), jnp.bfloat16)
         a, b = _call(
             lambda *refs: _split_kernel(list_dev, *refs),
-            [pair] * 2,
+            [wide] * 2,
             (payload, hop(payload, 0, 1), table, *after),
             flops=weight * flops,
         )
-        side_b, near_b = spread(b, (2, 0), 2), spread(b, (2, 0), 0)
-        side_a, near_a = spread(a, (1, 3), 2), spread(a, (1, 3), 0)
+        side_b, near_b = spread(b, (2, 3), 2), spread(b, (2, 3), 0)
+        side_a, near_a = spread(a, (1, 0), 2), spread(a, (1, 0), 0)
         return near_a, near_b, side_a, side_b
 
     row = lax.broadcasted_iota(jnp.int32, (item_dev + HEAD, width), 0)
     ids = jnp.where(row == item_dev, assign & 255, assign >> 8).astype(jnp.bfloat16)
     payload = jnp.where(row < item_dev, jnp.pad(embeds, ((0, HEAD), (0, 0))), ids)
     far = hop(payload, 4)
-    near = to_owners(payload, 1000)
-    away = to_owners(far, 1, near[3])
+    near = to_owners(payload, 1000, HEAD)
+    away = to_owners(far, 1, 0, *(near[i] for i in (2,)))
     flops = 2 * list_dev * capacity * width
     mine, near_pack = _call(_sums_kernel, [total, pair], near, flops=8 * flops)
     near_pack = hop(near_pack, 0, 1)

time: 33.6 us -> 32.9 us (0.979)
  waiting for transfers between devices: 7.36 us -> 6.8 us
  Pallas kernels: 4.62 us -> 4.12 us
    ppermute x6, waiting for transfers between devices: 3.63 us -> 2.48 us  [hop(): lax.ppermute(a, ('items', 'rep'), [(i, i ^ swap) for i in range(peers * r...]
    ppermute x8, waiting for transfers between devices: 3.73 us -> 4.32 us  [spread(): lax.ppermute(a, ('items', 'rep'), [(i, i ^ swap[i & 1]) for i in range(pe...]
    pallas_call x5, Pallas kernels: 4.62 us -> 4.12 us  [_call(): pl.pallas_call(kernel, out_shape=outs, in_specs=[VMEM] * len(args), out_s...]
  transfers between devices with their start and end apart: 14 -> 14, of which waited for: 6 -> 6; matrix products, arithmetic and copies ran while one was open for 0% -> 0% of each run, Pallas kernels for 7% -> 6%
where the time goes in v4:
time: 32.9 us; the launch traced here: 32.7 us
  starting transfers between devices  19.3 us (59%)
  waiting for transfers between devices  6.8 us (21%)
  Pallas kernels  4.12 us (13%)
  other arithmetic  1.06 us (3%)
  between operations  0.74 us (2%)
  local copies, waits for them, and re-layouts  0.67 us (2%)
    ppermute x8, starting transfers between devices, spread(): lax.ppermute(a, ('items', 'rep'), [(i, i ^ swap[i & 1]) for i in range(pe...  14.5 us
    ppermute x6, starting transfers between devices, hop(): lax.ppermute(a, ('items', 'rep'), [(i, i ^ swap) for i in range(peers * r...  4.83 us
    ppermute x8, waiting for transfers between devices, spread(): lax.ppermute(a, ('items', 'rep'), [(i, i ^ swap[i & 1]) for i in range(pe...  4.32 us
    pallas_call x5, Pallas kernels, _call(): pl.pallas_call(kernel, out_shape=outs, in_specs=[VMEM] * len(args), out_s...  4.12 us
    ppermute x6, waiting for transfers between devices, hop(): lax.ppermute(a, ('items', 'rep'), [(i, i ^ swap) for i in range(peers * r...  2.48 us
    select_n x1, other arithmetic, per_device_eight(): jnp.where(row < item_dev, jnp.pad(embeds, ((0, HEAD), (0, 0))), ids)  1.05 us
    unnamed x6, local copies, waits for them, and re-layouts  0.67 us
  transfers between devices with their start and end apart: 14, of which 6 were waited for; matrix products, arithmetic and copies ran while one was open for 0% of the time, Pallas kernels for 6%

profile of v4, /device:TPU:0, one launch (start us, length us, event | category | flops | bytes accessed | tf_op | source)
XLA Modules:
  0.0 32.7 jit_solution(10288148887079477832)
XLA Ops:
  0.6 0.0 copy-start.2
  0.7 0.7 %copy-done.2 = s32[256]{0:T(256)S(1)} copy-done((s32[256]{0:T(256)S(1)}, s32[256]{0:T(256)}, u32[]{:S(2)}) %copy-start.2) | copy-done | bytes 1048
  1.3 0.0 copy-start.1
  1.3 1.1 %fusion.refs_0_ = bf16[272,256]{1,0:T(8,128)(2,1)S(1)} fusion(s32[256]{0:T(256)S(1)} %get-tuple-element.26, s32[256]{0:T(256)S(1)} %get-tuple-element.25, bf16[256,256]{1,0:T(8,128)(2,1)} %param.4, pred[272]{0:T(512)(128)(4,1)S(1)} %get-tuple-element.27, pred[272]{0:T(512)(128)(4,1)S(1)} %get-tuple-element.28), kind=kLoop, calls=%fused_computation.1 | loop fusion | flops 208896 | bytes 272928 | tf_op jit(solution)/shard_map/jit(_where)/select_n | solution.py:247
  2.4 0.5 %collective-permute-start = (bf16[272,256]{1,0:T(8,128)(2,1)S(1)}, bf16[272,256]{1,0:T(8,128)(2,1)S(1)}, u32[]{:S(2)}, u32[]{:S(2)}) collective-permute-start(bf16[272,256]{1,0:T(8,128)(2,1)S(1)} %fusion.refs_0_), channel_id=1, source_target_pairs={{0,1},{1,0},{2,3},{3,2},{4,5},{5,4},{6,7},{7,6},{8,9},{9,8},{10,11... | collective-permute-start | bytes 417800 | tf_op jit(solution)/shard_map/ppermute | solution.py:222
  2.9 3.7 %collective-permute-start.5 = (bf16[272,256]{1,0:T(8,128)(2,1)S(1)}, bf16[272,256]{1,0:T(8,128)(2,1)S(1)}, u32[]{:S(2)}, u32[]{:S(2)}) collective-permute-start(bf16[272,256]{1,0:T(8,128)(2,1)S(1)} %fusion.refs_0_), channel_id=1, source_target_pairs={{0,16},{1,17},{2,18},{3,19},{4,20},{5,21},{6,22},{7,23},{8,24},{9,... | collective-permute-start | bytes 417800 | tf_op jit(solution)/shard_map/ppermute | solution.py:222
  6.6 0.0 collective-permute-done.refs_1_
  6.6 0.0 copy-done.1
  6.6 0.7 %shard_map.67 = (bf16[288,256]{1,0:T(8,128)(2,1)S(1)}, bf16[288,256]{1,0:T(8,128)(2,1)S(1)}) custom-call(bf16[272,256]{1,0:T(8,128)(2,1)S(1)} %fusion.refs_0_, bf16[272,256]{1,0:T(8,128)(2,1)S(1)} %collective-permute-done.refs_1_, s32[32,128]{1,0:T(8,128)S(1)} %bitcast.3), custom_call_target="tpu_custom_call" | custom-call | flops 67108864000 | bytes 589824 | tf_op jit(solution)/shard_map/pallas_call | solution.py:203
  7.2 2.5 %collective-permute-start.3 = (bf16[288,256]{1,0:T(8,128)(2,1)S(1)}, bf16[288,256]{1,0:T(8,128)(2,1)S(1)}, u32[]{:S(2)}, u32[]{:S(2)}) collective-permute-start(bf16[288,256]{1,0:T(8,128)(2,1)S(1)} %get-tuple-element.14), channel_id=1, source_target_pairs={{0,6},{1,3},{2,4},{3,1},{4,2},{5,7},{6,0},{7,5},{8,14},{9,11},{10,... | collective-permute-start | bytes 442376 | tf_op jit(solution)/shard_map/ppermute | solution.py:231
  9.7 2.4 %collective-permute-start.1 = (bf16[288,256]{1,0:T(8,128)(2,1)S(1)}, bf16[288,256]{1,0:T(8,128)(2,1)S(1)}, u32[]{:S(2)}, u32[]{:S(2)}) collective-permute-start(bf16[288,256]{1,0:T(8,128)(2,1)S(1)} %get-tuple-element.14), channel_id=1, source_target_pairs={{0,4},{1,1},{2,6},{3,3},{4,0},{5,5},{6,2},{7,7},{8,12},{9,9},{10,1... | collective-permute-start | bytes 442376 | tf_op jit(solution)/shard_map/ppermute | solution.py:231
  12.1 1.6 %collective-permute-start.4 = (bf16[288,256]{1,0:T(8,128)(2,1)S(1)}, bf16[288,256]{1,0:T(8,128)(2,1)S(1)}, u32[]{:S(2)}, u32[]{:S(2)}) collective-permute-start(bf16[288,256]{1,0:T(8,128)(2,1)S(1)} %get-tuple-element.15), channel_id=1, source_target_pairs={{0,10},{1,15},{2,8},{3,13},{4,14},{5,11},{6,12},{7,9},{8,2},{9,7},... | collective-permute-start | bytes 442376 | tf_op jit(solution)/shard_map/ppermute | solution.py:231
  13.8 0.1 collective-permute-done.5.refs_0_
  13.9 0.0 collective-permute-start.6
  13.9 0.8 %collective-permute-start.2 = (bf16[288,256]{1,0:T(8,128)(2,1)S(1)}, bf16[288,256]{1,0:T(8,128)(2,1)S(1)}, u32[]{:S(2)}, u32[]{:S(2)}) collective-permute-start(bf16[288,256]{1,0:T(8,128)(2,1)S(1)} %get-tuple-element.15), channel_id=1, source_target_pairs={{0,8},{1,13},{2,10},{3,15},{4,12},{5,9},{6,14},{7,11},{8,0},{9,5},... | collective-permute-start | bytes 442376 | tf_op jit(solution)/shard_map/ppermute | solution.py:231
  14.7 0.6 %collective-permute-done.6.refs_1_ = bf16[272,256]{1,0:T(8,128)(2,1)S(1)} collective-permute-done((bf16[272,256]{1,0:T(8,128)(2,1)S(1)}, bf16[272,256]{1,0:T(8,128)(2,1)S(1)}, u32[]{:S(2)}, u32[]{:S(2)}) %collective-permute-start.6) | collective-permute-done | bytes 139296 | tf_op jit(solution)/shard_map/ppermute | solution.py:222
  15.3 0.0 collective-permute-done.3.refs_2_.refs_3_
  15.3 0.7 %shard_map.69 = (bf16[272,256]{1,0:T(8,128)(2,1)S(1)}, bf16[272,256]{1,0:T(8,128)(2,1)S(1)}) custom-call(bf16[272,256]{1,0:T(8,128)(2,1)S(1)} %collective-permute-done.5.refs_0_, bf16[272,256]{1,0:T(8,128)(2,1)S(1)} %collective-permute-done.6.refs_1_, s32[32,128]{1,0:T(8,128)S(1)} %bitcast.4, bf16[288,256]{1,0:T(8,128)(2,1)S(1)} %collective-permute-done.3.refs_2_.refs_3_), custom_call_target="tpu_custom_call" | custom-call | flops 67108864 | bytes 720896 | tf_op jit(solution)/shard_map/pallas_call | solution.py:203
  15.9 2.6 %collective-permute-start.9 = (bf16[272,256]{1,0:T(8,128)(2,1)S(1)}, bf16[272,256]{1,0:T(8,128)(2,1)S(1)}, u32[]{:S(2)}, u32[]{:S(2)}) collective-permute-start(bf16[272,256]{1,0:T(8,128)(2,1)S(1)} %get-tuple-element.17), channel_id=1, source_target_pairs={{0,6},{1,3},{2,4},{3,1},{4,2},{5,7},{6,0},{7,5},{8,14},{9,11},{10,... | collective-permute-start | bytes 417800 | tf_op jit(solution)/shard_map/ppermute | solution.py:231
  18.5 2.4 %collective-permute-start.7 = (bf16[272,256]{1,0:T(8,128)(2,1)S(1)}, bf16[272,256]{1,0:T(8,128)(2,1)S(1)}, u32[]{:S(2)}, u32[]{:S(2)}) collective-permute-start(bf16[272,256]{1,0:T(8,128)(2,1)S(1)} %get-tuple-element.17), channel_id=1, source_target_pairs={{0,4},{1,1},{2,6},{3,3},{4,0},{5,5},{6,2},{7,7},{8,12},{9,9},{10,1... | collective-permute-start | bytes 417800 | tf_op jit(solution)/shard_map/ppermute | solution.py:231
  20.9 0.0 collective-permute-done.1.refs_0_
  20.9 2.1 %collective-permute-start.10 = (bf16[272,256]{1,0:T(8,128)(2,1)S(1)}, bf16[272,256]{1,0:T(8,128)(2,1)S(1)}, u32[]{:S(2)}, u32[]{:S(2)}) collective-permute-start(bf16[272,256]{1,0:T(8,128)(2,1)S(1)} %get-tuple-element.18), channel_id=1, source_target_pairs={{0,10},{1,15},{2,8},{3,13},{4,14},{5,11},{6,12},{7,9},{8,2},{9,7},... | collective-permute-start | bytes 417800 | tf_op jit(solution)/shard_map/ppermute | solution.py:231
  23.0 0.0 collective-permute-done.4.refs_3_
  23.0 0.1 collective-permute-start.8
  23.1 0.0 collective-permute-done.2.refs_1_
  23.1 0.6 %shard_map.68 = (f32[520,256]{1,0:T(8,128)S(1)}, bf16[272,256]{1,0:T(8,128)(2,1)S(1)}) custom-call(bf16[288,256]{1,0:T(8,128)(2,1)S(1)} %collective-permute-done.1.refs_0_, bf16[288,256]{1,0:T(8,128)(2,1)S(1)} %collective-permute-done.2.refs_1_, bf16[288,256]{1,0:T(8,128)(2,1)S(1)} %collective-permute-done.3.refs_2_.refs_3_, ...), custom_call_target="tpu_custom_call" | custom-call | flops 268435456 | bytes 1261568 | tf_op jit(solution)/shard_map/pallas_call | solution.py:203
  23.8 0.0 collective-permute-done.9.refs_3_
  23.8 3.6 %collective-permute-done.7.refs_1_.refs_3_ = bf16[272,256]{1,0:T(8,128)(2,1)S(1)} collective-permute-done((bf16[272,256]{1,0:T(8,128)(2,1)S(1)}, bf16[272,256]{1,0:T(8,128)(2,1)S(1)}, u32[]{:S(2)}, u32[]{:S(2)}) %collective-permute-start.7) | collective-permute-done | bytes 139296 | tf_op jit(solution)/shard_map/ppermute | solution.py:231
  27.4 0.0 collective-permute-done.10.refs_4_
  27.4 0.7 %collective-permute-done.8.refs_2_.refs_4_ = bf16[272,256]{1,0:T(8,128)(2,1)S(1)} collective-permute-done((bf16[272,256]{1,0:T(8,128)(2,1)S(1)}, bf16[272,256]{1,0:T(8,128)(2,1)S(1)}, u32[]{:S(2)}, u32[]{:S(2)}) %collective-permute-start.8) | collective-permute-done | bytes 139296 | tf_op jit(solution)/shard_map/ppermute | solution.py:231
  28.1 0.0 copy-start
  28.1 0.6 %shard_map.70 = (f32[520,256]{1,0:T(8,128)S(1)}, bf16[272,256]{1,0:T(8,128)(2,1)S(1)}) custom-call(f32[520,256]{1,0:T(8,128)S(1)} %get-tuple-element.16.refs_0_, bf16[272,256]{1,0:T(8,128)(2,1)S(1)} %collective-permute-done.7.refs_1_.refs_3_, bf16[272,256]{1,0:T(8,128)(2,1)S(1)} %collective-permute-done.8.refs_2_.refs_4_, ...), custom_call_target="tpu_custom_call" | custom-call | flops 268435456 | bytes 1761280 | tf_op jit(solution)/shard_map/pallas_call | solution.py:203
  28.7 0.1 collective-permute-start.11
  28.8 0.5 %collective-permute-start.12 = (bf16[272,256]{1,0:T(8,128)(2,1)S(1)}, bf16[272,256]{1,0:T(8,128)(2,1)S(1)}, u32[]{:S(2)}, u32[]{:S(2)}) collective-permute-start(bf16[272,256]{1,0:T(8,128)(2,1)S(1)} %get-tuple-element.20), channel_id=1, source_target_pairs={{0,1},{1,0},{2,3},{3,2},{4,5},{5,4},{6,7},{7,6},{8,9},{9,8},{10,11... | collective-permute-start | bytes 417800 | tf_op jit(solution)/shard_map/ppermute | solution.py:222
  29.3 0.1 collective-permute-start.13
  29.3 1.5 %collective-permute-done.12.refs_2_ = bf16[272,256]{1,0:T(8,128)(2,1)S(1)} collective-permute-done((bf16[272,256]{1,0:T(8,128)(2,1)S(1)}, bf16[272,256]{1,0:T(8,128)(2,1)S(1)}, u32[]{:S(2)}, u32[]{:S(2)}) %collective-permute-start.12) | collective-permute-done | bytes 139296 | tf_op jit(solution)/shard_map/ppermute | solution.py:222
  30.9 0.2 collective-permute-done.13.refs_5_
  31.1 0.0 collective-permute-done.11.other
  31.1 0.0 copy-done
  31.1 1.6 %shard_map.71 = (bf16[512,256]{1,0:T(8,128)(2,1)}, bf16[1024,256]{1,0:T(8,128)(2,1)}, f32[8,128]{1,0:T(8,128)}) custom-call(f32[520,256]{1,0:T(8,128)S(1)} %get-tuple-element.19.mine, f32[520,256]{1,0:T(8,128)S(1)} %collective-permute-done.11.other, bf16[512,256]{1,0:T(8,128)(2,1)S(1)} %copy-done, bf16[288,256]{1,0:T(8,128)(2,1)S(1)} %collective-permute-done.1.refs_0_, ...), custom_call_target="tpu_custom_call" | custom-call | flops 268435456 | bytes 2969600 | tf_op jit(solution)/shard_map/pallas_call | solution.py:203
  (2 shorter events, 0.0 us)
Async XLA Ops:
  0.6 0.7 %copy-start.2 = (s32[256]{0:T(256)S(1)}, s32[256]{0:T(256)}, u32[]{:S(2)}) copy-start(s32[256]{0:T(256)} %param.5) | copy-start | bytes 3076
  1.3 5.3 %copy-start.1 = (s32[4096]{0:T(1024)S(1)}, s32[4096]{0:T(1024)}, u32[]{:S(2)}) copy-start(s32[4096]{0:T(1024)} %param.6) | copy-start | bytes 49156
  2.4 4.2 %collective-permute-start = (bf16[272,256]{1,0:T(8,128)(2,1)S(1)}, bf16[272,256]{1,0:T(8,128)(2,1)S(1)}, u32[]{:S(2)}, u32[]{:S(2)}) collective-permute-start(bf16[272,256]{1,0:T(8,128)(2,1)S(1)} %fusion.refs_0_), channel_id=1, source_target_pairs={{0,1},{1,0},{2,3},{3,2},{4,5},{5,4},{6,7},{7,6},{8,9},{9,8},{10,11... | collective-permute-start | bytes 417800 | tf_op jit(solution)/shard_map/ppermute | solution.py:222
  2.9 11.0 %collective-permute-start.5 = (bf16[272,256]{1,0:T(8,128)(2,1)S(1)}, bf16[272,256]{1,0:T(8,128)(2,1)S(1)}, u32[]{:S(2)}, u32[]{:S(2)}) collective-permute-start(bf16[272,256]{1,0:T(8,128)(2,1)S(1)} %fusion.refs_0_), channel_id=1, source_target_pairs={{0,16},{1,17},{2,18},{3,19},{4,20},{5,21},{6,22},{7,23},{8,24},{9,... | collective-permute-start | bytes 417800 | tf_op jit(solution)/shard_map/ppermute | solution.py:222
  7.2 8.0 %collective-permute-start.3 = (bf16[288,256]{1,0:T(8,128)(2,1)S(1)}, bf16[288,256]{1,0:T(8,128)(2,1)S(1)}, u32[]{:S(2)}, u32[]{:S(2)}) collective-permute-start(bf16[288,256]{1,0:T(8,128)(2,1)S(1)} %get-tuple-element.14), channel_id=1, source_target_pairs={{0,6},{1,3},{2,4},{3,1},{4,2},{5,7},{6,0},{7,5},{8,14},{9,11},{10,... | collective-permute-start | bytes 442376 | tf_op jit(solution)/shard_map/ppermute | solution.py:231
  9.7 11.2 %collective-permute-start.1 = (bf16[288,256]{1,0:T(8,128)(2,1)S(1)}, bf16[288,256]{1,0:T(8,128)(2,1)S(1)}, u32[]{:S(2)}, u32[]{:S(2)}) collective-permute-start(bf16[288,256]{1,0:T(8,128)(2,1)S(1)} %get-tuple-element.14), channel_id=1, source_target_pairs={{0,4},{1,1},{2,6},{3,3},{4,0},{5,5},{6,2},{7,7},{8,12},{9,9},{10,1... | collective-permute-start | bytes 442376 | tf_op jit(solution)/shard_map/ppermute | solution.py:231
  12.1 10.9 %collective-permute-start.4 = (bf16[288,256]{1,0:T(8,128)(2,1)S(1)}, bf16[288,256]{1,0:T(8,128)(2,1)S(1)}, u32[]{:S(2)}, u32[]{:S(2)}) collective-permute-start(bf16[288,256]{1,0:T(8,128)(2,1)S(1)} %get-tuple-element.15), channel_id=1, source_target_pairs={{0,10},{1,15},{2,8},{3,13},{4,14},{5,11},{6,12},{7,9},{8,2},{9,7},... | collective-permute-start | bytes 442376 | tf_op jit(solution)/shard_map/ppermute | solution.py:231
  13.9 1.4 %collective-permute-start.6 = (bf16[272,256]{1,0:T(8,128)(2,1)S(1)}, bf16[272,256]{1,0:T(8,128)(2,1)S(1)}, u32[]{:S(2)}, u32[]{:S(2)}) collective-permute-start(bf16[272,256]{1,0:T(8,128)(2,1)S(1)} %collective-permute-done.5.refs_0_), channel_id=1, source_target_pairs={{0,1},{1,0},{2,3},{3,2},{4,5},{5,4},{6,7},{7,6},{8,9},{9,8},{10,11... | collective-permute-start | bytes 417800 | tf_op jit(solution)/shard_map/ppermute | solution.py:222
  13.9 9.2 %collective-permute-start.2 = (bf16[288,256]{1,0:T(8,128)(2,1)S(1)}, bf16[288,256]{1,0:T(8,128)(2,1)S(1)}, u32[]{:S(2)}, u32[]{:S(2)}) collective-permute-start(bf16[288,256]{1,0:T(8,128)(2,1)S(1)} %get-tuple-element.15), channel_id=1, source_target_pairs={{0,8},{1,13},{2,10},{3,15},{4,12},{5,9},{6,14},{7,11},{8,0},{9,5},... | collective-permute-start | bytes 442376 | tf_op jit(solution)/shard_map/ppermute | solution.py:231
  15.9 7.8 %collective-permute-start.9 = (bf16[272,256]{1,0:T(8,128)(2,1)S(1)}, bf16[272,256]{1,0:T(8,128)(2,1)S(1)}, u32[]{:S(2)}, u32[]{:S(2)}) collective-permute-start(bf16[272,256]{1,0:T(8,128)(2,1)S(1)} %get-tuple-element.17), channel_id=1, source_target_pairs={{0,6},{1,3},{2,4},{3,1},{4,2},{5,7},{6,0},{7,5},{8,14},{9,11},{10,... | collective-permute-start | bytes 417800 | tf_op jit(solution)/shard_map/ppermute | solution.py:231
  18.5 8.8 %collective-permute-start.7 = (bf16[272,256]{1,0:T(8,128)(2,1)S(1)}, bf16[272,256]{1,0:T(8,128)(2,1)S(1)}, u32[]{:S(2)}, u32[]{:S(2)}) collective-permute-start(bf16[272,256]{1,0:T(8,128)(2,1)S(1)} %get-tuple-element.17), channel_id=1, source_target_pairs={{0,4},{1,1},{2,6},{3,3},{4,0},{5,5},{6,2},{7,7},{8,12},{9,9},{10,1... | collective-permute-start | bytes 417800 | tf_op jit(solution)/shard_map/ppermute | solution.py:231
  20.9 6.4 %collective-permute-start.10 = (bf16[272,256]{1,0:T(8,128)(2,1)S(1)}, bf16[272,256]{1,0:T(8,128)(2,1)S(1)}, u32[]{:S(2)}, u32[]{:S(2)}) collective-permute-start(bf16[272,256]{1,0:T(8,128)(2,1)S(1)} %get-tuple-element.18), channel_id=1, source_target_pairs={{0,10},{1,15},{2,8},{3,13},{4,14},{5,11},{6,12},{7,9},{8,2},{9,7},... | collective-permute-start | bytes 417800 | tf_op jit(solution)/shard_map/ppermute | solution.py:231
  23.0 5.1 %collective-permute-start.8 = (bf16[272,256]{1,0:T(8,128)(2,1)S(1)}, bf16[272,256]{1,0:T(8,128)(2,1)S(1)}, u32[]{:S(2)}, u32[]{:S(2)}) collective-permute-start(bf16[272,256]{1,0:T(8,128)(2,1)S(1)} %get-tuple-element.18), channel_id=1, source_target_pairs={{0,8},{1,13},{2,10},{3,15},{4,12},{5,9},{6,14},{7,11},{8,0},{9,5},... | collective-permute-start | bytes 417800 | tf_op jit(solution)/shard_map/ppermute | solution.py:231
  28.1 3.0 %copy-start = (bf16[512,256]{1,0:T(8,128)(2,1)S(1)}, bf16[512,256]{1,0:T(8,128)(2,1)}, u32[]{:S(2)}) copy-start(bf16[512,256]{1,0:T(8,128)(2,1)} %old.1) | copy-start | bytes 786436
  28.7 2.4 %collective-permute-start.11 = (f32[520,256]{1,0:T(8,128)S(1)}, f32[520,256]{1,0:T(8,128)S(1)}, u32[]{:S(2)}, u32[]{:S(2)}) collective-permute-start(f32[520,256]{1,0:T(8,128)S(1)} %get-tuple-element.19.mine), channel_id=1, source_target_pairs={{0,1},{1,0},{2,3},{3,2},{4,5},{5,4},{6,7},{7,6},{8,9},{9,8},{10,11... | collective-permute-start | bytes 1597448 | tf_op jit(solution)/shard_map/ppermute | solution.py:222
  28.8 2.1 %collective-permute-start.12 = (bf16[272,256]{1,0:T(8,128)(2,1)S(1)}, bf16[272,256]{1,0:T(8,128)(2,1)S(1)}, u32[]{:S(2)}, u32[]{:S(2)}) collective-permute-start(bf16[272,256]{1,0:T(8,128)(2,1)S(1)} %get-tuple-element.20), channel_id=1, source_target_pairs={{0,1},{1,0},{2,3},{3,2},{4,5},{5,4},{6,7},{7,6},{8,9},{9,8},{10,11... | collective-permute-start | bytes 417800 | tf_op jit(solution)/shard_map/ppermute | solution.py:222
  29.3 1.8 %collective-permute-start.13 = (bf16[272,256]{1,0:T(8,128)(2,1)S(1)}, bf16[272,256]{1,0:T(8,128)(2,1)S(1)}, u32[]{:S(2)}, u32[]{:S(2)}) collective-permute-start(bf16[272,256]{1,0:T(8,128)(2,1)S(1)} %get-tuple-element.21), channel_id=1, source_target_pairs={{0,1},{1,0},{2,3},{3,2},{4,5},{5,4},{6,7},{7,6},{8,9},{9,8},{10,11... | collective-permute-start | bytes 417800 | tf_op jit(solution)/shard_map/ppermute | solution.py:222

commit v5 on v4

--- a/solution.py
+++ b/solution.py
@@ -81,6 +81,12 @@
     return [
         (moved[i, :], jnp.concatenate([labels[0:1, i], labels[1:2, i]], axis=1)) for i in at
     ]
+
+
+def _ids_kernel(assign, _, out):
+    lo, hi = (assign[...] & 255).astype(jnp.float32), (assign[...] >> 8).astype(jnp.float32)
+    n = assign.shape[1]
+    out[n:, :] = jnp.where(_iota((HEAD, n), 0) == 0, lo, hi).astype(jnp.bfloat16)
 
 
 def _owners():
@@ -156,7 +162,28 @@
     ).astype(jnp.bfloat16)
 
 
-def _codes_kernel(mine, other, old, *refs):
+def _hot(labels, lists):
+    capacity = labels.shape[1]
+    eye = _iota((capacity, capacity), 0) == _iota((capacity, capacity), 1)
+    column = jnp.sum(
+        jnp.where(eye, labels.astype(jnp.float32), 0.0), axis=1, keepdims=True
+    ).astype(jnp.int32)
+    return _bf16(_iota((capacity, lists), 1) == column)
+
+
+def _own_part(block):
+    (rows0, labels0), (rows1, labels1) = _parts(block)
+    return jnp.where(_core() == 0, rows0, rows1), jnp.where(_core() == 0, labels0, labels1)
+
+
+def _hot_kernel(*refs):
+    (*blocks, out) = refs
+    capacity = blocks[0].shape[1] // 2
+    for i, block in enumerate(blocks):
+        out[i * capacity : (i + 1) * capacity, :] = _hot(_own_part(block)[1], out.shape[1])
+
+
+def _codes_kernel(mine, other, old, hots, *refs):
     (*blocks, fresh, codes, scales) = refs
     lists, width = fresh.shape
     capacity = width // 2
@@ -173,17 +200,12 @@
     ordered = []
     for i, (a, b, pack) in enumerate((blocks[0:3], blocks[3:6])):
         base = me ^ (4 * i)
-        for block, k in zip((a, b), _owners()):
-            (rows0, labels0), (rows1, labels1) = _parts(block)
-            part = jnp.where(core == 0, rows0, rows1), jnp.where(core == 0, labels0, labels1)
-            ordered.append((base ^ k, part))
-        for part, k in zip(_parts(pack), (core, 3 - core)):
-            ordered.append((base ^ k, part))
-    for source, (rows, labels) in ordered:
-        column = jnp.sum(
-            jnp.where(eye, labels.astype(jnp.float32), 0.0), axis=1, keepdims=True
-        ).astype(jnp.int32)
-        hot = _bf16(_iota((capacity, lists), 1) == column)
+        for j, (block, k) in enumerate(zip((a, b), _owners())):
+            at = (2 * i + j) * capacity
+            ordered.append((base ^ k, _own_part(block)[0], hots[at : at + capacity, :]))
+        for (rows, labels), k in zip(_parts(pack), (core, 3 - core)):
+            ordered.append((base ^ k, rows, _hot(labels, lists)))
+    for source, rows, hot in ordered:
         lookup = jnp.dot(hot, table, preferred_element_type=jnp.float32)
         residual = rows.astype(jnp.float32) - lookup
         amax = jnp.max(jnp.abs(residual), axis=1, keepdims=True)
@@ -230,30 +252,38 @@
         swap = [x * reps + rep for x in items]
         return lax.ppermute(a, ("items", "rep"), [(i, i ^ swap[i & 1]) for i in range(peers * reps)])
 
-    def to_owners(payload, weight, extra, *after):
+    def to_owners(payload, extra, *after):
         wide = jax.ShapeDtypeStruct((pair.shape[0] + extra, width), jnp.bfloat16)
         a, b = _call(
             lambda *refs: _split_kernel(list_dev, *refs),
             [wide] * 2,
             (payload, hop(payload, 0, 1), table, *after),
-            flops=weight * flops,
+            flops=flops,
         )
         side_b, near_b = spread(b, (2, 3), 2), spread(b, (2, 3), 0)
         side_a, near_a = spread(a, (1, 0), 2), spread(a, (1, 0), 0)
         return near_a, near_b, side_a, side_b
 
-    row = lax.broadcasted_iota(jnp.int32, (item_dev + HEAD, width), 0)
-    ids = jnp.where(row == item_dev, assign & 255, assign >> 8).astype(jnp.bfloat16)
-    payload = jnp.where(row < item_dev, jnp.pad(embeds, ((0, HEAD), (0, 0))), ids)
+    payload = lax.optimization_barrier(jnp.pad(embeds, ((0, HEAD), (0, 0))))
+    (payload,) = _call(
+        _ids_kernel,
+        [jax.ShapeDtypeStruct(payload.shape, payload.dtype)],
+        (assign.reshape(1, item_dev), payload),
+        input_output_aliases={1: 0},
+    )
     far = hop(payload, 4)
-    near = to_owners(payload, 1000, HEAD)
-    away = to_owners(far, 1, 0, *(near[i] for i in (2,)))
+    near = to_owners(payload, HEAD)
+    away = to_owners(far, 0, near[2])
     flops = 2 * list_dev * capacity * width
     mine, near_pack = _call(_sums_kernel, [total, pair], near, flops=8 * flops)
     near_pack = hop(near_pack, 0, 1)
     mine, away_pack = _call(_sums_kernel, [total, pair], (mine, *away), flops=8 * flops)
     away_pack = hop(away_pack, 0, 1)
     other = hop(mine, 0, 1)
+    own = (*near[0:2], *away[0:2])
+    (hots,) = _call(
+        _hot_kernel, [jax.ShapeDtypeStruct((4 * capacity, list_dev), jnp.bfloat16)], own
+    )
     fresh, codes, scales = _call(
         _codes_kernel,
         [
@@ -261,7 +291,7 @@
             jax.ShapeDtypeStruct((peers * capacity, width), jnp.bfloat16),
             jax.ShapeDtypeStruct((peers, capacity), jnp.float32),
         ],
-        (mine, other, old_centroids, *near[0:2], near_pack, *away[0:2], away_pack),
+        (mine, other, old_centroids, hots, *near[0:2], near_pack, *away[0:2], away_pack),
         flops=8 * flops,
     )
     return (

time: 32.9 us -> 32.7 us (level)
  other arithmetic: 1.06 us -> 0 us
  local copies, waits for them, and re-layouts: 0.67 us -> 1.6 us
    select_n x1 -> x0, other arithmetic: 1.05 us -> none  [per_device_eight(): jnp.where(row < item_dev, jnp.pad(embeds, ((0, HEAD), (0, 0))), ids)]
    pad x0 -> x1, local copies, waits for them, and re-layouts: none -> 0.92 us  [per_device_eight(): payload = lax.optimization_barrier(jnp.pad(embeds, ((0, HEAD), (0, 0))))]
    pallas_call x5 -> x7, Pallas kernels: 4.12 us -> 4.25 us  [_call(): pl.pallas_call(kernel, out_shape=outs, in_specs=[VMEM] * len(args), out_s...]
where the time goes in v5:
time: 32.7 us; the launch traced here: 32.5 us
  starting transfers between devices  19.3 us (59%)
  waiting for transfers between devices  6.59 us (20%)
  Pallas kernels  4.25 us (13%)
  local copies, waits for them, and re-layouts  1.6 us (5%)
  between operations  0.73 us (2%)
    ppermute x8, starting transfers between devices, spread(): lax.ppermute(a, ('items', 'rep'), [(i, i ^ swap[i & 1]) for i in range(pe...  14.5 us
    ppermute x6, starting transfers between devices, hop(): lax.ppermute(a, ('items', 'rep'), [(i, i ^ swap) for i in range(peers * r...  4.83 us
    ppermute x8, waiting for transfers between devices, spread(): lax.ppermute(a, ('items', 'rep'), [(i, i ^ swap[i & 1]) for i in range(pe...  4.31 us
    pallas_call x7, Pallas kernels, _call(): pl.pallas_call(kernel, out_shape=outs, in_specs=[VMEM] * len(args), out_s...  4.25 us
    ppermute x6, waiting for transfers between devices, hop(): lax.ppermute(a, ('items', 'rep'), [(i, i ^ swap) for i in range(peers * r...  2.28 us
    pad x1, local copies, waits for them, and re-layouts, per_device_eight(): payload = lax.optimization_barrier(jnp.pad(embeds, ((0, HEAD), (0, 0))))  0.92 us
    unnamed x6, local copies, waits for them, and re-layouts  0.68 us
  transfers between devices with their start and end apart: 14, of which 6 were waited for; matrix products, arithmetic and copies ran while one was open for 0% of the time, Pallas kernels for 6%

profile of v5, /device:TPU:0, one launch (start us, length us, event | category | flops | bytes accessed | tf_op | source)
XLA Modules:
  0.0 32.5 jit_solution(17378300346097732920)
XLA Ops:
  0.6 0.9 %pad.4._ = bf16[272,256]{1,0:T(8,128)(2,1)S(1)} pad(bf16[256,256]{1,0:T(8,128)(2,1)} %param.4, bf16[]{:T(256)} %constant.2.clone.1), padding=0_16x0_0 | pad | bytes 270338 | tf_op jit(solution)/shard_map/jit(_pad)/pad | solution.py:267
  1.5 0.0 copy-start.2
  1.6 0.7 %copy-done.2 = s32[256]{0:T(256)S(1)} copy-done((s32[256]{0:T(256)S(1)}, s32[256]{0:T(256)}, u32[]{:S(2)}) %copy-start.2) | copy-done | bytes 1048
  2.2 0.0 copy-start.1
  2.2 0.5 %collective-permute-start = (bf16[272,256]{1,0:T(8,128)(2,1)S(1)}, bf16[272,256]{1,0:T(8,128)(2,1)S(1)}, u32[]{:S(2)}, u32[]{:S(2)}) collective-permute-start(bf16[272,256]{1,0:T(8,128)(2,1)S(1)} %shard_map.67.refs_0_), channel_id=1, source_target_pairs={{0,1},{1,0},{2,3},{3,2},{4,5},{5,4},{6,7},{7,6},{8,9},{9,8},{10,11... | collective-permute-start | bytes 417800 | tf_op jit(solution)/shard_map/ppermute | solution.py:244
  2.8 3.7 %collective-permute-start.5 = (bf16[272,256]{1,0:T(8,128)(2,1)S(1)}, bf16[272,256]{1,0:T(8,128)(2,1)S(1)}, u32[]{:S(2)}, u32[]{:S(2)}) collective-permute-start(bf16[272,256]{1,0:T(8,128)(2,1)S(1)} %shard_map.67.refs_0_), channel_id=1, source_target_pairs={{0,16},{1,17},{2,18},{3,19},{4,20},{5,21},{6,22},{7,23},{8,24},{9,... | collective-permute-start | bytes 417800 | tf_op jit(solution)/shard_map/ppermute | solution.py:244
  6.4 0.0 collective-permute-done.refs_1_
  6.4 0.0 copy-done.1
  6.4 0.7 %shard_map.68 = (bf16[288,256]{1,0:T(8,128)(2,1)S(1)}, bf16[288,256]{1,0:T(8,128)(2,1)S(1)}) custom-call(bf16[272,256]{1,0:T(8,128)(2,1)S(1)} %shard_map.67.refs_0_, bf16[272,256]{1,0:T(8,128)(2,1)S(1)} %collective-permute-done.refs_1_, s32[32,128]{1,0:T(8,128)S(1)} %bitcast.4), custom_call_target="tpu_custom_call" | custom-call | flops 67108864 | bytes 589824 | tf_op jit(solution)/shard_map/pallas_call | solution.py:225
  7.1 2.5 %collective-permute-start.3 = (bf16[288,256]{1,0:T(8,128)(2,1)S(1)}, bf16[288,256]{1,0:T(8,128)(2,1)S(1)}, u32[]{:S(2)}, u32[]{:S(2)}) collective-permute-start(bf16[288,256]{1,0:T(8,128)(2,1)S(1)} %get-tuple-element.14), channel_id=1, source_target_pairs={{0,6},{1,3},{2,4},{3,1},{4,2},{5,7},{6,0},{7,5},{8,14},{9,11},{10,... | collective-permute-start | bytes 442376 | tf_op jit(solution)/shard_map/ppermute | solution.py:253
  9.6 2.4 %collective-permute-start.1 = (bf16[288,256]{1,0:T(8,128)(2,1)S(1)}, bf16[288,256]{1,0:T(8,128)(2,1)S(1)}, u32[]{:S(2)}, u32[]{:S(2)}) collective-permute-start(bf16[288,256]{1,0:T(8,128)(2,1)S(1)} %get-tuple-element.14), channel_id=1, source_target_pairs={{0,4},{1,1},{2,6},{3,3},{4,0},{5,5},{6,2},{7,7},{8,12},{9,9},{10,1... | collective-permute-start | bytes 442376 | tf_op jit(solution)/shard_map/ppermute | solution.py:253
  12.0 1.6 %collective-permute-start.4 = (bf16[288,256]{1,0:T(8,128)(2,1)S(1)}, bf16[288,256]{1,0:T(8,128)(2,1)S(1)}, u32[]{:S(2)}, u32[]{:S(2)}) collective-permute-start(bf16[288,256]{1,0:T(8,128)(2,1)S(1)} %get-tuple-element.15), channel_id=1, source_target_pairs={{0,10},{1,15},{2,8},{3,13},{4,14},{5,11},{6,12},{7,9},{8,2},{9,7},... | collective-permute-start | bytes 442376 | tf_op jit(solution)/shard_map/ppermute | solution.py:253
  13.6 0.1 collective-permute-done.5.refs_0_
  13.8 0.0 collective-permute-start.6
  13.8 0.8 %collective-permute-start.2 = (bf16[288,256]{1,0:T(8,128)(2,1)S(1)}, bf16[288,256]{1,0:T(8,128)(2,1)S(1)}, u32[]{:S(2)}, u32[]{:S(2)}) collective-permute-start(bf16[288,256]{1,0:T(8,128)(2,1)S(1)} %get-tuple-element.15), channel_id=1, source_target_pairs={{0,8},{1,13},{2,10},{3,15},{4,12},{5,9},{6,14},{7,11},{8,0},{9,5},... | collective-permute-start | bytes 442376 | tf_op jit(solution)/shard_map/ppermute | solution.py:253
  14.5 0.6 %collective-permute-done.6.refs_1_ = bf16[272,256]{1,0:T(8,128)(2,1)S(1)} collective-permute-done((bf16[272,256]{1,0:T(8,128)(2,1)S(1)}, bf16[272,256]{1,0:T(8,128)(2,1)S(1)}, u32[]{:S(2)}, u32[]{:S(2)}) %collective-permute-start.6) | collective-permute-done | bytes 139296 | tf_op jit(solution)/shard_map/ppermute | solution.py:244
  15.1 0.0 collective-permute-done.3.refs_2_.refs_3_
  15.1 0.7 %shard_map.70 = (bf16[272,256]{1,0:T(8,128)(2,1)S(1)}, bf16[272,256]{1,0:T(8,128)(2,1)S(1)}) custom-call(bf16[272,256]{1,0:T(8,128)(2,1)S(1)} %collective-permute-done.5.refs_0_, bf16[272,256]{1,0:T(8,128)(2,1)S(1)} %collective-permute-done.6.refs_1_, s32[32,128]{1,0:T(8,128)S(1)} %bitcast.5, bf16[288,256]{1,0:T(8,128)(2,1)S(1)} %collective-permute-done.3.refs_2_.refs_3_), custom_call_target="tpu_custom_call" | custom-call | flops 67108864 | bytes 720896 | tf_op jit(solution)/shard_map/pallas_call | solution.py:225
  15.8 2.6 %collective-permute-start.9 = (bf16[272,256]{1,0:T(8,128)(2,1)S(1)}, bf16[272,256]{1,0:T(8,128)(2,1)S(1)}, u32[]{:S(2)}, u32[]{:S(2)}) collective-permute-start(bf16[272,256]{1,0:T(8,128)(2,1)S(1)} %get-tuple-element.17), channel_id=1, source_target_pairs={{0,6},{1,3},{2,4},{3,1},{4,2},{5,7},{6,0},{7,5},{8,14},{9,11},{10,... | collective-permute-start | bytes 417800 | tf_op jit(solution)/shard_map/ppermute | solution.py:253
  18.4 2.4 %collective-permute-start.7 = (bf16[272,256]{1,0:T(8,128)(2,1)S(1)}, bf16[272,256]{1,0:T(8,128)(2,1)S(1)}, u32[]{:S(2)}, u32[]{:S(2)}) collective-permute-start(bf16[272,256]{1,0:T(8,128)(2,1)S(1)} %get-tuple-element.17), channel_id=1, source_target_pairs={{0,4},{1,1},{2,6},{3,3},{4,0},{5,5},{6,2},{7,7},{8,12},{9,9},{10,1... | collective-permute-start | bytes 417800 | tf_op jit(solution)/shard_map/ppermute | solution.py:253
  20.8 0.0 collective-permute-done.1.refs_0_
  20.8 2.1 %collective-permute-start.10 = (bf16[272,256]{1,0:T(8,128)(2,1)S(1)}, bf16[272,256]{1,0:T(8,128)(2,1)S(1)}, u32[]{:S(2)}, u32[]{:S(2)}) collective-permute-start(bf16[272,256]{1,0:T(8,128)(2,1)S(1)} %get-tuple-element.18), channel_id=1, source_target_pairs={{0,10},{1,15},{2,8},{3,13},{4,14},{5,11},{6,12},{7,9},{8,2},{9,7},... | collective-permute-start | bytes 417800 | tf_op jit(solution)/shard_map/ppermute | solution.py:253
  22.9 0.0 collective-permute-done.4.refs_3_
  22.9 0.1 collective-permute-start.8
  23.0 0.0 collective-permute-done.2.refs_1_
  23.0 0.6 %shard_map.69 = (f32[520,256]{1,0:T(8,128)S(1)}, bf16[272,256]{1,0:T(8,128)(2,1)S(1)}) custom-call(bf16[288,256]{1,0:T(8,128)(2,1)S(1)} %collective-permute-done.1.refs_0_, bf16[288,256]{1,0:T(8,128)(2,1)S(1)} %collective-permute-done.2.refs_1_, bf16[288,256]{1,0:T(8,128)(2,1)S(1)} %collective-permute-done.3.refs_2_.refs_3_, ...), custom_call_target="tpu_custom_call" | custom-call | flops 268435456 | bytes 1261568 | tf_op jit(solution)/shard_map/pallas_call | solution.py:225
  23.6 0.0 collective-permute-done.9.refs_3_
  23.6 3.6 %collective-permute-done.7.refs_1_.refs_2_.refs_3_ = bf16[272,256]{1,0:T(8,128)(2,1)S(1)} collective-permute-done((bf16[272,256]{1,0:T(8,128)(2,1)S(1)}, bf16[272,256]{1,0:T(8,128)(2,1)S(1)}, u32[]{:S(2)}, u32[]{:S(2)}) %collective-permute-start.7) | collective-permute-done | bytes 139296 | tf_op jit(solution)/shard_map/ppermute | solution.py:253
  27.2 0.0 collective-permute-done.10.refs_4_
  27.2 0.7 %collective-permute-done.8.refs_2_.refs_3_.refs_4_ = bf16[272,256]{1,0:T(8,128)(2,1)S(1)} collective-permute-done((bf16[272,256]{1,0:T(8,128)(2,1)S(1)}, bf16[272,256]{1,0:T(8,128)(2,1)S(1)}, u32[]{:S(2)}, u32[]{:S(2)}) %collective-permute-start.8) | collective-permute-done | bytes 139296 | tf_op jit(solution)/shard_map/ppermute | solution.py:253
  27.9 0.6 %shard_map.71 = (f32[520,256]{1,0:T(8,128)S(1)}, bf16[272,256]{1,0:T(8,128)(2,1)S(1)}) custom-call(f32[520,256]{1,0:T(8,128)S(1)} %get-tuple-element.16.refs_0_, bf16[272,256]{1,0:T(8,128)(2,1)S(1)} %collective-permute-done.7.refs_1_.refs_2_.refs_3_, bf16[272,256]{1,0:T(8,128)(2,1)S(1)} %collective-permute-done.8.refs_2_.refs_3_.refs_4_, ...), custom_call_target="tpu_custom_call" | custom-call | flops 268435456 | bytes 1761280 | tf_op jit(solution)/shard_map/pallas_call | solution.py:225
  28.6 0.1 collective-permute-start.11
  28.6 0.5 %collective-permute-start.12 = (bf16[272,256]{1,0:T(8,128)(2,1)S(1)}, bf16[272,256]{1,0:T(8,128)(2,1)S(1)}, u32[]{:S(2)}, u32[]{:S(2)}) collective-permute-start(bf16[272,256]{1,0:T(8,128)(2,1)S(1)} %get-tuple-element.20), channel_id=1, source_target_pairs={{0,1},{1,0},{2,3},{3,2},{4,5},{5,4},{6,7},{7,6},{8,9},{9,8},{10,11... | collective-permute-start | bytes 417800 | tf_op jit(solution)/shard_map/ppermute | solution.py:244
  29.1 0.0 copy-start
  29.1 0.1 collective-permute-start.13
  29.2 0.2 shard_map.72.hots
  29.4 1.3 %collective-permute-done.12.refs_2_ = bf16[272,256]{1,0:T(8,128)(2,1)S(1)} collective-permute-done((bf16[272,256]{1,0:T(8,128)(2,1)S(1)}, bf16[272,256]{1,0:T(8,128)(2,1)S(1)}, u32[]{:S(2)}, u32[]{:S(2)}) %collective-permute-start.12) | collective-permute-done | bytes 139296 | tf_op jit(solution)/shard_map/ppermute | solution.py:244
  30.7 0.2 collective-permute-done.13.refs_5_
  30.9 0.0 collective-permute-done.11.other
  30.9 0.0 copy-done
  30.9 1.5 %shard_map.73 = (bf16[512,256]{1,0:T(8,128)(2,1)}, bf16[1024,256]{1,0:T(8,128)(2,1)}, f32[8,128]{1,0:T(8,128)}) custom-call(f32[520,256]{1,0:T(8,128)S(1)} %get-tuple-element.19.mine, f32[520,256]{1,0:T(8,128)S(1)} %collective-permute-done.11.other, bf16[512,256]{1,0:T(8,128)(2,1)S(1)} %copy-done, bf16[512,512]{1,0:T(8,128)(2,1)S(1)} %shard_map.72.hots, ...), custom_call_target="tpu_custom_call" | custom-call | flops 268435456 | bytes 3493888 | tf_op jit(solution)/shard_map/pallas_call | solution.py:225
  (1 shorter events, 0.0 us)
Async XLA Ops:
  1.5 0.7 %copy-start.2 = (s32[256]{0:T(256)S(1)}, s32[256]{0:T(256)}, u32[]{:S(2)}) copy-start(s32[256]{0:T(256)} %param.5) | copy-start | bytes 3076
  2.2 4.2 %copy-start.1 = (s32[4096]{0:T(1024)S(1)}, s32[4096]{0:T(1024)}, u32[]{:S(2)}) copy-start(s32[4096]{0:T(1024)} %param.6) | copy-start | bytes 49156
  2.2 4.2 %collective-permute-start = (bf16[272,256]{1,0:T(8,128)(2,1)S(1)}, bf16[272,256]{1,0:T(8,128)(2,1)S(1)}, u32[]{:S(2)}, u32[]{:S(2)}) collective-permute-start(bf16[272,256]{1,0:T(8,128)(2,1)S(1)} %shard_map.67.refs_0_), channel_id=1, source_target_pairs={{0,1},{1,0},{2,3},{3,2},{4,5},{5,4},{6,7},{7,6},{8,9},{9,8},{10,11... | collective-permute-start | bytes 417800 | tf_op jit(solution)/shard_map/ppermute | solution.py:244
  2.8 11.0 %collective-permute-start.5 = (bf16[272,256]{1,0:T(8,128)(2,1)S(1)}, bf16[272,256]{1,0:T(8,128)(2,1)S(1)}, u32[]{:S(2)}, u32[]{:S(2)}) collective-permute-start(bf16[272,256]{1,0:T(8,128)(2,1)S(1)} %shard_map.67.refs_0_), channel_id=1, source_target_pairs={{0,16},{1,17},{2,18},{3,19},{4,20},{5,21},{6,22},{7,23},{8,24},{9,... | collective-permute-start | bytes 417800 | tf_op jit(solution)/shard_map/ppermute | solution.py:244
  7.1 8.0 %collective-permute-start.3 = (bf16[288,256]{1,0:T(8,128)(2,1)S(1)}, bf16[288,256]{1,0:T(8,128)(2,1)S(1)}, u32[]{:S(2)}, u32[]{:S(2)}) collective-permute-start(bf16[288,256]{1,0:T(8,128)(2,1)S(1)} %get-tuple-element.14), channel_id=1, source_target_pairs={{0,6},{1,3},{2,4},{3,1},{4,2},{5,7},{6,0},{7,5},{8,14},{9,11},{10,... | collective-permute-start | bytes 442376 | tf_op jit(solution)/shard_map/ppermute | solution.py:253
  9.6 11.2 %collective-permute-start.1 = (bf16[288,256]{1,0:T(8,128)(2,1)S(1)}, bf16[288,256]{1,0:T(8,128)(2,1)S(1)}, u32[]{:S(2)}, u32[]{:S(2)}) collective-permute-start(bf16[288,256]{1,0:T(8,128)(2,1)S(1)} %get-tuple-element.14), channel_id=1, source_target_pairs={{0,4},{1,1},{2,6},{3,3},{4,0},{5,5},{6,2},{7,7},{8,12},{9,9},{10,1... | collective-permute-start | bytes 442376 | tf_op jit(solution)/shard_map/ppermute | solution.py:253
  12.0 10.9 %collective-permute-start.4 = (bf16[288,256]{1,0:T(8,128)(2,1)S(1)}, bf16[288,256]{1,0:T(8,128)(2,1)S(1)}, u32[]{:S(2)}, u32[]{:S(2)}) collective-permute-start(bf16[288,256]{1,0:T(8,128)(2,1)S(1)} %get-tuple-element.15), channel_id=1, source_target_pairs={{0,10},{1,15},{2,8},{3,13},{4,14},{5,11},{6,12},{7,9},{8,2},{9,7},... | collective-permute-start | bytes 442376 | tf_op jit(solution)/shard_map/ppermute | solution.py:253
  13.8 1.4 %collective-permute-start.6 = (bf16[272,256]{1,0:T(8,128)(2,1)S(1)}, bf16[272,256]{1,0:T(8,128)(2,1)S(1)}, u32[]{:S(2)}, u32[]{:S(2)}) collective-permute-start(bf16[272,256]{1,0:T(8,128)(2,1)S(1)} %collective-permute-done.5.refs_0_), channel_id=1, source_target_pairs={{0,1},{1,0},{2,3},{3,2},{4,5},{5,4},{6,7},{7,6},{8,9},{9,8},{10,11... | collective-permute-start | bytes 417800 | tf_op jit(solution)/shard_map/ppermute | solution.py:244
  13.8 9.2 %collective-permute-start.2 = (bf16[288,256]{1,0:T(8,128)(2,1)S(1)}, bf16[288,256]{1,0:T(8,128)(2,1)S(1)}, u32[]{:S(2)}, u32[]{:S(2)}) collective-permute-start(bf16[288,256]{1,0:T(8,128)(2,1)S(1)} %get-tuple-element.15), channel_id=1, source_target_pairs={{0,8},{1,13},{2,10},{3,15},{4,12},{5,9},{6,14},{7,11},{8,0},{9,5},... | collective-permute-start | bytes 442376 | tf_op jit(solution)/shard_map/ppermute | solution.py:253
  15.8 7.8 %collective-permute-start.9 = (bf16[272,256]{1,0:T(8,128)(2,1)S(1)}, bf16[272,256]{1,0:T(8,128)(2,1)S(1)}, u32[]{:S(2)}, u32[]{:S(2)}) collective-permute-start(bf16[272,256]{1,0:T(8,128)(2,1)S(1)} %get-tuple-element.17), channel_id=1, source_target_pairs={{0,6},{1,3},{2,4},{3,1},{4,2},{5,7},{6,0},{7,5},{8,14},{9,11},{10,... | collective-permute-start | bytes 417800 | tf_op jit(solution)/shard_map/ppermute | solution.py:253
  18.4 8.8 %collective-permute-start.7 = (bf16[272,256]{1,0:T(8,128)(2,1)S(1)}, bf16[272,256]{1,0:T(8,128)(2,1)S(1)}, u32[]{:S(2)}, u32[]{:S(2)}) collective-permute-start(bf16[272,256]{1,0:T(8,128)(2,1)S(1)} %get-tuple-element.17), channel_id=1, source_target_pairs={{0,4},{1,1},{2,6},{3,3},{4,0},{5,5},{6,2},{7,7},{8,12},{9,9},{10,1... | collective-permute-start | bytes 417800 | tf_op jit(solution)/shard_map/ppermute | solution.py:253
  20.8 6.4 %collective-permute-start.10 = (bf16[272,256]{1,0:T(8,128)(2,1)S(1)}, bf16[272,256]{1,0:T(8,128)(2,1)S(1)}, u32[]{:S(2)}, u32[]{:S(2)}) collective-permute-start(bf16[272,256]{1,0:T(8,128)(2,1)S(1)} %get-tuple-element.18), channel_id=1, source_target_pairs={{0,10},{1,15},{2,8},{3,13},{4,14},{5,11},{6,12},{7,9},{8,2},{9,7},... | collective-permute-start | bytes 417800 | tf_op jit(solution)/shard_map/ppermute | solution.py:253
  22.9 5.1 %collective-permute-start.8 = (bf16[272,256]{1,0:T(8,128)(2,1)S(1)}, bf16[272,256]{1,0:T(8,128)(2,1)S(1)}, u32[]{:S(2)}, u32[]{:S(2)}) collective-permute-start(bf16[272,256]{1,0:T(8,128)(2,1)S(1)} %get-tuple-element.18), channel_id=1, source_target_pairs={{0,8},{1,13},{2,10},{3,15},{4,12},{5,9},{6,14},{7,11},{8,0},{9,5},... | collective-permute-start | bytes 417800 | tf_op jit(solution)/shard_map/ppermute | solution.py:253
  28.6 2.4 %collective-permute-start.11 = (f32[520,256]{1,0:T(8,128)S(1)}, f32[520,256]{1,0:T(8,128)S(1)}, u32[]{:S(2)}, u32[]{:S(2)}) collective-permute-start(f32[520,256]{1,0:T(8,128)S(1)} %get-tuple-element.19.mine), channel_id=1, source_target_pairs={{0,1},{1,0},{2,3},{3,2},{4,5},{5,4},{6,7},{7,6},{8,9},{9,8},{10,11... | collective-permute-start | bytes 1597448 | tf_op jit(solution)/shard_map/ppermute | solution.py:244
  28.6 2.1 %collective-permute-start.12 = (bf16[272,256]{1,0:T(8,128)(2,1)S(1)}, bf16[272,256]{1,0:T(8,128)(2,1)S(1)}, u32[]{:S(2)}, u32[]{:S(2)}) collective-permute-start(bf16[272,256]{1,0:T(8,128)(2,1)S(1)} %get-tuple-element.20), channel_id=1, source_target_pairs={{0,1},{1,0},{2,3},{3,2},{4,5},{5,4},{6,7},{7,6},{8,9},{9,8},{10,11... | collective-permute-start | bytes 417800 | tf_op jit(solution)/shard_map/ppermute | solution.py:244
  29.1 1.8 %copy-start = (bf16[512,256]{1,0:T(8,128)(2,1)S(1)}, bf16[512,256]{1,0:T(8,128)(2,1)}, u32[]{:S(2)}) copy-start(bf16[512,256]{1,0:T(8,128)(2,1)} %old.1) | copy-start | bytes 786436
  29.1 1.8 %collective-permute-start.13 = (bf16[272,256]{1,0:T(8,128)(2,1)S(1)}, bf16[272,256]{1,0:T(8,128)(2,1)S(1)}, u32[]{:S(2)}, u32[]{:S(2)}) collective-permute-start(bf16[272,256]{1,0:T(8,128)(2,1)S(1)} %get-tuple-element.21), channel_id=1, source_target_pairs={{0,1},{1,0},{2,3},{3,2},{4,5},{5,4},{6,7},{7,6},{8,9},{9,8},{10,11... | collective-permute-start | bytes 417800 | tf_op jit(solution)/shard_map/ppermute | solution.py:244

commit v6 on v5

--- a/solution.py
+++ b/solution.py
@@ -103,9 +103,8 @@
         capacity = rows0.shape[0]
         out[0:capacity, :] = rows0
         out[capacity : 2 * capacity, :] = rows1
-        out[2 * capacity : 2 * capacity + HEAD, :] = jnp.where(
-            _iota((HEAD, line0.shape[1]), 0) == 0, line0, line1
-        ).astype(jnp.bfloat16)
+        first_line = _iota((out.shape[0] - 2 * capacity, line0.shape[1]), 0) == 0
+        out[2 * capacity :, :] = jnp.where(first_line, line0, line1).astype(jnp.bfloat16)
 
 
 def _labels(line):

time: 32.7 us -> 32.7 us (level)
  no operation moved by 1% of the time
where the time goes in v6:
time: 32.7 us; the launch traced here: 32.5 us
  starting transfers between devices  19.3 us (59%)
  waiting for transfers between devices  6.6 us (20%)
  Pallas kernels  4.25 us (13%)
  local copies, waits for them, and re-layouts  1.6 us (5%)
  between operations  0.73 us (2%)
    ppermute x8, starting transfers between devices, spread(): lax.ppermute(a, ('items', 'rep'), [(i, i ^ swap[i & 1]) for i in range(pe...  14.5 us
    ppermute x6, starting transfers between devices, hop(): lax.ppermute(a, ('items', 'rep'), [(i, i ^ swap) for i in range(peers * r...  4.83 us
    ppermute x8, waiting for transfers between devices, spread(): lax.ppermute(a, ('items', 'rep'), [(i, i ^ swap[i & 1]) for i in range(pe...  4.32 us
    pallas_call x7, Pallas kernels, _call(): pl.pallas_call(kernel, out_shape=outs, in_specs=[VMEM] * len(args), out_s...  4.25 us
    ppermute x6, waiting for transfers between devices, hop(): lax.ppermute(a, ('items', 'rep'), [(i, i ^ swap) for i in range(peers * r...  2.28 us
    pad x1, local copies, waits for them, and re-layouts, per_device_eight(): payload = lax.optimization_barrier(jnp.pad(embeds, ((0, HEAD), (0, 0))))  0.92 us
    unnamed x6, local copies, waits for them, and re-layouts  0.68 us
  transfers between devices with their start and end apart: 14, of which 6 were waited for; matrix products, arithmetic and copies ran while one was open for 0% of the time, Pallas kernels for 6%

profile of v6, /device:TPU:0, one launch (start us, length us, event | category | flops | bytes accessed | tf_op | source)
XLA Modules:
  0.0 32.5 jit_solution(4253533603014679951)
XLA Ops:
  0.6 0.9 %pad.4._ = bf16[272,256]{1,0:T(8,128)(2,1)S(1)} pad(bf16[256,256]{1,0:T(8,128)(2,1)} %param.4, bf16[]{:T(256)} %constant.2.clone.1), padding=0_16x0_0 | pad | bytes 270338 | tf_op jit(solution)/shard_map/jit(_pad)/pad | solution.py:266
  1.5 0.0 copy-start.2
  1.6 0.7 %copy-done.2 = s32[256]{0:T(256)S(1)} copy-done((s32[256]{0:T(256)S(1)}, s32[256]{0:T(256)}, u32[]{:S(2)}) %copy-start.2) | copy-done | bytes 1048
  2.2 0.0 copy-start.1
  2.2 0.5 %collective-permute-start = (bf16[272,256]{1,0:T(8,128)(2,1)S(1)}, bf16[272,256]{1,0:T(8,128)(2,1)S(1)}, u32[]{:S(2)}, u32[]{:S(2)}) collective-permute-start(bf16[272,256]{1,0:T(8,128)(2,1)S(1)} %shard_map.67.refs_0_), channel_id=1, source_target_pairs={{0,1},{1,0},{2,3},{3,2},{4,5},{5,4},{6,7},{7,6},{8,9},{9,8},{10,11... | collective-permute-start | bytes 417800 | tf_op jit(solution)/shard_map/ppermute | solution.py:243
  2.8 3.7 %collective-permute-start.5 = (bf16[272,256]{1,0:T(8,128)(2,1)S(1)}, bf16[272,256]{1,0:T(8,128)(2,1)S(1)}, u32[]{:S(2)}, u32[]{:S(2)}) collective-permute-start(bf16[272,256]{1,0:T(8,128)(2,1)S(1)} %shard_map.67.refs_0_), channel_id=1, source_target_pairs={{0,16},{1,17},{2,18},{3,19},{4,20},{5,21},{6,22},{7,23},{8,24},{9,... | collective-permute-start | bytes 417800 | tf_op jit(solution)/shard_map/ppermute | solution.py:243
  6.4 0.0 collective-permute-done.refs_1_
  6.4 0.0 copy-done.1
  6.4 0.7 %shard_map.68 = (bf16[288,256]{1,0:T(8,128)(2,1)S(1)}, bf16[288,256]{1,0:T(8,128)(2,1)S(1)}) custom-call(bf16[272,256]{1,0:T(8,128)(2,1)S(1)} %shard_map.67.refs_0_, bf16[272,256]{1,0:T(8,128)(2,1)S(1)} %collective-permute-done.refs_1_, s32[32,128]{1,0:T(8,128)S(1)} %bitcast.4), custom_call_target="tpu_custom_call" | custom-call | flops 67108864 | bytes 589824 | tf_op jit(solution)/shard_map/pallas_call | solution.py:224
  7.1 2.5 %collective-permute-start.3 = (bf16[288,256]{1,0:T(8,128)(2,1)S(1)}, bf16[288,256]{1,0:T(8,128)(2,1)S(1)}, u32[]{:S(2)}, u32[]{:S(2)}) collective-permute-start(bf16[288,256]{1,0:T(8,128)(2,1)S(1)} %get-tuple-element.14), channel_id=1, source_target_pairs={{0,6},{1,3},{2,4},{3,1},{4,2},{5,7},{6,0},{7,5},{8,14},{9,11},{10,... | collective-permute-start | bytes 442376 | tf_op jit(solution)/shard_map/ppermute | solution.py:252
  9.6 2.4 %collective-permute-start.1 = (bf16[288,256]{1,0:T(8,128)(2,1)S(1)}, bf16[288,256]{1,0:T(8,128)(2,1)S(1)}, u32[]{:S(2)}, u32[]{:S(2)}) collective-permute-start(bf16[288,256]{1,0:T(8,128)(2,1)S(1)} %get-tuple-element.14), channel_id=1, source_target_pairs={{0,4},{1,1},{2,6},{3,3},{4,0},{5,5},{6,2},{7,7},{8,12},{9,9},{10,1... | collective-permute-start | bytes 442376 | tf_op jit(solution)/shard_map/ppermute | solution.py:252
  12.0 1.6 %collective-permute-start.4 = (bf16[288,256]{1,0:T(8,128)(2,1)S(1)}, bf16[288,256]{1,0:T(8,128)(2,1)S(1)}, u32[]{:S(2)}, u32[]{:S(2)}) collective-permute-start(bf16[288,256]{1,0:T(8,128)(2,1)S(1)} %get-tuple-element.15), channel_id=1, source_target_pairs={{0,10},{1,15},{2,8},{3,13},{4,14},{5,11},{6,12},{7,9},{8,2},{9,7},... | collective-permute-start | bytes 442376 | tf_op jit(solution)/shard_map/ppermute | solution.py:252
  13.6 0.1 collective-permute-done.5.refs_0_
  13.8 0.0 collective-permute-start.6
  13.8 0.8 %collective-permute-start.2 = (bf16[288,256]{1,0:T(8,128)(2,1)S(1)}, bf16[288,256]{1,0:T(8,128)(2,1)S(1)}, u32[]{:S(2)}, u32[]{:S(2)}) collective-permute-start(bf16[288,256]{1,0:T(8,128)(2,1)S(1)} %get-tuple-element.15), channel_id=1, source_target_pairs={{0,8},{1,13},{2,10},{3,15},{4,12},{5,9},{6,14},{7,11},{8,0},{9,5},... | collective-permute-start | bytes 442376 | tf_op jit(solution)/shard_map/ppermute | solution.py:252
  14.5 0.6 %collective-permute-done.6.refs_1_ = bf16[272,256]{1,0:T(8,128)(2,1)S(1)} collective-permute-done((bf16[272,256]{1,0:T(8,128)(2,1)S(1)}, bf16[272,256]{1,0:T(8,128)(2,1)S(1)}, u32[]{:S(2)}, u32[]{:S(2)}) %collective-permute-start.6) | collective-permute-done | bytes 139296 | tf_op jit(solution)/shard_map/ppermute | solution.py:243
  15.1 0.0 collective-permute-done.3.refs_2_.refs_3_
  15.1 0.7 %shard_map.70 = (bf16[272,256]{1,0:T(8,128)(2,1)S(1)}, bf16[272,256]{1,0:T(8,128)(2,1)S(1)}) custom-call(bf16[272,256]{1,0:T(8,128)(2,1)S(1)} %collective-permute-done.5.refs_0_, bf16[272,256]{1,0:T(8,128)(2,1)S(1)} %collective-permute-done.6.refs_1_, s32[32,128]{1,0:T(8,128)S(1)} %bitcast.5, bf16[288,256]{1,0:T(8,128)(2,1)S(1)} %collective-permute-done.3.refs_2_.refs_3_), custom_call_target="tpu_custom_call" | custom-call | flops 67108864 | bytes 720896 | tf_op jit(solution)/shard_map/pallas_call | solution.py:224
  15.8 2.6 %collective-permute-start.9 = (bf16[272,256]{1,0:T(8,128)(2,1)S(1)}, bf16[272,256]{1,0:T(8,128)(2,1)S(1)}, u32[]{:S(2)}, u32[]{:S(2)}) collective-permute-start(bf16[272,256]{1,0:T(8,128)(2,1)S(1)} %get-tuple-element.17), channel_id=1, source_target_pairs={{0,6},{1,3},{2,4},{3,1},{4,2},{5,7},{6,0},{7,5},{8,14},{9,11},{10,... | collective-permute-start | bytes 417800 | tf_op jit(solution)/shard_map/ppermute | solution.py:252
  18.4 2.4 %collective-permute-start.7 = (bf16[272,256]{1,0:T(8,128)(2,1)S(1)}, bf16[272,256]{1,0:T(8,128)(2,1)S(1)}, u32[]{:S(2)}, u32[]{:S(2)}) collective-permute-start(bf16[272,256]{1,0:T(8,128)(2,1)S(1)} %get-tuple-element.17), channel_id=1, source_target_pairs={{0,4},{1,1},{2,6},{3,3},{4,0},{5,5},{6,2},{7,7},{8,12},{9,9},{10,1... | collective-permute-start | bytes 417800 | tf_op jit(solution)/shard_map/ppermute | solution.py:252
  20.8 0.0 collective-permute-done.1.refs_0_
  20.8 2.1 %collective-permute-start.10 = (bf16[272,256]{1,0:T(8,128)(2,1)S(1)}, bf16[272,256]{1,0:T(8,128)(2,1)S(1)}, u32[]{:S(2)}, u32[]{:S(2)}) collective-permute-start(bf16[272,256]{1,0:T(8,128)(2,1)S(1)} %get-tuple-element.18), channel_id=1, source_target_pairs={{0,10},{1,15},{2,8},{3,13},{4,14},{5,11},{6,12},{7,9},{8,2},{9,7},... | collective-permute-start | bytes 417800 | tf_op jit(solution)/shard_map/ppermute | solution.py:252
  22.9 0.0 collective-permute-done.4.refs_3_
  22.9 0.1 collective-permute-start.8
  23.0 0.0 collective-permute-done.2.refs_1_
  23.0 0.6 %shard_map.69 = (f32[520,256]{1,0:T(8,128)S(1)}, bf16[272,256]{1,0:T(8,128)(2,1)S(1)}) custom-call(bf16[288,256]{1,0:T(8,128)(2,1)S(1)} %collective-permute-done.1.refs_0_, bf16[288,256]{1,0:T(8,128)(2,1)S(1)} %collective-permute-done.2.refs_1_, bf16[288,256]{1,0:T(8,128)(2,1)S(1)} %collective-permute-done.3.refs_2_.refs_3_, ...), custom_call_target="tpu_custom_call" | custom-call | flops 268435456 | bytes 1261568 | tf_op jit(solution)/shard_map/pallas_call | solution.py:224
  23.6 0.0 collective-permute-done.9.refs_3_
  23.6 3.6 %collective-permute-done.7.refs_1_.refs_2_.refs_3_ = bf16[272,256]{1,0:T(8,128)(2,1)S(1)} collective-permute-done((bf16[272,256]{1,0:T(8,128)(2,1)S(1)}, bf16[272,256]{1,0:T(8,128)(2,1)S(1)}, u32[]{:S(2)}, u32[]{:S(2)}) %collective-permute-start.7) | collective-permute-done | bytes 139296 | tf_op jit(solution)/shard_map/ppermute | solution.py:252
  27.2 0.0 collective-permute-done.10.refs_4_
  27.2 0.7 %collective-permute-done.8.refs_2_.refs_3_.refs_4_ = bf16[272,256]{1,0:T(8,128)(2,1)S(1)} collective-permute-done((bf16[272,256]{1,0:T(8,128)(2,1)S(1)}, bf16[272,256]{1,0:T(8,128)(2,1)S(1)}, u32[]{:S(2)}, u32[]{:S(2)}) %collective-permute-start.8) | collective-permute-done | bytes 139296 | tf_op jit(solution)/shard_map/ppermute | solution.py:252
  27.9 0.6 %shard_map.71 = (f32[520,256]{1,0:T(8,128)S(1)}, bf16[272,256]{1,0:T(8,128)(2,1)S(1)}) custom-call(f32[520,256]{1,0:T(8,128)S(1)} %get-tuple-element.16.refs_0_, bf16[272,256]{1,0:T(8,128)(2,1)S(1)} %collective-permute-done.7.refs_1_.refs_2_.refs_3_, bf16[272,256]{1,0:T(8,128)(2,1)S(1)} %collective-permute-done.8.refs_2_.refs_3_.refs_4_, ...), custom_call_target="tpu_custom_call" | custom-call | flops 268435456 | bytes 1761280 | tf_op jit(solution)/shard_map/pallas_call | solution.py:224
  28.6 0.1 collective-permute-start.11
  28.6 0.5 %collective-permute-start.12 = (bf16[272,256]{1,0:T(8,128)(2,1)S(1)}, bf16[272,256]{1,0:T(8,128)(2,1)S(1)}, u32[]{:S(2)}, u32[]{:S(2)}) collective-permute-start(bf16[272,256]{1,0:T(8,128)(2,1)S(1)} %get-tuple-element.20), channel_id=1, source_target_pairs={{0,1},{1,0},{2,3},{3,2},{4,5},{5,4},{6,7},{7,6},{8,9},{9,8},{10,11... | collective-permute-start | bytes 417800 | tf_op jit(solution)/shard_map/ppermute | solution.py:243
  29.1 0.0 copy-start
  29.1 0.1 collective-permute-start.13
  29.2 0.2 shard_map.72.hots
  29.4 1.3 %collective-permute-done.12.refs_2_ = bf16[272,256]{1,0:T(8,128)(2,1)S(1)} collective-permute-done((bf16[272,256]{1,0:T(8,128)(2,1)S(1)}, bf16[272,256]{1,0:T(8,128)(2,1)S(1)}, u32[]{:S(2)}, u32[]{:S(2)}) %collective-permute-start.12) | collective-permute-done | bytes 139296 | tf_op jit(solution)/shard_map/ppermute | solution.py:243
  30.7 0.2 collective-permute-done.13.refs_5_
  30.9 0.0 collective-permute-done.11.other
  30.9 0.0 copy-done
  30.9 1.5 %shard_map.73 = (bf16[512,256]{1,0:T(8,128)(2,1)}, bf16[1024,256]{1,0:T(8,128)(2,1)}, f32[8,128]{1,0:T(8,128)}) custom-call(f32[520,256]{1,0:T(8,128)S(1)} %get-tuple-element.19.mine, f32[520,256]{1,0:T(8,128)S(1)} %collective-permute-done.11.other, bf16[512,256]{1,0:T(8,128)(2,1)S(1)} %copy-done, bf16[512,512]{1,0:T(8,128)(2,1)S(1)} %shard_map.72.hots, ...), custom_call_target="tpu_custom_call" | custom-call | flops 268435456 | bytes 3493888 | tf_op jit(solution)/shard_map/pallas_call | solution.py:224
  (1 shorter events, 0.0 us)
Async XLA Ops:
  1.5 0.7 %copy-start.2 = (s32[256]{0:T(256)S(1)}, s32[256]{0:T(256)}, u32[]{:S(2)}) copy-start(s32[256]{0:T(256)} %param.5) | copy-start | bytes 3076
  2.2 4.2 %copy-start.1 = (s32[4096]{0:T(1024)S(1)}, s32[4096]{0:T(1024)}, u32[]{:S(2)}) copy-start(s32[4096]{0:T(1024)} %param.6) | copy-start | bytes 49156
  2.2 4.2 %collective-permute-start = (bf16[272,256]{1,0:T(8,128)(2,1)S(1)}, bf16[272,256]{1,0:T(8,128)(2,1)S(1)}, u32[]{:S(2)}, u32[]{:S(2)}) collective-permute-start(bf16[272,256]{1,0:T(8,128)(2,1)S(1)} %shard_map.67.refs_0_), channel_id=1, source_target_pairs={{0,1},{1,0},{2,3},{3,2},{4,5},{5,4},{6,7},{7,6},{8,9},{9,8},{10,11... | collective-permute-start | bytes 417800 | tf_op jit(solution)/shard_map/ppermute | solution.py:243
  2.8 11.0 %collective-permute-start.5 = (bf16[272,256]{1,0:T(8,128)(2,1)S(1)}, bf16[272,256]{1,0:T(8,128)(2,1)S(1)}, u32[]{:S(2)}, u32[]{:S(2)}) collective-permute-start(bf16[272,256]{1,0:T(8,128)(2,1)S(1)} %shard_map.67.refs_0_), channel_id=1, source_target_pairs={{0,16},{1,17},{2,18},{3,19},{4,20},{5,21},{6,22},{7,23},{8,24},{9,... | collective-permute-start | bytes 417800 | tf_op jit(solution)/shard_map/ppermute | solution.py:243
  7.1 8.0 %collective-permute-start.3 = (bf16[288,256]{1,0:T(8,128)(2,1)S(1)}, bf16[288,256]{1,0:T(8,128)(2,1)S(1)}, u32[]{:S(2)}, u32[]{:S(2)}) collective-permute-start(bf16[288,256]{1,0:T(8,128)(2,1)S(1)} %get-tuple-element.14), channel_id=1, source_target_pairs={{0,6},{1,3},{2,4},{3,1},{4,2},{5,7},{6,0},{7,5},{8,14},{9,11},{10,... | collective-permute-start | bytes 442376 | tf_op jit(solution)/shard_map/ppermute | solution.py:252
  9.6 11.2 %collective-permute-start.1 = (bf16[288,256]{1,0:T(8,128)(2,1)S(1)}, bf16[288,256]{1,0:T(8,128)(2,1)S(1)}, u32[]{:S(2)}, u32[]{:S(2)}) collective-permute-start(bf16[288,256]{1,0:T(8,128)(2,1)S(1)} %get-tuple-element.14), channel_id=1, source_target_pairs={{0,4},{1,1},{2,6},{3,3},{4,0},{5,5},{6,2},{7,7},{8,12},{9,9},{10,1... | collective-permute-start | bytes 442376 | tf_op jit(solution)/shard_map/ppermute | solution.py:252
  12.0 10.9 %collective-permute-start.4 = (bf16[288,256]{1,0:T(8,128)(2,1)S(1)}, bf16[288,256]{1,0:T(8,128)(2,1)S(1)}, u32[]{:S(2)}, u32[]{:S(2)}) collective-permute-start(bf16[288,256]{1,0:T(8,128)(2,1)S(1)} %get-tuple-element.15), channel_id=1, source_target_pairs={{0,10},{1,15},{2,8},{3,13},{4,14},{5,11},{6,12},{7,9},{8,2},{9,7},... | collective-permute-start | bytes 442376 | tf_op jit(solution)/shard_map/ppermute | solution.py:252
  13.8 1.4 %collective-permute-start.6 = (bf16[272,256]{1,0:T(8,128)(2,1)S(1)}, bf16[272,256]{1,0:T(8,128)(2,1)S(1)}, u32[]{:S(2)}, u32[]{:S(2)}) collective-permute-start(bf16[272,256]{1,0:T(8,128)(2,1)S(1)} %collective-permute-done.5.refs_0_), channel_id=1, source_target_pairs={{0,1},{1,0},{2,3},{3,2},{4,5},{5,4},{6,7},{7,6},{8,9},{9,8},{10,11... | collective-permute-start | bytes 417800 | tf_op jit(solution)/shard_map/ppermute | solution.py:243
  13.8 9.2 %collective-permute-start.2 = (bf16[288,256]{1,0:T(8,128)(2,1)S(1)}, bf16[288,256]{1,0:T(8,128)(2,1)S(1)}, u32[]{:S(2)}, u32[]{:S(2)}) collective-permute-start(bf16[288,256]{1,0:T(8,128)(2,1)S(1)} %get-tuple-element.15), channel_id=1, source_target_pairs={{0,8},{1,13},{2,10},{3,15},{4,12},{5,9},{6,14},{7,11},{8,0},{9,5},... | collective-permute-start | bytes 442376 | tf_op jit(solution)/shard_map/ppermute | solution.py:252
  15.8 7.8 %collective-permute-start.9 = (bf16[272,256]{1,0:T(8,128)(2,1)S(1)}, bf16[272,256]{1,0:T(8,128)(2,1)S(1)}, u32[]{:S(2)}, u32[]{:S(2)}) collective-permute-start(bf16[272,256]{1,0:T(8,128)(2,1)S(1)} %get-tuple-element.17), channel_id=1, source_target_pairs={{0,6},{1,3},{2,4},{3,1},{4,2},{5,7},{6,0},{7,5},{8,14},{9,11},{10,... | collective-permute-start | bytes 417800 | tf_op jit(solution)/shard_map/ppermute | solution.py:252
  18.4 8.8 %collective-permute-start.7 = (bf16[272,256]{1,0:T(8,128)(2,1)S(1)}, bf16[272,256]{1,0:T(8,128)(2,1)S(1)}, u32[]{:S(2)}, u32[]{:S(2)}) collective-permute-start(bf16[272,256]{1,0:T(8,128)(2,1)S(1)} %get-tuple-element.17), channel_id=1, source_target_pairs={{0,4},{1,1},{2,6},{3,3},{4,0},{5,5},{6,2},{7,7},{8,12},{9,9},{10,1... | collective-permute-start | bytes 417800 | tf_op jit(solution)/shard_map/ppermute | solution.py:252
  20.8 6.4 %collective-permute-start.10 = (bf16[272,256]{1,0:T(8,128)(2,1)S(1)}, bf16[272,256]{1,0:T(8,128)(2,1)S(1)}, u32[]{:S(2)}, u32[]{:S(2)}) collective-permute-start(bf16[272,256]{1,0:T(8,128)(2,1)S(1)} %get-tuple-element.18), channel_id=1, source_target_pairs={{0,10},{1,15},{2,8},{3,13},{4,14},{5,11},{6,12},{7,9},{8,2},{9,7},... | collective-permute-start | bytes 417800 | tf_op jit(solution)/shard_map/ppermute | solution.py:252
  22.9 5.1 %collective-permute-start.8 = (bf16[272,256]{1,0:T(8,128)(2,1)S(1)}, bf16[272,256]{1,0:T(8,128)(2,1)S(1)}, u32[]{:S(2)}, u32[]{:S(2)}) collective-permute-start(bf16[272,256]{1,0:T(8,128)(2,1)S(1)} %get-tuple-element.18), channel_id=1, source_target_pairs={{0,8},{1,13},{2,10},{3,15},{4,12},{5,9},{6,14},{7,11},{8,0},{9,5},... | collective-permute-start | bytes 417800 | tf_op jit(solution)/shard_map/ppermute | solution.py:252
  28.6 2.4 %collective-permute-start.11 = (f32[520,256]{1,0:T(8,128)S(1)}, f32[520,256]{1,0:T(8,128)S(1)}, u32[]{:S(2)}, u32[]{:S(2)}) collective-permute-start(f32[520,256]{1,0:T(8,128)S(1)} %get-tuple-element.19.mine), channel_id=1, source_target_pairs={{0,1},{1,0},{2,3},{3,2},{4,5},{5,4},{6,7},{7,6},{8,9},{9,8},{10,11... | collective-permute-start | bytes 1597448 | tf_op jit(solution)/shard_map/ppermute | solution.py:243
  28.6 2.1 %collective-permute-start.12 = (bf16[272,256]{1,0:T(8,128)(2,1)S(1)}, bf16[272,256]{1,0:T(8,128)(2,1)S(1)}, u32[]{:S(2)}, u32[]{:S(2)}) collective-permute-start(bf16[272,256]{1,0:T(8,128)(2,1)S(1)} %get-tuple-element.20), channel_id=1, source_target_pairs={{0,1},{1,0},{2,3},{3,2},{4,5},{5,4},{6,7},{7,6},{8,9},{9,8},{10,11... | collective-permute-start | bytes 417800 | tf_op jit(solution)/shard_map/ppermute | solution.py:243
  29.1 1.8 %copy-start = (bf16[512,256]{1,0:T(8,128)(2,1)S(1)}, bf16[512,256]{1,0:T(8,128)(2,1)}, u32[]{:S(2)}) copy-start(bf16[512,256]{1,0:T(8,128)(2,1)} %old.1) | copy-start | bytes 786436
  29.1 1.8 %collective-permute-start.13 = (bf16[272,256]{1,0:T(8,128)(2,1)S(1)}, bf16[272,256]{1,0:T(8,128)(2,1)S(1)}, u32[]{:S(2)}, u32[]{:S(2)}) collective-permute-start(bf16[272,256]{1,0:T(8,128)(2,1)S(1)} %get-tuple-element.21), channel_id=1, source_target_pairs={{0,1},{1,0},{2,3},{3,2},{4,5},{5,4},{6,7},{7,6},{8,9},{9,8},{10,11... | collective-permute-start | bytes 417800 | tf_op jit(solution)/shard_map/ppermute | solution.py:243

commit v7 on v6

--- a/solution.py
+++ b/solution.py
@@ -131,8 +131,8 @@
     return sums, jnp.sum(hot, axis=1, keepdims=True)
 
 
-def _sums_kernel(*refs):
-    *before, a, b, side_a, side_b, out, pack = refs
+def _add_sums(*refs):
+    *before, a, b, side_a, side_b, out = refs
     lists, width = out.shape[0] - 8, out.shape[1]
     mine, mine_n = _totals((a, b), lists)
     side, side_n = _totals((side_a, side_b), lists)
@@ -149,16 +149,29 @@
     else:
         out[0:lists, :] = mine + side
         out[lists:, :] = lines
+
+
+def _near_sums_kernel(a, b, side_a, side_b, out):
+    _add_sums(a, b, side_a, side_b, out)
+
+
+def _away_sums_kernel(before, near_a, near_b, a, b, side_a, side_b, out, pack):
+    _add_sums(before, a, b, side_a, side_b, out)
+    width = out.shape[1]
     capacity = width // 2
-    lines = []
-    for i, block in enumerate((a, b)):
-        rows = jnp.where(_core() == 0, block[capacity : 2 * capacity, :], block[0:capacity, :])
-        pack[i * capacity : (i + 1) * capacity, :] = rows
-        head = block[2 * capacity :, :].astype(jnp.float32)
-        lines.append(jnp.where(_core() == 0, head[1:2, :], head[0:1, :]))
-    pack[2 * capacity :, :] = jnp.where(
-        _iota((HEAD, width), 0) == 0, lines[0], lines[1]
-    ).astype(jnp.bfloat16)
+    size = 2 * capacity + HEAD
+    for j, pair in enumerate(((near_a, near_b), (a, b))):
+        lines = []
+        for i, block in enumerate(pair):
+            rows = jnp.where(_core() == 0, block[capacity : 2 * capacity, :], block[0:capacity, :])
+            at = j * size + i * capacity
+            pack[at : at + capacity, :] = rows
+            head = block[2 * capacity :, :].astype(jnp.float32)
+            lines.append(jnp.where(_core() == 0, head[1:2, :], head[0:1, :]))
+        at = j * size + 2 * capacity
+        pack[at : at + HEAD, :] = jnp.where(
+            _iota((HEAD, width), 0) == 0, lines[0], lines[1]
+        ).astype(jnp.bfloat16)
 
 
 def _hot(labels, lists):
@@ -197,7 +210,9 @@
     table = fresh[...]
     eye = _iota((capacity, capacity), 0) == _iota((capacity, capacity), 1)
     ordered = []
-    for i, (a, b, pack) in enumerate((blocks[0:3], blocks[3:6])):
+    size = 2 * capacity + HEAD
+    for i, (a, b) in enumerate((blocks[0:2], blocks[2:4])):
+        pack = blocks[4][i * size : (i + 1) * size, :]
         base = me ^ (4 * i)
         for j, (block, k) in enumerate(zip((a, b), _owners())):
             at = (2 * i + j) * capacity
@@ -274,10 +289,12 @@
     near = to_owners(payload, HEAD)
     away = to_owners(far, 0, near[2])
     flops = 2 * list_dev * capacity * width
-    mine, near_pack = _call(_sums_kernel, [total, pair], near, flops=8 * flops)
-    near_pack = hop(near_pack, 0, 1)
-    mine, away_pack = _call(_sums_kernel, [total, pair], (mine, *away), flops=8 * flops)
-    away_pack = hop(away_pack, 0, 1)
+    (mine,) = _call(_near_sums_kernel, [total], near, flops=8 * flops)
+    packs = jax.ShapeDtypeStruct((2 * pair.shape[0], width), jnp.bfloat16)
+    mine, pack = _call(
+        _away_sums_kernel, [total, packs], (mine, *near[0:2], *away), flops=8 * flops
+    )
+    pack = hop(pack, 0, 1)
     other = hop(mine, 0, 1)
     own = (*near[0:2], *away[0:2])
     (hots,) = _call(
@@ -290,7 +307,7 @@
             jax.ShapeDtypeStruct((peers * capacity, width), jnp.bfloat16),
             jax.ShapeDtypeStruct((peers, capacity), jnp.float32),
         ],
-        (mine, other, old_centroids, hots, *near[0:2], near_pack, *away[0:2], away_pack),
+        (mine, other, old_centroids, hots, *near[0:2], *away[0:2], pack),
         flops=8 * flops,
     )
     return (

time: 32.7 us -> 32.7 us (level)
    ppermute x6 -> x5, starting transfers between devices: 4.83 us -> 4.74 us  [hop(): lax.ppermute(a, ('items', 'rep'), [(i, i ^ swap) for i in range(peers * r...]
    ppermute x6 -> x5, waiting for transfers between devices: 2.28 us -> 2.36 us  [hop(): lax.ppermute(a, ('items', 'rep'), [(i, i ^ swap) for i in range(peers * r...]
  transfers between devices with their start and end apart: 14 -> 13, of which waited for: 6 -> 5; matrix products, arithmetic and copies ran while one was open for 0% -> 0% of each run, Pallas kernels for 6% -> 6%
where the time goes in v7:
time: 32.7 us; the launch traced here: 32.5 us
  starting transfers between devices  19.2 us (59%)
  waiting for transfers between devices  6.68 us (20%)
  Pallas kernels  4.24 us (13%)
  local copies, waits for them, and re-layouts  1.6 us (5%)
  between operations  0.74 us (2%)
    ppermute x8, starting transfers between devices, spread(): lax.ppermute(a, ('items', 'rep'), [(i, i ^ swap[i & 1]) for i in range(pe...  14.5 us
    ppermute x5, starting transfers between devices, hop(): lax.ppermute(a, ('items', 'rep'), [(i, i ^ swap) for i in range(peers * r...  4.74 us
    ppermute x8, waiting for transfers between devices, spread(): lax.ppermute(a, ('items', 'rep'), [(i, i ^ swap[i & 1]) for i in range(pe...  4.32 us
    pallas_call x7, Pallas kernels, _call(): pl.pallas_call(kernel, out_shape=outs, in_specs=[VMEM] * len(args), out_s...  4.24 us
    ppermute x5, waiting for transfers between devices, hop(): lax.ppermute(a, ('items', 'rep'), [(i, i ^ swap) for i in range(peers * r...  2.36 us
    pad x1, local copies, waits for them, and re-layouts, per_device_eight(): payload = lax.optimization_barrier(jnp.pad(embeds, ((0, HEAD), (0, 0))))  0.92 us
    unnamed x6, local copies, waits for them, and re-layouts  0.68 us
  transfers between devices with their start and end apart: 13, of which 5 were waited for; matrix products, arithmetic and copies ran while one was open for 0% of the time, Pallas kernels for 6%

profile of v7, /device:TPU:0, one launch (start us, length us, event | category | flops | bytes accessed | tf_op | source)
XLA Modules:
  0.0 32.5 jit_solution(6745730750111141582)
XLA Ops:
  0.6 0.9 %pad.4._ = bf16[272,256]{1,0:T(8,128)(2,1)S(1)} pad(bf16[256,256]{1,0:T(8,128)(2,1)} %param.4, bf16[]{:T(256)} %constant.2.clone.1), padding=0_16x0_0 | pad | bytes 270338 | tf_op jit(solution)/shard_map/jit(_pad)/pad | solution.py:281
  1.5 0.0 copy-start.2
  1.6 0.7 %copy-done.2 = s32[256]{0:T(256)S(1)} copy-done((s32[256]{0:T(256)S(1)}, s32[256]{0:T(256)}, u32[]{:S(2)}) %copy-start.2) | copy-done | bytes 1048
  2.2 0.0 copy-start.1
  2.2 0.5 %collective-permute-start = (bf16[272,256]{1,0:T(8,128)(2,1)S(1)}, bf16[272,256]{1,0:T(8,128)(2,1)S(1)}, u32[]{:S(2)}, u32[]{:S(2)}) collective-permute-start(bf16[272,256]{1,0:T(8,128)(2,1)S(1)} %shard_map.67.refs_0_), channel_id=1, source_target_pairs={{0,1},{1,0},{2,3},{3,2},{4,5},{5,4},{6,7},{7,6},{8,9},{9,8},{10,11... | collective-permute-start | bytes 417800 | tf_op jit(solution)/shard_map/ppermute | solution.py:258
  2.8 3.7 %collective-permute-start.5 = (bf16[272,256]{1,0:T(8,128)(2,1)S(1)}, bf16[272,256]{1,0:T(8,128)(2,1)S(1)}, u32[]{:S(2)}, u32[]{:S(2)}) collective-permute-start(bf16[272,256]{1,0:T(8,128)(2,1)S(1)} %shard_map.67.refs_0_), channel_id=1, source_target_pairs={{0,16},{1,17},{2,18},{3,19},{4,20},{5,21},{6,22},{7,23},{8,24},{9,... | collective-permute-start | bytes 417800 | tf_op jit(solution)/shard_map/ppermute | solution.py:258
  6.4 0.0 collective-permute-done.refs_1_
  6.4 0.0 copy-done.1
  6.4 0.7 %shard_map.68 = (bf16[288,256]{1,0:T(8,128)(2,1)S(1)}, bf16[288,256]{1,0:T(8,128)(2,1)S(1)}) custom-call(bf16[272,256]{1,0:T(8,128)(2,1)S(1)} %shard_map.67.refs_0_, bf16[272,256]{1,0:T(8,128)(2,1)S(1)} %collective-permute-done.refs_1_, s32[32,128]{1,0:T(8,128)S(1)} %bitcast.4), custom_call_target="tpu_custom_call" | custom-call | flops 67108864 | bytes 589824 | tf_op jit(solution)/shard_map/pallas_call | solution.py:239
  7.1 2.5 %collective-permute-start.3 = (bf16[288,256]{1,0:T(8,128)(2,1)S(1)}, bf16[288,256]{1,0:T(8,128)(2,1)S(1)}, u32[]{:S(2)}, u32[]{:S(2)}) collective-permute-start(bf16[288,256]{1,0:T(8,128)(2,1)S(1)} %get-tuple-element.12), channel_id=1, source_target_pairs={{0,6},{1,3},{2,4},{3,1},{4,2},{5,7},{6,0},{7,5},{8,14},{9,11},{10,... | collective-permute-start | bytes 442376 | tf_op jit(solution)/shard_map/ppermute | solution.py:267
  9.6 2.4 %collective-permute-start.1 = (bf16[288,256]{1,0:T(8,128)(2,1)S(1)}, bf16[288,256]{1,0:T(8,128)(2,1)S(1)}, u32[]{:S(2)}, u32[]{:S(2)}) collective-permute-start(bf16[288,256]{1,0:T(8,128)(2,1)S(1)} %get-tuple-element.12), channel_id=1, source_target_pairs={{0,4},{1,1},{2,6},{3,3},{4,0},{5,5},{6,2},{7,7},{8,12},{9,9},{10,1... | collective-permute-start | bytes 442376 | tf_op jit(solution)/shard_map/ppermute | solution.py:267
  12.0 1.6 %collective-permute-start.4 = (bf16[288,256]{1,0:T(8,128)(2,1)S(1)}, bf16[288,256]{1,0:T(8,128)(2,1)S(1)}, u32[]{:S(2)}, u32[]{:S(2)}) collective-permute-start(bf16[288,256]{1,0:T(8,128)(2,1)S(1)} %get-tuple-element.13), channel_id=1, source_target_pairs={{0,10},{1,15},{2,8},{3,13},{4,14},{5,11},{6,12},{7,9},{8,2},{9,7},... | collective-permute-start | bytes 442376 | tf_op jit(solution)/shard_map/ppermute | solution.py:267
  13.6 0.1 collective-permute-done.5.refs_0_
  13.8 0.0 collective-permute-start.6
  13.8 0.8 %collective-permute-start.2 = (bf16[288,256]{1,0:T(8,128)(2,1)S(1)}, bf16[288,256]{1,0:T(8,128)(2,1)S(1)}, u32[]{:S(2)}, u32[]{:S(2)}) collective-permute-start(bf16[288,256]{1,0:T(8,128)(2,1)S(1)} %get-tuple-element.13), channel_id=1, source_target_pairs={{0,8},{1,13},{2,10},{3,15},{4,12},{5,9},{6,14},{7,11},{8,0},{9,5},... | collective-permute-start | bytes 442376 | tf_op jit(solution)/shard_map/ppermute | solution.py:267
  14.5 0.6 %collective-permute-done.6.refs_1_ = bf16[272,256]{1,0:T(8,128)(2,1)S(1)} collective-permute-done((bf16[272,256]{1,0:T(8,128)(2,1)S(1)}, bf16[272,256]{1,0:T(8,128)(2,1)S(1)}, u32[]{:S(2)}, u32[]{:S(2)}) %collective-permute-start.6) | collective-permute-done | bytes 139296 | tf_op jit(solution)/shard_map/ppermute | solution.py:258
  15.1 0.0 collective-permute-done.3.side_a.refs_3_
  15.1 0.7 %shard_map.70 = (bf16[272,256]{1,0:T(8,128)(2,1)S(1)}, bf16[272,256]{1,0:T(8,128)(2,1)S(1)}) custom-call(bf16[272,256]{1,0:T(8,128)(2,1)S(1)} %collective-permute-done.5.refs_0_, bf16[272,256]{1,0:T(8,128)(2,1)S(1)} %collective-permute-done.6.refs_1_, s32[32,128]{1,0:T(8,128)S(1)} %bitcast.5, bf16[288,256]{1,0:T(8,128)(2,1)S(1)} %collective-permute-done.3.side_a.refs_3_), custom_call_target="tpu_custom_call" | custom-call | flops 67108864 | bytes 720896 | tf_op jit(solution)/shard_map/pallas_call | solution.py:239
  15.8 2.6 %collective-permute-start.9 = (bf16[272,256]{1,0:T(8,128)(2,1)S(1)}, bf16[272,256]{1,0:T(8,128)(2,1)S(1)}, u32[]{:S(2)}, u32[]{:S(2)}) collective-permute-start(bf16[272,256]{1,0:T(8,128)(2,1)S(1)} %get-tuple-element.14), channel_id=1, source_target_pairs={{0,6},{1,3},{2,4},{3,1},{4,2},{5,7},{6,0},{7,5},{8,14},{9,11},{10,... | collective-permute-start | bytes 417800 | tf_op jit(solution)/shard_map/ppermute | solution.py:267
  18.4 2.4 %collective-permute-start.7 = (bf16[272,256]{1,0:T(8,128)(2,1)S(1)}, bf16[272,256]{1,0:T(8,128)(2,1)S(1)}, u32[]{:S(2)}, u32[]{:S(2)}) collective-permute-start(bf16[272,256]{1,0:T(8,128)(2,1)S(1)} %get-tuple-element.14), channel_id=1, source_target_pairs={{0,4},{1,1},{2,6},{3,3},{4,0},{5,5},{6,2},{7,7},{8,12},{9,9},{10,1... | collective-permute-start | bytes 417800 | tf_op jit(solution)/shard_map/ppermute | solution.py:267
  20.8 0.0 collective-permute-done.1.a.near_a.refs_0_
  20.8 2.1 %collective-permute-start.10 = (bf16[272,256]{1,0:T(8,128)(2,1)S(1)}, bf16[272,256]{1,0:T(8,128)(2,1)S(1)}, u32[]{:S(2)}, u32[]{:S(2)}) collective-permute-start(bf16[272,256]{1,0:T(8,128)(2,1)S(1)} %get-tuple-element.15), channel_id=1, source_target_pairs={{0,10},{1,15},{2,8},{3,13},{4,14},{5,11},{6,12},{7,9},{8,2},{9,7},... | collective-permute-start | bytes 417800 | tf_op jit(solution)/shard_map/ppermute | solution.py:267
  22.9 0.0 collective-permute-done.4.side_b
  22.9 0.1 collective-permute-start.8
  23.0 0.0 collective-permute-done.2.b.near_b.refs_1_
  23.0 0.6 %shard_map.69.before = f32[520,256]{1,0:T(8,128)S(1)} custom-call(bf16[288,256]{1,0:T(8,128)(2,1)S(1)} %collective-permute-done.1.a.near_a.refs_0_, bf16[288,256]{1,0:T(8,128)(2,1)S(1)} %collective-permute-done.2.b.near_b.refs_1_, bf16[288,256]{1,0:T(8,128)(2,1)S(1)} %collective-permute-done.3.side_a.refs_3_, bf16[288,256]{1,0:T(8,128)(2,1)S(1)} %collective-permute-done.4.side_b), custom_call_target="tpu_custom_call" | custom-call | flops 268435456 | bytes 1122304 | tf_op jit(solution)/shard_map/pallas_call | solution.py:239
  23.6 0.0 collective-permute-done.9.side_a
  23.6 3.6 %collective-permute-done.7.a.refs_2_ = bf16[272,256]{1,0:T(8,128)(2,1)S(1)} collective-permute-done((bf16[272,256]{1,0:T(8,128)(2,1)S(1)}, bf16[272,256]{1,0:T(8,128)(2,1)S(1)}, u32[]{:S(2)}, u32[]{:S(2)}) %collective-permute-start.7) | collective-permute-done | bytes 139296 | tf_op jit(solution)/shard_map/ppermute | solution.py:267
  27.2 0.0 collective-permute-done.10.side_b
  27.2 0.7 %collective-permute-done.8.b.refs_3_ = bf16[272,256]{1,0:T(8,128)(2,1)S(1)} collective-permute-done((bf16[272,256]{1,0:T(8,128)(2,1)S(1)}, bf16[272,256]{1,0:T(8,128)(2,1)S(1)}, u32[]{:S(2)}, u32[]{:S(2)}) %collective-permute-start.8) | collective-permute-done | bytes 139296 | tf_op jit(solution)/shard_map/ppermute | solution.py:267
  27.9 0.6 %shard_map.71 = (f32[520,256]{1,0:T(8,128)S(1)}, bf16[544,256]{1,0:T(8,128)(2,1)S(1)}) custom-call(f32[520,256]{1,0:T(8,128)S(1)} %shard_map.69.before, bf16[288,256]{1,0:T(8,128)(2,1)S(1)} %collective-permute-done.1.a.near_a.refs_0_, bf16[288,256]{1,0:T(8,128)(2,1)S(1)} %collective-permute-done.2.b.near_b.refs_1_, ...), custom_call_target="tpu_custom_call" | custom-call | flops 268435456 | bytes 2195456 | tf_op jit(solution)/shard_map/pallas_call | solution.py:239
  28.6 0.1 collective-permute-start.11
  28.6 0.0 copy-start
  28.6 0.5 %collective-permute-start.12 = (bf16[544,256]{1,0:T(8,128)(2,1)S(1)}, bf16[544,256]{1,0:T(8,128)(2,1)S(1)}, u32[]{:S(2)}, u32[]{:S(2)}) collective-permute-start(bf16[544,256]{1,0:T(8,128)(2,1)S(1)} %get-tuple-element.17), channel_id=1, source_target_pairs={{0,1},{1,0},{2,3},{3,2},{4,5},{5,4},{6,7},{7,6},{8,9},{9,8},{10,11... | collective-permute-start | bytes 835592 | tf_op jit(solution)/shard_map/ppermute | solution.py:258
  29.1 0.2 shard_map.72.hots
  29.3 1.6 %collective-permute-done.12.refs_4_ = bf16[544,256]{1,0:T(8,128)(2,1)S(1)} collective-permute-done((bf16[544,256]{1,0:T(8,128)(2,1)S(1)}, bf16[544,256]{1,0:T(8,128)(2,1)S(1)}, u32[]{:S(2)}, u32[]{:S(2)}) %collective-permute-start.12) | collective-permute-done | bytes 278560 | tf_op jit(solution)/shard_map/ppermute | solution.py:258
  30.9 0.0 collective-permute-done.11.other
  30.9 0.0 copy-done
  30.9 1.5 %shard_map.73 = (bf16[512,256]{1,0:T(8,128)(2,1)}, bf16[1024,256]{1,0:T(8,128)(2,1)}, f32[8,128]{1,0:T(8,128)}) custom-call(f32[520,256]{1,0:T(8,128)S(1)} %get-tuple-element.16.mine, f32[520,256]{1,0:T(8,128)S(1)} %collective-permute-done.11.other, bf16[512,256]{1,0:T(8,128)(2,1)S(1)} %copy-done, bf16[512,512]{1,0:T(8,128)(2,1)S(1)} %shard_map.72.hots, ...), custom_call_target="tpu_custom_call" | custom-call | flops 268435456 | bytes 3493888 | tf_op jit(solution)/shard_map/pallas_call | solution.py:239
  (1 shorter events, 0.0 us)
Async XLA Ops:
  1.5 0.7 %copy-start.2 = (s32[256]{0:T(256)S(1)}, s32[256]{0:T(256)}, u32[]{:S(2)}) copy-start(s32[256]{0:T(256)} %param.5) | copy-start | bytes 3076
  2.2 4.2 %copy-start.1 = (s32[4096]{0:T(1024)S(1)}, s32[4096]{0:T(1024)}, u32[]{:S(2)}) copy-start(s32[4096]{0:T(1024)} %param.6) | copy-start | bytes 49156
  2.2 4.2 %collective-permute-start = (bf16[272,256]{1,0:T(8,128)(2,1)S(1)}, bf16[272,256]{1,0:T(8,128)(2,1)S(1)}, u32[]{:S(2)}, u32[]{:S(2)}) collective-permute-start(bf16[272,256]{1,0:T(8,128)(2,1)S(1)} %shard_map.67.refs_0_), channel_id=1, source_target_pairs={{0,1},{1,0},{2,3},{3,2},{4,5},{5,4},{6,7},{7,6},{8,9},{9,8},{10,11... | collective-permute-start | bytes 417800 | tf_op jit(solution)/shard_map/ppermute | solution.py:258
  2.8 11.0 %collective-permute-start.5 = (bf16[272,256]{1,0:T(8,128)(2,1)S(1)}, bf16[272,256]{1,0:T(8,128)(2,1)S(1)}, u32[]{:S(2)}, u32[]{:S(2)}) collective-permute-start(bf16[272,256]{1,0:T(8,128)(2,1)S(1)} %shard_map.67.refs_0_), channel_id=1, source_target_pairs={{0,16},{1,17},{2,18},{3,19},{4,20},{5,21},{6,22},{7,23},{8,24},{9,... | collective-permute-start | bytes 417800 | tf_op jit(solution)/shard_map/ppermute | solution.py:258
  7.1 8.0 %collective-permute-start.3 = (bf16[288,256]{1,0:T(8,128)(2,1)S(1)}, bf16[288,256]{1,0:T(8,128)(2,1)S(1)}, u32[]{:S(2)}, u32[]{:S(2)}) collective-permute-start(bf16[288,256]{1,0:T(8,128)(2,1)S(1)} %get-tuple-element.12), channel_id=1, source_target_pairs={{0,6},{1,3},{2,4},{3,1},{4,2},{5,7},{6,0},{7,5},{8,14},{9,11},{10,... | collective-permute-start | bytes 442376 | tf_op jit(solution)/shard_map/ppermute | solution.py:267
  9.6 11.2 %collective-permute-start.1 = (bf16[288,256]{1,0:T(8,128)(2,1)S(1)}, bf16[288,256]{1,0:T(8,128)(2,1)S(1)}, u32[]{:S(2)}, u32[]{:S(2)}) collective-permute-start(bf16[288,256]{1,0:T(8,128)(2,1)S(1)} %get-tuple-element.12), channel_id=1, source_target_pairs={{0,4},{1,1},{2,6},{3,3},{4,0},{5,5},{6,2},{7,7},{8,12},{9,9},{10,1... | collective-permute-start | bytes 442376 | tf_op jit(solution)/shard_map/ppermute | solution.py:267
  12.0 10.9 %collective-permute-start.4 = (bf16[288,256]{1,0:T(8,128)(2,1)S(1)}, bf16[288,256]{1,0:T(8,128)(2,1)S(1)}, u32[]{:S(2)}, u32[]{:S(2)}) collective-permute-start(bf16[288,256]{1,0:T(8,128)(2,1)S(1)} %get-tuple-element.13), channel_id=1, source_target_pairs={{0,10},{1,15},{2,8},{3,13},{4,14},{5,11},{6,12},{7,9},{8,2},{9,7},... | collective-permute-start | bytes 442376 | tf_op jit(solution)/shard_map/ppermute | solution.py:267
  13.8 1.4 %collective-permute-start.6 = (bf16[272,256]{1,0:T(8,128)(2,1)S(1)}, bf16[272,256]{1,0:T(8,128)(2,1)S(1)}, u32[]{:S(2)}, u32[]{:S(2)}) collective-permute-start(bf16[272,256]{1,0:T(8,128)(2,1)S(1)} %collective-permute-done.5.refs_0_), channel_id=1, source_target_pairs={{0,1},{1,0},{2,3},{3,2},{4,5},{5,4},{6,7},{7,6},{8,9},{9,8},{10,11... | collective-permute-start | bytes 417800 | tf_op jit(solution)/shard_map/ppermute | solution.py:258
  13.8 9.2 %collective-permute-start.2 = (bf16[288,256]{1,0:T(8,128)(2,1)S(1)}, bf16[288,256]{1,0:T(8,128)(2,1)S(1)}, u32[]{:S(2)}, u32[]{:S(2)}) collective-permute-start(bf16[288,256]{1,0:T(8,128)(2,1)S(1)} %get-tuple-element.13), channel_id=1, source_target_pairs={{0,8},{1,13},{2,10},{3,15},{4,12},{5,9},{6,14},{7,11},{8,0},{9,5},... | collective-permute-start | bytes 442376 | tf_op jit(solution)/shard_map/ppermute | solution.py:267
  15.8 7.8 %collective-permute-start.9 = (bf16[272,256]{1,0:T(8,128)(2,1)S(1)}, bf16[272,256]{1,0:T(8,128)(2,1)S(1)}, u32[]{:S(2)}, u32[]{:S(2)}) collective-permute-start(bf16[272,256]{1,0:T(8,128)(2,1)S(1)} %get-tuple-element.14), channel_id=1, source_target_pairs={{0,6},{1,3},{2,4},{3,1},{4,2},{5,7},{6,0},{7,5},{8,14},{9,11},{10,... | collective-permute-start | bytes 417800 | tf_op jit(solution)/shard_map/ppermute | solution.py:267
  18.4 8.8 %collective-permute-start.7 = (bf16[272,256]{1,0:T(8,128)(2,1)S(1)}, bf16[272,256]{1,0:T(8,128)(2,1)S(1)}, u32[]{:S(2)}, u32[]{:S(2)}) collective-permute-start(bf16[272,256]{1,0:T(8,128)(2,1)S(1)} %get-tuple-element.14), channel_id=1, source_target_pairs={{0,4},{1,1},{2,6},{3,3},{4,0},{5,5},{6,2},{7,7},{8,12},{9,9},{10,1... | collective-permute-start | bytes 417800 | tf_op jit(solution)/shard_map/ppermute | solution.py:267
  20.8 6.4 %collective-permute-start.10 = (bf16[272,256]{1,0:T(8,128)(2,1)S(1)}, bf16[272,256]{1,0:T(8,128)(2,1)S(1)}, u32[]{:S(2)}, u32[]{:S(2)}) collective-permute-start(bf16[272,256]{1,0:T(8,128)(2,1)S(1)} %get-tuple-element.15), channel_id=1, source_target_pairs={{0,10},{1,15},{2,8},{3,13},{4,14},{5,11},{6,12},{7,9},{8,2},{9,7},... | collective-permute-start | bytes 417800 | tf_op jit(solution)/shard_map/ppermute | solution.py:267
  22.9 5.1 %collective-permute-start.8 = (bf16[272,256]{1,0:T(8,128)(2,1)S(1)}, bf16[272,256]{1,0:T(8,128)(2,1)S(1)}, u32[]{:S(2)}, u32[]{:S(2)}) collective-permute-start(bf16[272,256]{1,0:T(8,128)(2,1)S(1)} %get-tuple-element.15), channel_id=1, source_target_pairs={{0,8},{1,13},{2,10},{3,15},{4,12},{5,9},{6,14},{7,11},{8,0},{9,5},... | collective-permute-start | bytes 417800 | tf_op jit(solution)/shard_map/ppermute | solution.py:267
  28.6 2.4 %collective-permute-start.11 = (f32[520,256]{1,0:T(8,128)S(1)}, f32[520,256]{1,0:T(8,128)S(1)}, u32[]{:S(2)}, u32[]{:S(2)}) collective-permute-start(f32[520,256]{1,0:T(8,128)S(1)} %get-tuple-element.16.mine), channel_id=1, source_target_pairs={{0,1},{1,0},{2,3},{3,2},{4,5},{5,4},{6,7},{7,6},{8,9},{9,8},{10,11... | collective-permute-start | bytes 1597448 | tf_op jit(solution)/shard_map/ppermute | solution.py:258
  28.6 2.3 %copy-start = (bf16[512,256]{1,0:T(8,128)(2,1)S(1)}, bf16[512,256]{1,0:T(8,128)(2,1)}, u32[]{:S(2)}) copy-start(bf16[512,256]{1,0:T(8,128)(2,1)} %old.1) | copy-start | bytes 786436
  28.6 2.3 %collective-permute-start.12 = (bf16[544,256]{1,0:T(8,128)(2,1)S(1)}, bf16[544,256]{1,0:T(8,128)(2,1)S(1)}, u32[]{:S(2)}, u32[]{:S(2)}) collective-permute-start(bf16[544,256]{1,0:T(8,128)(2,1)S(1)} %get-tuple-element.17), channel_id=1, source_target_pairs={{0,1},{1,0},{2,3},{3,2},{4,5},{5,4},{6,7},{7,6},{8,9},{9,8},{10,11... | collective-permute-start | bytes 835592 | tf_op jit(solution)/shard_map/ppermute | solution.py:258

commit v8 on v6

--- a/solution.py
+++ b/solution.py
@@ -26,13 +26,12 @@
     hot = _bf16(_iota((t, n), 0) == (assign >> 7))
     lane = _iota((128, n), 0) == (assign & 127)
 
-    def pick(part):
-        rows = lax.dot_general(
-            _bf16(part), hot, (((0,), (0,)), ((), ())), preferred_element_type=jnp.float32
-        )
-        return jnp.sum(jnp.where(lane, rows, 0.0), axis=0, keepdims=True)
-
-    return (pick(table & 255) + 256.0 * pick(table >> 8)).astype(jnp.int32)
+    parts = _bf16(jnp.concatenate([table & 255, table >> 8], axis=1))
+    rows = lax.dot_general(
+        parts, hot, (((0,), (0,)), ((), ())), preferred_element_type=jnp.float32
+    )
+    whole = rows[:128, :] + 256.0 * rows[128:, :]
+    return jnp.sum(jnp.where(lane, whole, 0.0), axis=0, keepdims=True).astype(jnp.int32)
 
 
 def _core():

time: 32.7 us -> 32.7 us (level)
  transfers between devices with their start and end apart: 14 -> 14, of which waited for: 6 -> 6; matrix products, arithmetic and copies ran while one was open for 0% -> 0% of each run, Pallas kernels for 6% -> 7%
where the time goes in v8:
time: 32.7 us; the launch traced here: 32.5 us
  starting transfers between devices  19.3 us (59%)
  waiting for transfers between devices  6.59 us (20%)
  Pallas kernels  4.26 us (13%)
  local copies, waits for them, and re-layouts  1.6 us (5%)
  between operations  0.73 us (2%)
    ppermute x8, starting transfers between devices, spread(): lax.ppermute(a, ('items', 'rep'), [(i, i ^ swap[i & 1]) for i in range(pe...  14.5 us
    ppermute x6, starting transfers between devices, hop(): lax.ppermute(a, ('items', 'rep'), [(i, i ^ swap) for i in range(peers * r...  4.83 us
    ppermute x8, waiting for transfers between devices, spread(): lax.ppermute(a, ('items', 'rep'), [(i, i ^ swap[i & 1]) for i in range(pe...  4.32 us
    pallas_call x7, Pallas kernels, _call(): pl.pallas_call(kernel, out_shape=outs, in_specs=[VMEM] * len(args), out_s...  4.26 us
    ppermute x6, waiting for transfers between devices, hop(): lax.ppermute(a, ('items', 'rep'), [(i, i ^ swap) for i in range(peers * r...  2.27 us
    pad x1, local copies, waits for them, and re-layouts, per_device_eight(): payload = lax.optimization_barrier(jnp.pad(embeds, ((0, HEAD), (0, 0))))  0.92 us
    unnamed x6, local copies, waits for them, and re-layouts  0.68 us
  transfers between devices with their start and end apart: 14, of which 6 were waited for; matrix products, arithmetic and copies ran while one was open for 0% of the time, Pallas kernels for 7%

profile of v8, /device:TPU:0, one launch (start us, length us, event | category | flops | bytes accessed | tf_op | source)
XLA Modules:
  0.0 32.5 jit_solution(9709824130847465061)
XLA Ops:
  0.6 0.9 %pad.4._ = bf16[272,256]{1,0:T(8,128)(2,1)S(1)} pad(bf16[256,256]{1,0:T(8,128)(2,1)} %param.4, bf16[]{:T(256)} %constant.2.clone.1), padding=0_16x0_0 | pad | bytes 270338 | tf_op jit(solution)/shard_map/jit(_pad)/pad | solution.py:265
  1.5 0.0 copy-start.2
  1.6 0.7 %copy-done.2 = s32[256]{0:T(256)S(1)} copy-done((s32[256]{0:T(256)S(1)}, s32[256]{0:T(256)}, u32[]{:S(2)}) %copy-start.2) | copy-done | bytes 1048
  2.2 0.0 copy-start.1
  2.2 0.5 %collective-permute-start = (bf16[272,256]{1,0:T(8,128)(2,1)S(1)}, bf16[272,256]{1,0:T(8,128)(2,1)S(1)}, u32[]{:S(2)}, u32[]{:S(2)}) collective-permute-start(bf16[272,256]{1,0:T(8,128)(2,1)S(1)} %shard_map.67.refs_0_), channel_id=1, source_target_pairs={{0,1},{1,0},{2,3},{3,2},{4,5},{5,4},{6,7},{7,6},{8,9},{9,8},{10,11... | collective-permute-start | bytes 417800 | tf_op jit(solution)/shard_map/ppermute | solution.py:242
  2.8 3.7 %collective-permute-start.5 = (bf16[272,256]{1,0:T(8,128)(2,1)S(1)}, bf16[272,256]{1,0:T(8,128)(2,1)S(1)}, u32[]{:S(2)}, u32[]{:S(2)}) collective-permute-start(bf16[272,256]{1,0:T(8,128)(2,1)S(1)} %shard_map.67.refs_0_), channel_id=1, source_target_pairs={{0,16},{1,17},{2,18},{3,19},{4,20},{5,21},{6,22},{7,23},{8,24},{9,... | collective-permute-start | bytes 417800 | tf_op jit(solution)/shard_map/ppermute | solution.py:242
  6.4 0.0 collective-permute-done.refs_1_
  6.4 0.0 copy-done.1
  6.4 0.7 %shard_map.68 = (bf16[288,256]{1,0:T(8,128)(2,1)S(1)}, bf16[288,256]{1,0:T(8,128)(2,1)S(1)}) custom-call(bf16[272,256]{1,0:T(8,128)(2,1)S(1)} %shard_map.67.refs_0_, bf16[272,256]{1,0:T(8,128)(2,1)S(1)} %collective-permute-done.refs_1_, s32[32,128]{1,0:T(8,128)S(1)} %bitcast.4), custom_call_target="tpu_custom_call" | custom-call | flops 67108864 | bytes 589824 | tf_op jit(solution)/shard_map/pallas_call | solution.py:223
  7.1 2.5 %collective-permute-start.3 = (bf16[288,256]{1,0:T(8,128)(2,1)S(1)}, bf16[288,256]{1,0:T(8,128)(2,1)S(1)}, u32[]{:S(2)}, u32[]{:S(2)}) collective-permute-start(bf16[288,256]{1,0:T(8,128)(2,1)S(1)} %get-tuple-element.14), channel_id=1, source_target_pairs={{0,6},{1,3},{2,4},{3,1},{4,2},{5,7},{6,0},{7,5},{8,14},{9,11},{10,... | collective-permute-start | bytes 442376 | tf_op jit(solution)/shard_map/ppermute | solution.py:251
  9.6 2.4 %collective-permute-start.1 = (bf16[288,256]{1,0:T(8,128)(2,1)S(1)}, bf16[288,256]{1,0:T(8,128)(2,1)S(1)}, u32[]{:S(2)}, u32[]{:S(2)}) collective-permute-start(bf16[288,256]{1,0:T(8,128)(2,1)S(1)} %get-tuple-element.14), channel_id=1, source_target_pairs={{0,4},{1,1},{2,6},{3,3},{4,0},{5,5},{6,2},{7,7},{8,12},{9,9},{10,1... | collective-permute-start | bytes 442376 | tf_op jit(solution)/shard_map/ppermute | solution.py:251
  12.0 1.6 %collective-permute-start.4 = (bf16[288,256]{1,0:T(8,128)(2,1)S(1)}, bf16[288,256]{1,0:T(8,128)(2,1)S(1)}, u32[]{:S(2)}, u32[]{:S(2)}) collective-permute-start(bf16[288,256]{1,0:T(8,128)(2,1)S(1)} %get-tuple-element.15), channel_id=1, source_target_pairs={{0,10},{1,15},{2,8},{3,13},{4,14},{5,11},{6,12},{7,9},{8,2},{9,7},... | collective-permute-start | bytes 442376 | tf_op jit(solution)/shard_map/ppermute | solution.py:251
  13.6 0.1 collective-permute-done.5.refs_0_
  13.8 0.0 collective-permute-start.6
  13.8 0.8 %collective-permute-start.2 = (bf16[288,256]{1,0:T(8,128)(2,1)S(1)}, bf16[288,256]{1,0:T(8,128)(2,1)S(1)}, u32[]{:S(2)}, u32[]{:S(2)}) collective-permute-start(bf16[288,256]{1,0:T(8,128)(2,1)S(1)} %get-tuple-element.15), channel_id=1, source_target_pairs={{0,8},{1,13},{2,10},{3,15},{4,12},{5,9},{6,14},{7,11},{8,0},{9,5},... | collective-permute-start | bytes 442376 | tf_op jit(solution)/shard_map/ppermute | solution.py:251
  14.5 0.6 %collective-permute-done.6.refs_1_ = bf16[272,256]{1,0:T(8,128)(2,1)S(1)} collective-permute-done((bf16[272,256]{1,0:T(8,128)(2,1)S(1)}, bf16[272,256]{1,0:T(8,128)(2,1)S(1)}, u32[]{:S(2)}, u32[]{:S(2)}) %collective-permute-start.6) | collective-permute-done | bytes 139296 | tf_op jit(solution)/shard_map/ppermute | solution.py:242
  15.1 0.0 collective-permute-done.3.refs_2_.refs_3_
  15.1 0.7 %shard_map.70 = (bf16[272,256]{1,0:T(8,128)(2,1)S(1)}, bf16[272,256]{1,0:T(8,128)(2,1)S(1)}) custom-call(bf16[272,256]{1,0:T(8,128)(2,1)S(1)} %collective-permute-done.5.refs_0_, bf16[272,256]{1,0:T(8,128)(2,1)S(1)} %collective-permute-done.6.refs_1_, s32[32,128]{1,0:T(8,128)S(1)} %bitcast.5, bf16[288,256]{1,0:T(8,128)(2,1)S(1)} %collective-permute-done.3.refs_2_.refs_3_), custom_call_target="tpu_custom_call" | custom-call | flops 67108864 | bytes 720896 | tf_op jit(solution)/shard_map/pallas_call | solution.py:223
  15.8 2.6 %collective-permute-start.9 = (bf16[272,256]{1,0:T(8,128)(2,1)S(1)}, bf16[272,256]{1,0:T(8,128)(2,1)S(1)}, u32[]{:S(2)}, u32[]{:S(2)}) collective-permute-start(bf16[272,256]{1,0:T(8,128)(2,1)S(1)} %get-tuple-element.17), channel_id=1, source_target_pairs={{0,6},{1,3},{2,4},{3,1},{4,2},{5,7},{6,0},{7,5},{8,14},{9,11},{10,... | collective-permute-start | bytes 417800 | tf_op jit(solution)/shard_map/ppermute | solution.py:251
  18.4 2.4 %collective-permute-start.7 = (bf16[272,256]{1,0:T(8,128)(2,1)S(1)}, bf16[272,256]{1,0:T(8,128)(2,1)S(1)}, u32[]{:S(2)}, u32[]{:S(2)}) collective-permute-start(bf16[272,256]{1,0:T(8,128)(2,1)S(1)} %get-tuple-element.17), channel_id=1, source_target_pairs={{0,4},{1,1},{2,6},{3,3},{4,0},{5,5},{6,2},{7,7},{8,12},{9,9},{10,1... | collective-permute-start | bytes 417800 | tf_op jit(solution)/shard_map/ppermute | solution.py:251
  20.8 0.0 collective-permute-done.1.refs_0_
  20.8 2.1 %collective-permute-start.10 = (bf16[272,256]{1,0:T(8,128)(2,1)S(1)}, bf16[272,256]{1,0:T(8,128)(2,1)S(1)}, u32[]{:S(2)}, u32[]{:S(2)}) collective-permute-start(bf16[272,256]{1,0:T(8,128)(2,1)S(1)} %get-tuple-element.18), channel_id=1, source_target_pairs={{0,10},{1,15},{2,8},{3,13},{4,14},{5,11},{6,12},{7,9},{8,2},{9,7},... | collective-permute-start | bytes 417800 | tf_op jit(solution)/shard_map/ppermute | solution.py:251
  22.9 0.0 collective-permute-done.4.refs_3_
  22.9 0.1 collective-permute-start.8
  23.0 0.0 collective-permute-done.2.refs_1_
  23.0 0.6 %shard_map.69 = (f32[520,256]{1,0:T(8,128)S(1)}, bf16[272,256]{1,0:T(8,128)(2,1)S(1)}) custom-call(bf16[288,256]{1,0:T(8,128)(2,1)S(1)} %collective-permute-done.1.refs_0_, bf16[288,256]{1,0:T(8,128)(2,1)S(1)} %collective-permute-done.2.refs_1_, bf16[288,256]{1,0:T(8,128)(2,1)S(1)} %collective-permute-done.3.refs_2_.refs_3_, ...), custom_call_target="tpu_custom_call" | custom-call | flops 268435456 | bytes 1261568 | tf_op jit(solution)/shard_map/pallas_call | solution.py:223
  23.6 0.0 collective-permute-done.9.refs_3_
  23.6 3.6 %collective-permute-done.7.refs_1_.refs_2_.refs_3_ = bf16[272,256]{1,0:T(8,128)(2,1)S(1)} collective-permute-done((bf16[272,256]{1,0:T(8,128)(2,1)S(1)}, bf16[272,256]{1,0:T(8,128)(2,1)S(1)}, u32[]{:S(2)}, u32[]{:S(2)}) %collective-permute-start.7) | collective-permute-done | bytes 139296 | tf_op jit(solution)/shard_map/ppermute | solution.py:251
  27.2 0.0 collective-permute-done.10.refs_4_
  27.2 0.7 %collective-permute-done.8.refs_2_.refs_3_.refs_4_ = bf16[272,256]{1,0:T(8,128)(2,1)S(1)} collective-permute-done((bf16[272,256]{1,0:T(8,128)(2,1)S(1)}, bf16[272,256]{1,0:T(8,128)(2,1)S(1)}, u32[]{:S(2)}, u32[]{:S(2)}) %collective-permute-start.8) | collective-permute-done | bytes 139296 | tf_op jit(solution)/shard_map/ppermute | solution.py:251
  28.0 0.6 %shard_map.71 = (f32[520,256]{1,0:T(8,128)S(1)}, bf16[272,256]{1,0:T(8,128)(2,1)S(1)}) custom-call(f32[520,256]{1,0:T(8,128)S(1)} %get-tuple-element.16.refs_0_, bf16[272,256]{1,0:T(8,128)(2,1)S(1)} %collective-permute-done.7.refs_1_.refs_2_.refs_3_, bf16[272,256]{1,0:T(8,128)(2,1)S(1)} %collective-permute-done.8.refs_2_.refs_3_.refs_4_, ...), custom_call_target="tpu_custom_call" | custom-call | flops 268435456 | bytes 1761280 | tf_op jit(solution)/shard_map/pallas_call | solution.py:223
  28.6 0.1 collective-permute-start.11
  28.6 0.5 %collective-permute-start.12 = (bf16[272,256]{1,0:T(8,128)(2,1)S(1)}, bf16[272,256]{1,0:T(8,128)(2,1)S(1)}, u32[]{:S(2)}, u32[]{:S(2)}) collective-permute-start(bf16[272,256]{1,0:T(8,128)(2,1)S(1)} %get-tuple-element.20), channel_id=1, source_target_pairs={{0,1},{1,0},{2,3},{3,2},{4,5},{5,4},{6,7},{7,6},{8,9},{9,8},{10,11... | collective-permute-start | bytes 417800 | tf_op jit(solution)/shard_map/ppermute | solution.py:242
  29.1 0.0 copy-start
  29.1 0.1 collective-permute-start.13
  29.2 0.2 shard_map.72.hots
  29.4 1.3 %collective-permute-done.12.refs_2_ = bf16[272,256]{1,0:T(8,128)(2,1)S(1)} collective-permute-done((bf16[272,256]{1,0:T(8,128)(2,1)S(1)}, bf16[272,256]{1,0:T(8,128)(2,1)S(1)}, u32[]{:S(2)}, u32[]{:S(2)}) %collective-permute-start.12) | collective-permute-done | bytes 139296 | tf_op jit(solution)/shard_map/ppermute | solution.py:242
  30.8 0.2 collective-permute-done.13.refs_5_
  31.0 0.0 collective-permute-done.11.other
  31.0 0.0 copy-done
  31.0 1.5 %shard_map.73 = (bf16[512,256]{1,0:T(8,128)(2,1)}, bf16[1024,256]{1,0:T(8,128)(2,1)}, f32[8,128]{1,0:T(8,128)}) custom-call(f32[520,256]{1,0:T(8,128)S(1)} %get-tuple-element.19.mine, f32[520,256]{1,0:T(8,128)S(1)} %collective-permute-done.11.other, bf16[512,256]{1,0:T(8,128)(2,1)S(1)} %copy-done, bf16[512,512]{1,0:T(8,128)(2,1)S(1)} %shard_map.72.hots, ...), custom_call_target="tpu_custom_call" | custom-call | flops 268435456 | bytes 3493888 | tf_op jit(solution)/shard_map/pallas_call | solution.py:223
  (1 shorter events, 0.0 us)
Async XLA Ops:
  1.5 0.7 %copy-start.2 = (s32[256]{0:T(256)S(1)}, s32[256]{0:T(256)}, u32[]{:S(2)}) copy-start(s32[256]{0:T(256)} %param.5) | copy-start | bytes 3076
  2.2 4.2 %copy-start.1 = (s32[4096]{0:T(1024)S(1)}, s32[4096]{0:T(1024)}, u32[]{:S(2)}) copy-start(s32[4096]{0:T(1024)} %param.6) | copy-start | bytes 49156
  2.2 4.2 %collective-permute-start = (bf16[272,256]{1,0:T(8,128)(2,1)S(1)}, bf16[272,256]{1,0:T(8,128)(2,1)S(1)}, u32[]{:S(2)}, u32[]{:S(2)}) collective-permute-start(bf16[272,256]{1,0:T(8,128)(2,1)S(1)} %shard_map.67.refs_0_), channel_id=1, source_target_pairs={{0,1},{1,0},{2,3},{3,2},{4,5},{5,4},{6,7},{7,6},{8,9},{9,8},{10,11... | collective-permute-start | bytes 417800 | tf_op jit(solution)/shard_map/ppermute | solution.py:242
  2.8 11.0 %collective-permute-start.5 = (bf16[272,256]{1,0:T(8,128)(2,1)S(1)}, bf16[272,256]{1,0:T(8,128)(2,1)S(1)}, u32[]{:S(2)}, u32[]{:S(2)}) collective-permute-start(bf16[272,256]{1,0:T(8,128)(2,1)S(1)} %shard_map.67.refs_0_), channel_id=1, source_target_pairs={{0,16},{1,17},{2,18},{3,19},{4,20},{5,21},{6,22},{7,23},{8,24},{9,... | collective-permute-start | bytes 417800 | tf_op jit(solution)/shard_map/ppermute | solution.py:242
  7.1 8.0 %collective-permute-start.3 = (bf16[288,256]{1,0:T(8,128)(2,1)S(1)}, bf16[288,256]{1,0:T(8,128)(2,1)S(1)}, u32[]{:S(2)}, u32[]{:S(2)}) collective-permute-start(bf16[288,256]{1,0:T(8,128)(2,1)S(1)} %get-tuple-element.14), channel_id=1, source_target_pairs={{0,6},{1,3},{2,4},{3,1},{4,2},{5,7},{6,0},{7,5},{8,14},{9,11},{10,... | collective-permute-start | bytes 442376 | tf_op jit(solution)/shard_map/ppermute | solution.py:251
  9.6 11.2 %collective-permute-start.1 = (bf16[288,256]{1,0:T(8,128)(2,1)S(1)}, bf16[288,256]{1,0:T(8,128)(2,1)S(1)}, u32[]{:S(2)}, u32[]{:S(2)}) collective-permute-start(bf16[288,256]{1,0:T(8,128)(2,1)S(1)} %get-tuple-element.14), channel_id=1, source_target_pairs={{0,4},{1,1},{2,6},{3,3},{4,0},{5,5},{6,2},{7,7},{8,12},{9,9},{10,1... | collective-permute-start | bytes 442376 | tf_op jit(solution)/shard_map/ppermute | solution.py:251
  12.0 10.9 %collective-permute-start.4 = (bf16[288,256]{1,0:T(8,128)(2,1)S(1)}, bf16[288,256]{1,0:T(8,128)(2,1)S(1)}, u32[]{:S(2)}, u32[]{:S(2)}) collective-permute-start(bf16[288,256]{1,0:T(8,128)(2,1)S(1)} %get-tuple-element.15), channel_id=1, source_target_pairs={{0,10},{1,15},{2,8},{3,13},{4,14},{5,11},{6,12},{7,9},{8,2},{9,7},... | collective-permute-start | bytes 442376 | tf_op jit(solution)/shard_map/ppermute | solution.py:251
  13.8 1.4 %collective-permute-start.6 = (bf16[272,256]{1,0:T(8,128)(2,1)S(1)}, bf16[272,256]{1,0:T(8,128)(2,1)S(1)}, u32[]{:S(2)}, u32[]{:S(2)}) collective-permute-start(bf16[272,256]{1,0:T(8,128)(2,1)S(1)} %collective-permute-done.5.refs_0_), channel_id=1, source_target_pairs={{0,1},{1,0},{2,3},{3,2},{4,5},{5,4},{6,7},{7,6},{8,9},{9,8},{10,11... | collective-permute-start | bytes 417800 | tf_op jit(solution)/shard_map/ppermute | solution.py:242
  13.8 9.2 %collective-permute-start.2 = (bf16[288,256]{1,0:T(8,128)(2,1)S(1)}, bf16[288,256]{1,0:T(8,128)(2,1)S(1)}, u32[]{:S(2)}, u32[]{:S(2)}) collective-permute-start(bf16[288,256]{1,0:T(8,128)(2,1)S(1)} %get-tuple-element.15), channel_id=1, source_target_pairs={{0,8},{1,13},{2,10},{3,15},{4,12},{5,9},{6,14},{7,11},{8,0},{9,5},... | collective-permute-start | bytes 442376 | tf_op jit(solution)/shard_map/ppermute | solution.py:251
  15.8 7.8 %collective-permute-start.9 = (bf16[272,256]{1,0:T(8,128)(2,1)S(1)}, bf16[272,256]{1,0:T(8,128)(2,1)S(1)}, u32[]{:S(2)}, u32[]{:S(2)}) collective-permute-start(bf16[272,256]{1,0:T(8,128)(2,1)S(1)} %get-tuple-element.17), channel_id=1, source_target_pairs={{0,6},{1,3},{2,4},{3,1},{4,2},{5,7},{6,0},{7,5},{8,14},{9,11},{10,... | collective-permute-start | bytes 417800 | tf_op jit(solution)/shard_map/ppermute | solution.py:251
  18.4 8.8 %collective-permute-start.7 = (bf16[272,256]{1,0:T(8,128)(2,1)S(1)}, bf16[272,256]{1,0:T(8,128)(2,1)S(1)}, u32[]{:S(2)}, u32[]{:S(2)}) collective-permute-start(bf16[272,256]{1,0:T(8,128)(2,1)S(1)} %get-tuple-element.17), channel_id=1, source_target_pairs={{0,4},{1,1},{2,6},{3,3},{4,0},{5,5},{6,2},{7,7},{8,12},{9,9},{10,1... | collective-permute-start | bytes 417800 | tf_op jit(solution)/shard_map/ppermute | solution.py:251
  20.8 6.4 %collective-permute-start.10 = (bf16[272,256]{1,0:T(8,128)(2,1)S(1)}, bf16[272,256]{1,0:T(8,128)(2,1)S(1)}, u32[]{:S(2)}, u32[]{:S(2)}) collective-permute-start(bf16[272,256]{1,0:T(8,128)(2,1)S(1)} %get-tuple-element.18), channel_id=1, source_target_pairs={{0,10},{1,15},{2,8},{3,13},{4,14},{5,11},{6,12},{7,9},{8,2},{9,7},... | collective-permute-start | bytes 417800 | tf_op jit(solution)/shard_map/ppermute | solution.py:251
  22.9 5.1 %collective-permute-start.8 = (bf16[272,256]{1,0:T(8,128)(2,1)S(1)}, bf16[272,256]{1,0:T(8,128)(2,1)S(1)}, u32[]{:S(2)}, u32[]{:S(2)}) collective-permute-start(bf16[272,256]{1,0:T(8,128)(2,1)S(1)} %get-tuple-element.18), channel_id=1, source_target_pairs={{0,8},{1,13},{2,10},{3,15},{4,12},{5,9},{6,14},{7,11},{8,0},{9,5},... | collective-permute-start | bytes 417800 | tf_op jit(solution)/shard_map/ppermute | solution.py:251
  28.6 2.4 %collective-permute-start.11 = (f32[520,256]{1,0:T(8,128)S(1)}, f32[520,256]{1,0:T(8,128)S(1)}, u32[]{:S(2)}, u32[]{:S(2)}) collective-permute-start(f32[520,256]{1,0:T(8,128)S(1)} %get-tuple-element.19.mine), channel_id=1, source_target_pairs={{0,1},{1,0},{2,3},{3,2},{4,5},{5,4},{6,7},{7,6},{8,9},{9,8},{10,11... | collective-permute-start | bytes 1597448 | tf_op jit(solution)/shard_map/ppermute | solution.py:242
  28.6 2.1 %collective-permute-start.12 = (bf16[272,256]{1,0:T(8,128)(2,1)S(1)}, bf16[272,256]{1,0:T(8,128)(2,1)S(1)}, u32[]{:S(2)}, u32[]{:S(2)}) collective-permute-start(bf16[272,256]{1,0:T(8,128)(2,1)S(1)} %get-tuple-element.20), channel_id=1, source_target_pairs={{0,1},{1,0},{2,3},{3,2},{4,5},{5,4},{6,7},{7,6},{8,9},{9,8},{10,11... | collective-permute-start | bytes 417800 | tf_op jit(solution)/shard_map/ppermute | solution.py:242
  29.1 1.8 %copy-start = (bf16[512,256]{1,0:T(8,128)(2,1)S(1)}, bf16[512,256]{1,0:T(8,128)(2,1)}, u32[]{:S(2)}) copy-start(bf16[512,256]{1,0:T(8,128)(2,1)} %old.1) | copy-start | bytes 786436
  29.1 1.8 %collective-permute-start.13 = (bf16[272,256]{1,0:T(8,128)(2,1)S(1)}, bf16[272,256]{1,0:T(8,128)(2,1)S(1)}, u32[]{:S(2)}, u32[]{:S(2)}) collective-permute-start(bf16[272,256]{1,0:T(8,128)(2,1)S(1)} %get-tuple-element.21), channel_id=1, source_target_pairs={{0,1},{1,0},{2,3},{3,2},{4,5},{5,4},{6,7},{7,6},{8,9},{9,8},{10,11... | collective-permute-start | bytes 417800 | tf_op jit(solution)/shard_map/ppermute | solution.py:242
